TPU v7x, 512 devices: a whole 4x4x16 slice. The times are simulated.
512 devices in a mesh: img: 128 (over x, z, core), sub: 4 (over y).
Axes of the slice: x: 4, y: 4, z: 16, core: 2. Of those that a mesh axis runs over, the one named last changes fastest.
Arguments:
- descriptors: bfloat16 [1024, 256, 256], P('img', 'sub'), may hold values from -6 to 6
- counts: int32 [1024], P('img'), may hold values from 128 to 256, as said below
- visible: int32 [1024, 256], P('img', 'sub'), may hold values 0 or 1
- pair_list: int32 [4096, 2], P('img'), may hold values from 0 to 1023, as said below
- pair_count: int32 [128], P('img'), may hold values from 16 to 32, as said below
- w_attend: bfloat16 [256, 256], replicated, may hold values from -0.375 to 0.375
- w_value: bfloat16 [256, 256], replicated, may hold values from -0.375 to 0.375
- w_output: bfloat16 [256, 256], replicated, may hold values from -0.375 to 0.375
- w_hidden: bfloat16 [512, 512], replicated, may hold values from -0.25 to 0.25
- norm_gain: float32 [512], replicated, may hold values from 0.1 to 1.9
- w_down: bfloat16 [512, 256], replicated, may hold values from -0.25 to 0.25
- w_match: bfloat16 [256, 256], replicated, may hold values from -0.375 to 0.375
- unassigned_bucket: float32 [1], replicated, may hold values from 0.5 to 2
Outputs:
- updates: bfloat16 [1024, 256, 256], P('img', 'sub')
- masses: float32 [1024, 256], P('img', 'sub')
Inputs may be any that keep to these rules, and one draw needn't show every extreme that they name: `counts`: multiples of 128; some image has all 256. `pair_list`: rows o * 32 to (o + 1) * 32 - 1 are owner o's slots; in every row image i is held by img index o and image j by img index (o + d) mod 128 for some d in -3 to 3 other than 0; no unordered pair of images appears twice among live rows; among one owner's live rows at most 6 have image j on one img index, reached in every draw. `pair_count`: some owner has all 32 slots live.
All inputs are finite; a program needn't handle non-finite values. No bound on the sum of `visible` on one device may be relied on, other than what follows from the above.
Results may differ from a plain program's by a relative error of at most 0.01.
Values may be sent and summed in bfloat16 or wider, within the bound.
A program may use at most 64 MiB of HBM per device.

v0:
```python
import math

import jax
import jax.numpy as jnp
from jax import lax
from jax.sharding import PartitionSpec as P

HEADS = 4
WIN = 3
ITERS = 10


MASKED = -1e30
FORGET = 30.0


def shifted(shard, axis, by):
    size = lax.axis_size(axis)
    return lax.ppermute(shard, axis, [(i, (i + by) % size) for i in range(size)])


def project(features, weight):
    return jnp.dot(features, weight, preferred_element_type=jnp.float32).astype(jnp.bfloat16)


def split_heads(values):
    return values.reshape(values.shape[0], HEADS, -1)


def softmax_weights(similarity, kept, axis):
    masked = jnp.where(kept, similarity, MASKED)
    top_value = jnp.max(masked, axis=axis, keepdims=True)
    raised = jnp.exp(masked - top_value)
    return (raised / jnp.sum(raised, axis=axis, keepdims=True)).astype(jnp.bfloat16)


def refine(features, message, w_output, w_hidden, norm_gain, w_down):
    sent = project(message, w_output)
    joined = jnp.concatenate([features, sent], axis=-1)
    hidden = jnp.dot(joined, w_hidden, preferred_element_type=jnp.float32)
    average = jnp.mean(hidden, axis=-1, keepdims=True)
    centred = hidden - average
    variance = jnp.mean(centred * centred, axis=-1, keepdims=True)
    normed = centred * lax.rsqrt(variance + 1e-05) * norm_gain
    activated = jax.nn.gelu(normed, approximate=False).astype(jnp.bfloat16)
    return project(activated, w_down)


def entropic_transport_iterate(
    affinity_matrix, source_valid_indicator, target_valid_indicator, unassigned_bucket
):
    count_rows = jnp.sum(source_valid_indicator)
    count_cols = jnp.sum(target_valid_indicator)
    total = count_rows + count_cols
    offset = -jnp.log(jnp.maximum(total, 1.0))
    bin_value = unassigned_bucket[0]
    side_column = jnp.zeros((affinity_matrix.shape[0], 1), jnp.float32) + bin_value
    bottom_row = jnp.zeros((1, affinity_matrix.shape[1] + 1), jnp.float32) + bin_value
    coupling = jnp.concatenate(
        [jnp.concatenate([affinity_matrix, side_column], axis=1), bottom_row], axis=0
    )
    log_rows = jnp.concatenate(
        [
            jnp.where(source_valid_indicator > 0, offset, offset - FORGET),
            jnp.reshape(jnp.log(jnp.maximum(count_cols, 1.0)) + offset, (1,)),
        ]
    )
    log_cols = jnp.concatenate(
        [
            jnp.where(target_valid_indicator > 0, offset, offset - FORGET),
            jnp.reshape(jnp.log(jnp.maximum(count_rows, 1.0)) + offset, (1,)),
        ]
    )
    row_pot = jnp.zeros((coupling.shape[0],), jnp.float32)
    col_pot = jnp.zeros((coupling.shape[1],), jnp.float32)
    for sweep in range(ITERS):
        row_pot = log_rows - jax.nn.logsumexp(coupling + col_pot[None, :], axis=1)
        col_pot = log_cols - jax.nn.logsumexp(coupling + row_pot[:, None], axis=0)
    plan = jnp.exp(coupling[:-1, :-1] + row_pot[:-1, None] + col_pot[None, :-1])
    mass_rows = (jnp.sum(plan, axis=1) * total * source_valid_indicator).astype(jnp.bfloat16)
    mass_cols = (jnp.sum(plan, axis=0) * total * target_valid_indicator).astype(jnp.bfloat16)
    return (mass_rows, mass_cols)


def pair_work(
    own_feat,
    source_valid_entries,
    own_attend,
    own_value,
    other_feat,
    target_valid_entries,
    w_attend,
    w_value,
    w_output,
    w_hidden,
    norm_gain,
    w_down,
    w_match,
    unassigned_bucket,
):
    key_count, width = own_feat.shape
    head_size = width // HEADS
    other_attend = project(other_feat, w_attend)
    other_value = project(other_feat, w_value)
    similarity = jnp.einsum(
        "khd,lhd->hkl",
        split_heads(own_attend),
        split_heads(other_attend),
        preferred_element_type=jnp.float32,
    ) / math.sqrt(head_size)
    to_other = softmax_weights(similarity, target_valid_entries[None, None, :] > 0, 2)
    to_own = softmax_weights(similarity, source_valid_entries[None, :, None] > 0, 1)
    own_message = jnp.einsum(
        "hkl,lhd->khd", to_other, split_heads(other_value), preferred_element_type=jnp.float32
    )
    own_message = own_message.reshape(key_count, width).astype(jnp.bfloat16)
    other_message = jnp.einsum(
        "hkl,khd->lhd", to_own, split_heads(own_value), preferred_element_type=jnp.float32
    )
    other_message = other_message.reshape(key_count, width).astype(jnp.bfloat16)
    own_delta = refine(own_feat, own_message, w_output, w_hidden, norm_gain, w_down)
    other_delta = refine(other_feat, other_message, w_output, w_hidden, norm_gain, w_down)
    own_new = (own_feat.astype(jnp.float32) + own_delta.astype(jnp.float32)).astype(jnp.bfloat16)
    other_new = (other_feat.astype(jnp.float32) + other_delta.astype(jnp.float32)).astype(
        jnp.bfloat16
    )
    own_match = project(own_new, w_match)
    other_match = project(other_new, w_match)
    affinity_matrix = jnp.dot(
        own_match, other_match.T, preferred_element_type=jnp.float32
    ) / math.sqrt(width)
    source_marginal_weight, target_marginal_weight = entropic_transport_iterate(
        affinity_matrix, source_valid_entries, target_valid_entries, unassigned_bucket
    )
    return (own_delta, other_delta, source_marginal_weight, target_marginal_weight)


def step_of(turn):
    return (turn // 2 + 1) * (1 - 2 * (turn % 2))


def local(
    descriptors,
    counts,
    visible,
    pair_list,
    pair_count,
    w_attend,
    w_value,
    w_output,
    w_hidden,
    norm_gain,
    w_down,
    w_match,
    unassigned_bucket,
):
    img_count = lax.axis_size("img")
    sub_count = lax.axis_size("sub")
    my_img = lax.axis_index("img")
    my_sub = lax.axis_index("sub")
    groups, row_count, width = descriptors.shape
    slot_total = pair_list.shape[0]
    reach = 2 * WIN
    capacity = (slot_total + reach - 1) // reach
    slot_space = reach * capacity
    positions = my_sub * row_count + jnp.arange(row_count, dtype=jnp.int32)
    keep_local = ((positions[None, :] < counts[:, None]) & (visible > 0)).astype(jnp.bfloat16)
    own_local = jnp.clip(pair_list[:, 0] - my_img * groups, 0, groups - 1)
    partner = pair_list[:, 1]
    source = partner // groups
    partner_local = partner - source * groups
    distance = (source - my_img + img_count) % img_count
    turn_ids = jnp.where(distance <= WIN, 2 * (distance - 1), 2 * (img_count - distance - 1) + 1)
    live = jnp.arange(slot_total, dtype=jnp.int32) < pair_count[0]
    by_turn = (
        (turn_ids[:, None] == jnp.arange(reach, dtype=jnp.int32)[None, :]) & live[:, None]
    ).astype(jnp.float32)
    earlier = (jnp.arange(slot_total)[:, None] > jnp.arange(slot_total)[None, :]).astype(
        jnp.float32
    )
    before = jnp.dot(earlier, by_turn, precision=lax.Precision.HIGHEST)
    rank_ids = jnp.take_along_axis(before, jnp.clip(turn_ids, 0, reach - 1)[:, None], axis=1)[
        :, 0
    ].astype(jnp.int32)
    slot_ids = jnp.where(live, turn_ids * capacity + rank_ids, slot_space)
    asking = jnp.full((slot_space,), -1, jnp.int32).at[slot_ids].set(partner_local, mode="drop")
    asking = asking.reshape(reach, capacity)
    choosers = []
    fetched_rows = []
    fetched_masks = []
    for turn in range(reach):
        step = step_of(turn)
        asked = shifted(asking[turn], "img", step)
        chooser = (asked[:, None] == jnp.arange(groups, dtype=jnp.int32)[None, :]).astype(
            jnp.bfloat16
        )
        outgoing = jnp.einsum(
            "cg,grd->crd", chooser, descriptors, preferred_element_type=jnp.float32
        ).astype(jnp.bfloat16)
        outgoing_keep = jnp.einsum(
            "cg,gr->cr", chooser, keep_local, preferred_element_type=jnp.float32
        ).astype(jnp.bfloat16)
        got_rows, got_keep = shifted((outgoing, outgoing_keep), "img", -step)
        choosers.append(chooser)
        fetched_rows.append(got_rows)
        fetched_masks.append(got_keep)
    fetched = jnp.stack(fetched_rows).reshape(slot_space, row_count, width)
    fetched_keep = jnp.stack(fetched_masks).reshape(slot_space, row_count)
    clipped = jnp.minimum(slot_ids, slot_space - 1)
    partner_rows = fetched[clipped]
    partner_keep = fetched_keep[clipped]
    partner_full, partner_mask = (
        lax.all_to_all(partner_rows, "sub", split_axis=0, concat_axis=1, tiled=True),
        lax.all_to_all(partner_keep, "sub", split_axis=0, concat_axis=1, tiled=True),
    )
    own_full, own_mask = (
        lax.all_gather(descriptors, "sub", axis=1, tiled=True),
        lax.all_gather(keep_local, "sub", axis=1, tiled=True),
    )
    own_attend = jnp.einsum(
        "gkd,de->gke", own_full, w_attend, preferred_element_type=jnp.float32
    ).astype(jnp.bfloat16)
    own_value = jnp.einsum(
        "gkd,de->gke", own_full, w_value, preferred_element_type=jnp.float32
    ).astype(jnp.bfloat16)
    quarter = slot_total // sub_count
    mine_local = lax.dynamic_slice_in_dim(own_local, my_sub * quarter, quarter)
    mine_live = lax.dynamic_slice_in_dim(live, my_sub * quarter, quarter)

    def one_pair(items):
        other_feat, target_valid_entries, which = items
        return pair_work(
            own_full[which],
            own_mask[which].astype(jnp.float32),
            own_attend[which],
            own_value[which],
            other_feat,
            target_valid_entries.astype(jnp.float32),
            w_attend,
            w_value,
            w_output,
            w_hidden,
            norm_gain,
            w_down,
            w_match,
            unassigned_bucket,
        )

    own_delta, other_delta, source_marginal_weight, target_marginal_weight = lax.map(
        one_pair, (partner_full, partner_mask, mine_local)
    )
    alive = mine_live.astype(jnp.bfloat16)
    own_delta = own_delta * alive[:, None, None]
    other_delta = other_delta * alive[:, None, None]
    source_marginal_weight = source_marginal_weight * alive[:, None]
    target_marginal_weight = target_marginal_weight * alive[:, None]
    owner_pick = (
        (mine_local[:, None] == jnp.arange(groups, dtype=jnp.int32)[None, :]) & mine_live[:, None]
    ).astype(jnp.bfloat16)
    own_terms = jnp.einsum("pg,pkd->gkd", owner_pick, own_delta, preferred_element_type=jnp.float32)
    own_mass_terms = jnp.einsum(
        "pg,pk->gk", owner_pick, source_marginal_weight, preferred_element_type=jnp.float32
    )
    own_sum, own_mass_sum = (
        lax.psum_scatter(
            own_terms.astype(jnp.bfloat16), "sub", scatter_dimension=1, tiled=True
        ).astype(jnp.float32),
        lax.psum_scatter(
            own_mass_terms.astype(jnp.bfloat16), "sub", scatter_dimension=1, tiled=True
        ).astype(jnp.float32),
    )
    back_delta, back_mass = (
        lax.all_to_all(other_delta, "sub", split_axis=1, concat_axis=0, tiled=True),
        lax.all_to_all(target_marginal_weight, "sub", split_axis=1, concat_axis=0, tiled=True),
    )
    slot_rows = (
        jnp.zeros((slot_space, row_count, width), jnp.bfloat16)
        .at[slot_ids]
        .set(back_delta, mode="drop")
    )
    slot_rows = slot_rows.reshape(reach, capacity, row_count, width)
    home_rows = jnp.zeros((groups, row_count, width), jnp.float32)
    slot_mass = (
        jnp.zeros((slot_space, row_count), jnp.bfloat16).at[slot_ids].set(back_mass, mode="drop")
    )
    slot_mass = slot_mass.reshape(reach, capacity, row_count)
    home_mass = jnp.zeros((groups, row_count), jnp.float32)
    for turn in range(reach):
        got_rows, got_mass = shifted((slot_rows[turn], slot_mass[turn]), "img", step_of(turn))
        home_rows = home_rows + jnp.einsum(
            "cg,crd->grd", choosers[turn], got_rows, preferred_element_type=jnp.float32
        )
        home_mass = home_mass + jnp.einsum(
            "cg,cr->gr", choosers[turn], got_mass, preferred_element_type=jnp.float32
        )
    updates = (own_sum + home_rows).astype(jnp.bfloat16)
    masses = own_mass_sum + home_mass
    return (updates, masses)


def solution(mesh):
    placed = (
        P("img", "sub", None),
        P("img"),
        P("img", "sub"),
        P("img", None),
        P("img"),
        P(),
        P(),
        P(),
        P(),
        P(),
        P(),
        P(),
        P(),
    )
    return jax.shard_map(
        local,
        mesh=mesh,
        in_specs=placed,
        out_specs=(P("img", "sub", None), P("img", "sub")),
        check_vma=False,
    )
```

profile of v0, /device:TPU:1, one launch (start us, length us, event | category | flops | bytes accessed | tf_op | source)
XLA Modules:
  0.0 650.7 jit_solution(16585080124674581325)
XLA Ops:
  11.2 4.9 collective-permute-start
  16.1 5.8 collective-permute-start.2
  23.8 7.9 %collective-permute-start.6 = (s32[6]{0:T(128)S(1)}, s32[6]{0:T(128)S(1)}, u32[]{:S(2)}, u32[]{:S(2)}) collective-permute-start(s32[6]{0:T(128)S(1)} %get-tuple-element.489), channel_id=1, source_target_pairs={{0,504},{4,508},{8,0},{12,4},{16,8},{20,12},{24,16},{28,20},{32,24... | collective-permute-start | bytes 80 | tf_op jit(solution)/shard_map/ppermute | solution.py:19
  34.5 7.0 %collective-permute-start.10 = (s32[6]{0:T(128)S(1)}, s32[6]{0:T(128)S(1)}, u32[]{:S(2)}, u32[]{:S(2)}) collective-permute-start(s32[6]{0:T(128)S(1)} %get-tuple-element.487), channel_id=1, source_target_pairs={{0,500},{4,504},{8,508},{12,0},{16,4},{20,8},{24,12},{28,16},{32,2... | collective-permute-start | bytes 80 | tf_op jit(solution)/shard_map/ppermute | solution.py:19
  42.9 7.9 %collective-permute-start.12 = (bf16[6,64]{1,0:T(8,128)(2,1)S(1)}, bf16[6,64]{1,0:T(8,128)(2,1)S(1)}, u32[]{:S(2)}, u32[]{:S(2)}) collective-permute-start(bf16[6,64]{1,0:T(8,128)(2,1)S(1)} %convolution_convert_fusion.25), channel_id=1, source_target_pairs={{0,508},{4,0},{8,4},{12,8},{16,12},{20,16},{24,20},{28,24},{32,28}... | collective-permute-start | bytes 2312 | tf_op jit(solution)/shard_map/ppermute | solution.py:19
  53.7 6.6 %collective-permute-start.14 = (bf16[6,64]{1,0:T(8,128)(2,1)S(1)}, bf16[6,64]{1,0:T(8,128)(2,1)S(1)}, u32[]{:S(2)}, u32[]{:S(2)}) collective-permute-start(bf16[6,64]{1,0:T(8,128)(2,1)S(1)} %convolution_convert_fusion.23), channel_id=1, source_target_pairs={{0,504},{4,508},{8,0},{12,4},{16,8},{20,12},{24,16},{28,20},{32,24... | collective-permute-start | bytes 2312 | tf_op jit(solution)/shard_map/ppermute | solution.py:19
  60.7 1.9 collective-permute-start.15
  63.2 2.8 collective-permute-start.16
  66.4 3.7 collective-permute-start.17
  72.1 5.5 collective-permute-start.3
  77.6 11.5 %collective-permute-start.5 = (bf16[6,64,256]{2,0,1:T(8,128)(2,1)S(1)}, bf16[6,64,256]{2,0,1:T(8,128)(2,1)S(1)}, u32[]{:S(2)}, u32[]{:S(2)}) collective-permute-start(bf16[6,64,256]{2,0,1:T(8,128)(2,1)S(1)} %convolution_convert_fusion.16), channel_id=1, source_target_pairs={{0,504},{4,508},{8,0},{12,4},{16,8},{20,12},{24,16},{28,20},{32,24... | collective-permute-start | bytes 589832 | tf_op jit(solution)/shard_map/ppermute | solution.py:19
  91.1 2.6 collective-permute-start.9
  95.0 4.2 all-to-all-start.1
  99.1 4.1 collective-permute-start.11
  103.5 7.5 %collective-permute-done.11 = bf16[6,64,256]{2,0,1:T(8,128)(2,1)S(1)} collective-permute-done((bf16[6,64,256]{2,0,1:T(8,128)(2,1)S(1)}, bf16[6,64,256]{2,0,1:T(8,128)(2,1)S(1)}, u32[]{:S(2)}, u32[]{:S(2)}) %collective-permute-start.11) | collective-permute-done | bytes 196640 | tf_op jit(solution)/shard_map/ppermute | solution.py:19
  112.9 4.0 all-to-all-start
  117.0 12.9 %all-gather = bf16[4,64,8]{1,2,0:T(8,128)(2,1)S(1)} all-gather(bf16[1,64,8]{1,2,0:T(8,128)(2,1)S(1)} %get-tuple-element.452), channel_id=1, replica_groups=mesh['img'=128,'sub'=4] {'sub'}, dimensions={0}, use_global_device_ids=true | all-gather | bytes 5120 | tf_op jit(solution)/shard_map/all_gather | solution.py:218
  131.3 2.8 convolution_convert_fusion.11
  135.6 427.4 %while.18 = (s32[]{:T(128)}, bf16[8,256,256]{1,2,0:T(8,128)(2,1)}, bf16[8,256,256]{1,2,0:T(8,128)(2,1)}, bf16[8,256]{1,0:T(8,128)(2,1)S(1)}, bf16[8,256]{1,0:T(8...) while((s32[]{:T(128)}, bf16[8,256,256]{1,2,0:T(8,128)(2,1)}, ...), condition=%wide.region_54.55_spmd, body=%wide.region_1.54_spmd.sunk | while | flops 871521536 | bytes 23359456 | solution.py:249
  142.9 3.1 bitcast_dynamic-update-slice_fusion.11
  149.0 3.1 bitcast_dynamic-update-slice_fusion.10
  196.3 3.1 bitcast_dynamic-update-slice_fusion.11
  202.3 3.1 bitcast_dynamic-update-slice_fusion.10
  249.7 3.1 bitcast_dynamic-update-slice_fusion.11
  255.7 3.1 bitcast_dynamic-update-slice_fusion.10
  303.1 3.1 bitcast_dynamic-update-slice_fusion.11
  309.2 3.1 bitcast_dynamic-update-slice_fusion.10
  356.5 3.1 bitcast_dynamic-update-slice_fusion.11
  362.6 3.1 bitcast_dynamic-update-slice_fusion.10
  409.9 3.1 bitcast_dynamic-update-slice_fusion.11
  416.0 3.1 bitcast_dynamic-update-slice_fusion.10
  463.3 3.1 bitcast_dynamic-update-slice_fusion.11
  469.4 3.1 bitcast_dynamic-update-slice_fusion.10
  516.7 3.1 bitcast_dynamic-update-slice_fusion.11
  522.8 3.1 bitcast_dynamic-update-slice_fusion.10
  563.9 4.3 all-to-all-start.3
  573.6 4.2 all-to-all-start.2
  578.7 6.8 %collective-permute-start.29 = (bf16[6,64]{1,0:T(8,128)(2,1)S(1)}, bf16[6,64]{1,0:T(8,128)(2,1)S(1)}, u32[]{:S(2)}, u32[]{:S(2)}) collective-permute-start(bf16[6,64]{1,0:T(8,128)(2,1)S(1)} %get-tuple-element.481), channel_id=1, source_target_pairs={{0,500},{4,504},{8,508},{12,0},{16,4},{20,8},{24,12},{28,16},{32,2... | collective-permute-start | bytes 2312 | tf_op jit(solution)/shard_map/ppermute | solution.py:19
  587.0 6.7 %collective-permute-start.28 = (bf16[6,64]{1,0:T(8,128)(2,1)S(1)}, bf16[6,64]{1,0:T(8,128)(2,1)S(1)}, u32[]{:S(2)}, u32[]{:S(2)}) collective-permute-start(bf16[6,64]{1,0:T(8,128)(2,1)S(1)} %get-tuple-element.482), channel_id=1, source_target_pairs={{0,12},{4,16},{8,20},{12,24},{16,28},{20,32},{24,36},{28,40},{32,4... | collective-permute-start | bytes 2312 | tf_op jit(solution)/shard_map/ppermute | solution.py:19
  593.7 6.8 %collective-permute-start.27 = (bf16[6,64]{1,0:T(8,128)(2,1)S(1)}, bf16[6,64]{1,0:T(8,128)(2,1)S(1)}, u32[]{:S(2)}, u32[]{:S(2)}) collective-permute-start(bf16[6,64]{1,0:T(8,128)(2,1)S(1)} %get-tuple-element.483), channel_id=1, source_target_pairs={{0,504},{4,508},{8,0},{12,4},{16,8},{20,12},{24,16},{28,20},{32,24... | collective-permute-start | bytes 2312 | tf_op jit(solution)/shard_map/ppermute | solution.py:19
  600.5 1.9 collective-permute-start.26
  602.4 1.9 collective-permute-start.25
  604.4 3.6 collective-permute-start.24
  614.5 10.0 %collective-permute-start.21 = (bf16[6,64,256]{2,0,1:T(8,128)(2,1)S(1)}, bf16[6,64,256]{2,0,1:T(8,128)(2,1)S(1)}, u32[]{:S(2)}, u32[]{:S(2)}) collective-permute-start(bf16[6,64,256]{2,0,1:T(8,128)(2,1)S(1)} %copy.250), channel_id=1, source_target_pairs={{0,504},{4,508},{8,0},{12,4},{16,8},{20,12},{24,16},{28,20},{32,24... | collective-permute-start | bytes 589832 | tf_op jit(solution)/shard_map/ppermute | solution.py:19
  624.6 1.9 collective-permute-start.20
  626.6 1.9 collective-permute-start.19
  628.7 4.8 collective-permute-start.23
  633.6 5.2 collective-permute-start.18
  (1112 shorter events, 380.8 us)
Async XLA Ops:
  7.2 43.8 %copy-start.3 = (bf16[8,64,256]{2,1,0:T(8,128)(2,1)S(1)}, bf16[8,64,256]{2,1,0:T(8,128)(2,1)}, u32[]{:S(2)}) copy-start(bf16[8,64,256]{2,1,0:T(8,128)(2,1)} %param.15) | copy-start | bytes 786436
  7.2 124.2 %all-gather.3.cloned.1.call-start = ((), (), s32[]{:S(2)}) async-start(), calls=%async_computation.6 | async-start | bytes 1310720 | tf_op jit(solution)/shard_map/all_gather | solution.py:217
  11.2 23.3 %collective-permute-start = (s32[6]{0:T(128)S(1)}, s32[6]{0:T(128)S(1)}, u32[]{:S(2)}, u32[]{:S(2)}) collective-permute-start(s32[6]{0:T(128)S(1)} %get-tuple-element.492), channel_id=1, source_target_pairs={{0,4},{4,8},{8,12},{12,16},{16,20},{20,24},{24,28},{28,32},{32,36}... | collective-permute-start | bytes 80 | tf_op jit(solution)/shard_map/ppermute | solution.py:19
  16.1 26.8 %collective-permute-start.2 = (s32[6]{0:T(128)S(1)}, s32[6]{0:T(128)S(1)}, u32[]{:S(2)}, u32[]{:S(2)}) collective-permute-start(s32[6]{0:T(128)S(1)} %get-tuple-element.491), channel_id=1, source_target_pairs={{0,508},{4,0},{8,4},{12,8},{16,12},{20,16},{24,20},{28,24},{32,28}... | collective-permute-start | bytes 80 | tf_op jit(solution)/shard_map/ppermute | solution.py:19
  21.9 29.4 %collective-permute-start.4 = (s32[6]{0:T(128)S(1)}, s32[6]{0:T(128)S(1)}, u32[]{:S(2)}, u32[]{:S(2)}) collective-permute-start(s32[6]{0:T(128)S(1)} %get-tuple-element.490), channel_id=1, source_target_pairs={{0,8},{4,12},{8,16},{12,20},{16,24},{20,28},{24,32},{28,36},{32,40... | collective-permute-start | bytes 80 | tf_op jit(solution)/shard_map/ppermute | solution.py:19
  23.8 29.9 %collective-permute-start.6 = (s32[6]{0:T(128)S(1)}, s32[6]{0:T(128)S(1)}, u32[]{:S(2)}, u32[]{:S(2)}) collective-permute-start(s32[6]{0:T(128)S(1)} %get-tuple-element.489), channel_id=1, source_target_pairs={{0,504},{4,508},{8,0},{12,4},{16,8},{20,12},{24,16},{28,20},{32,24... | collective-permute-start | bytes 80 | tf_op jit(solution)/shard_map/ppermute | solution.py:19
  31.8 29.0 %collective-permute-start.8 = (s32[6]{0:T(128)S(1)}, s32[6]{0:T(128)S(1)}, u32[]{:S(2)}, u32[]{:S(2)}) collective-permute-start(s32[6]{0:T(128)S(1)} %get-tuple-element.488), channel_id=1, source_target_pairs={{0,12},{4,16},{8,20},{12,24},{16,28},{20,32},{24,36},{28,40},{32,4... | collective-permute-start | bytes 80 | tf_op jit(solution)/shard_map/ppermute | solution.py:19
  34.5 28.7 %collective-permute-start.10 = (s32[6]{0:T(128)S(1)}, s32[6]{0:T(128)S(1)}, u32[]{:S(2)}, u32[]{:S(2)}) collective-permute-start(s32[6]{0:T(128)S(1)} %get-tuple-element.487), channel_id=1, source_target_pairs={{0,500},{4,504},{8,508},{12,0},{16,4},{20,8},{24,12},{28,16},{32,2... | collective-permute-start | bytes 80 | tf_op jit(solution)/shard_map/ppermute | solution.py:19
  42.9 23.5 %collective-permute-start.12 = (bf16[6,64]{1,0:T(8,128)(2,1)S(1)}, bf16[6,64]{1,0:T(8,128)(2,1)S(1)}, u32[]{:S(2)}, u32[]{:S(2)}) collective-permute-start(bf16[6,64]{1,0:T(8,128)(2,1)S(1)} %convolution_convert_fusion.25), channel_id=1, source_target_pairs={{0,508},{4,0},{8,4},{12,8},{16,12},{20,16},{24,20},{28,24},{32,28}... | collective-permute-start | bytes 2312 | tf_op jit(solution)/shard_map/ppermute | solution.py:19
  51.2 18.9 %collective-permute-start.13 = (bf16[6,64]{1,0:T(8,128)(2,1)S(1)}, bf16[6,64]{1,0:T(8,128)(2,1)S(1)}, u32[]{:S(2)}, u32[]{:S(2)}) collective-permute-start(bf16[6,64]{1,0:T(8,128)(2,1)S(1)} %convolution_convert_fusion.24), channel_id=1, source_target_pairs={{0,4},{4,8},{8,12},{12,16},{16,20},{20,24},{24,28},{28,32},{32,36}... | collective-permute-start | bytes 2312 | tf_op jit(solution)/shard_map/ppermute | solution.py:19
  53.7 18.4 %collective-permute-start.14 = (bf16[6,64]{1,0:T(8,128)(2,1)S(1)}, bf16[6,64]{1,0:T(8,128)(2,1)S(1)}, u32[]{:S(2)}, u32[]{:S(2)}) collective-permute-start(bf16[6,64]{1,0:T(8,128)(2,1)S(1)} %convolution_convert_fusion.23), channel_id=1, source_target_pairs={{0,504},{4,508},{8,0},{12,4},{16,8},{20,12},{24,16},{28,20},{32,24... | collective-permute-start | bytes 2312 | tf_op jit(solution)/shard_map/ppermute | solution.py:19
  60.7 16.9 %collective-permute-start.15 = (bf16[6,64]{1,0:T(8,128)(2,1)S(1)}, bf16[6,64]{1,0:T(8,128)(2,1)S(1)}, u32[]{:S(2)}, u32[]{:S(2)}) collective-permute-start(bf16[6,64]{1,0:T(8,128)(2,1)S(1)} %convolution_convert_fusion.22), channel_id=1, source_target_pairs={{0,8},{4,12},{8,16},{12,20},{16,24},{20,28},{24,32},{28,36},{32,40... | collective-permute-start | bytes 2312 | tf_op jit(solution)/shard_map/ppermute | solution.py:19
  63.2 25.9 %collective-permute-start.16 = (bf16[6,64]{1,0:T(8,128)(2,1)S(1)}, bf16[6,64]{1,0:T(8,128)(2,1)S(1)}, u32[]{:S(2)}, u32[]{:S(2)}) collective-permute-start(bf16[6,64]{1,0:T(8,128)(2,1)S(1)} %convolution_convert_fusion.21), channel_id=1, source_target_pairs={{0,500},{4,504},{8,508},{12,0},{16,4},{20,8},{24,12},{28,16},{32,2... | collective-permute-start | bytes 2312 | tf_op jit(solution)/shard_map/ppermute | solution.py:19
  66.4 24.6 %collective-permute-start.17 = (bf16[6,64]{1,0:T(8,128)(2,1)S(1)}, bf16[6,64]{1,0:T(8,128)(2,1)S(1)}, u32[]{:S(2)}, u32[]{:S(2)}) collective-permute-start(bf16[6,64]{1,0:T(8,128)(2,1)S(1)} %convolution_convert_fusion.20), channel_id=1, source_target_pairs={{0,12},{4,16},{8,20},{12,24},{16,28},{20,32},{24,36},{28,40},{32,4... | collective-permute-start | bytes 2312 | tf_op jit(solution)/shard_map/ppermute | solution.py:19
  70.1 29.0 %collective-permute-start.1 = (bf16[6,64,256]{2,0,1:T(8,128)(2,1)S(1)}, bf16[6,64,256]{2,0,1:T(8,128)(2,1)S(1)}, u32[]{:S(2)}, u32[]{:S(2)}) collective-permute-start(bf16[6,64,256]{2,0,1:T(8,128)(2,1)S(1)} %convolution_convert_fusion.18), channel_id=1, source_target_pairs={{0,508},{4,0},{8,4},{12,8},{16,12},{20,16},{24,20},{28,24},{32,28}... | collective-permute-start | bytes 589832 | tf_op jit(solution)/shard_map/ppermute | solution.py:19
  72.1 31.2 %collective-permute-start.3 = (bf16[6,64,256]{2,0,1:T(8,128)(2,1)S(1)}, bf16[6,64,256]{2,0,1:T(8,128)(2,1)S(1)}, u32[]{:S(2)}, u32[]{:S(2)}) collective-permute-start(bf16[6,64,256]{2,0,1:T(8,128)(2,1)S(1)} %convolution_convert_fusion.17), channel_id=1, source_target_pairs={{0,4},{4,8},{8,12},{12,16},{16,20},{20,24},{24,28},{28,32},{32,36}... | collective-permute-start | bytes 589832 | tf_op jit(solution)/shard_map/ppermute | solution.py:19
  77.6 25.7 %collective-permute-start.5 = (bf16[6,64,256]{2,0,1:T(8,128)(2,1)S(1)}, bf16[6,64,256]{2,0,1:T(8,128)(2,1)S(1)}, u32[]{:S(2)}, u32[]{:S(2)}) collective-permute-start(bf16[6,64,256]{2,0,1:T(8,128)(2,1)S(1)} %convolution_convert_fusion.16), channel_id=1, source_target_pairs={{0,504},{4,508},{8,0},{12,4},{16,8},{20,12},{24,16},{28,20},{32,24... | collective-permute-start | bytes 589832 | tf_op jit(solution)/shard_map/ppermute | solution.py:19
  89.1 14.3 %collective-permute-start.7 = (bf16[6,64,256]{2,0,1:T(8,128)(2,1)S(1)}, bf16[6,64,256]{2,0,1:T(8,128)(2,1)S(1)}, u32[]{:S(2)}, u32[]{:S(2)}) collective-permute-start(bf16[6,64,256]{2,0,1:T(8,128)(2,1)S(1)} %convolution_convert_fusion.15), channel_id=1, source_target_pairs={{0,8},{4,12},{8,16},{12,20},{16,24},{20,28},{24,32},{28,36},{32,40... | collective-permute-start | bytes 589832 | tf_op jit(solution)/shard_map/ppermute | solution.py:19
  91.1 12.4 %collective-permute-start.9 = (bf16[6,64,256]{2,0,1:T(8,128)(2,1)S(1)}, bf16[6,64,256]{2,0,1:T(8,128)(2,1)S(1)}, u32[]{:S(2)}, u32[]{:S(2)}) collective-permute-start(bf16[6,64,256]{2,0,1:T(8,128)(2,1)S(1)} %convolution_convert_fusion.14), channel_id=1, source_target_pairs={{0,500},{4,504},{8,508},{12,0},{16,4},{20,8},{24,12},{28,16},{32,2... | collective-permute-start | bytes 589832 | tf_op jit(solution)/shard_map/ppermute | solution.py:19
  95.0 18.0 %all-to-all-start.1 = ((bf16[4,2,256]{2,1,0:T(2,128)(2,1)}), bf16[4,2,256]{2,1,0:T(2,128)(2,1)S(1)}, u32[]{:S(2)}, u32[]{:S(2)}) async-start(bf16[4,2,256]{2,1,0:T(2,128)(2,1)} %reshape.970), calls=%async_computation.1 | async-start | bytes 8192 | tf_op jit(solution)/shard_map/all_to_all | solution.py:214
  99.1 11.9 %collective-permute-start.11 = (bf16[6,64,256]{2,0,1:T(8,128)(2,1)S(1)}, bf16[6,64,256]{2,0,1:T(8,128)(2,1)S(1)}, u32[]{:S(2)}, u32[]{:S(2)}) collective-permute-start(bf16[6,64,256]{2,0,1:T(8,128)(2,1)S(1)} %convolution_convert_fusion.13), channel_id=1, source_target_pairs={{0,12},{4,16},{8,20},{12,24},{16,28},{20,32},{24,36},{28,40},{32,4... | collective-permute-start | bytes 589832 | tf_op jit(solution)/shard_map/ppermute | solution.py:19
  112.9 17.3 %all-to-all-start = ((bf16[32,64,256]{2,1,0:T(8,128)(2,1)}), bf16[32,64,256]{2,1,0:T(8,128)(2,1)S(1)}, u32[]{:S(2)}, u32[]{:S(2)}) async-start(bf16[32,64,256]{2,1,0:T(8,128)(2,1)} %gather_fusion), calls=%async_computation | async-start | bytes 2097152 | tf_op jit(solution)/shard_map/all_to_all | solution.py:213
  117.0 14.4 %copy-start.5 = (bf16[256,256]{1,0:T(8,128)(2,1)S(1)}, bf16[256,256]{1,0:T(8,128)(2,1)}, u32[]{:S(2)}) copy-start(bf16[256,256]{1,0:T(8,128)(2,1)} %param.21) | copy-start | bytes 393220
  131.3 2.8 copy-start.6
  131.3 2.8 copy-start.4
  134.1 1.5 copy-start
  134.1 1.5 copy-start.1
  134.1 1.4 copy-start.2
  134.2 1.4 copy-start.8
  563.9 9.8 %all-to-all-start.3 = ((bf16[4,2,256]{2,1,0:T(2,128)(2,1)}), bf16[4,2,256]{2,1,0:T(2,128)(2,1)S(1)}, u32[]{:S(2)}, u32[]{:S(2)}) async-start(bf16[4,2,256]{2,1,0:T(2,128)(2,1)} %reshape.972), calls=%async_computation.4 | async-start | bytes 8192 | tf_op jit(solution)/shard_map/all_to_all | solution.py:274
  568.2 40.5 %reduce-scatter.7.cloned.1.call-start = ((), (), s32[]{:S(2)}) async-start(), calls=%async_computation.8 | async-start | bytes 81920
  571.0 1.6 copy-start.7
  573.6 35.8 %all-to-all-start.2 = ((bf16[8,256,256]{2,0,1:T(8,128)(2,1)}), bf16[8,256,256]{2,0,1:T(8,128)(2,1)S(1)}, u32[]{:S(2)}, u32[]{:S(2)}) async-start(bf16[8,256,256]{2,0,1:T(8,128)(2,1)} %broadcast_multiply_fusion.4), calls=%async_computation.3 | async-start | bytes 2097152 | tf_op jit(solution)/shard_map/all_to_all | solution.py:273
  577.9 64.3 %reduce-scatter.5.cloned.1.call-start = ((), (), s32[]{:S(2)}) async-start(), calls=%async_computation.7 | async-start | bytes 1310720 | tf_op jit(solution)/shard_map/reduce_scatter | solution.py:265
  578.7 25.7 %collective-permute-start.29 = (bf16[6,64]{1,0:T(8,128)(2,1)S(1)}, bf16[6,64]{1,0:T(8,128)(2,1)S(1)}, u32[]{:S(2)}, u32[]{:S(2)}) collective-permute-start(bf16[6,64]{1,0:T(8,128)(2,1)S(1)} %get-tuple-element.481), channel_id=1, source_target_pairs={{0,500},{4,504},{8,508},{12,0},{16,4},{20,8},{24,12},{28,16},{32,2... | collective-permute-start | bytes 2312 | tf_op jit(solution)/shard_map/ppermute | solution.py:19
  587.0 21.1 %collective-permute-start.28 = (bf16[6,64]{1,0:T(8,128)(2,1)S(1)}, bf16[6,64]{1,0:T(8,128)(2,1)S(1)}, u32[]{:S(2)}, u32[]{:S(2)}) collective-permute-start(bf16[6,64]{1,0:T(8,128)(2,1)S(1)} %get-tuple-element.482), channel_id=1, source_target_pairs={{0,12},{4,16},{8,20},{12,24},{16,28},{20,32},{24,36},{28,40},{32,4... | collective-permute-start | bytes 2312 | tf_op jit(solution)/shard_map/ppermute | solution.py:19
  593.7 14.6 %collective-permute-start.27 = (bf16[6,64]{1,0:T(8,128)(2,1)S(1)}, bf16[6,64]{1,0:T(8,128)(2,1)S(1)}, u32[]{:S(2)}, u32[]{:S(2)}) collective-permute-start(bf16[6,64]{1,0:T(8,128)(2,1)S(1)} %get-tuple-element.483), channel_id=1, source_target_pairs={{0,504},{4,508},{8,0},{12,4},{16,8},{20,12},{24,16},{28,20},{32,24... | collective-permute-start | bytes 2312 | tf_op jit(solution)/shard_map/ppermute | solution.py:19
  600.5 7.9 %collective-permute-start.26 = (bf16[6,64]{1,0:T(8,128)(2,1)S(1)}, bf16[6,64]{1,0:T(8,128)(2,1)S(1)}, u32[]{:S(2)}, u32[]{:S(2)}) collective-permute-start(bf16[6,64]{1,0:T(8,128)(2,1)S(1)} %get-tuple-element.484), channel_id=1, source_target_pairs={{0,8},{4,12},{8,16},{12,20},{16,24},{20,28},{24,32},{28,36},{32,40... | collective-permute-start | bytes 2312 | tf_op jit(solution)/shard_map/ppermute | solution.py:19
  602.4 6.1 collective-permute-start.25
  604.4 9.2 %collective-permute-start.24 = (bf16[6,64]{1,0:T(8,128)(2,1)S(1)}, bf16[6,64]{1,0:T(8,128)(2,1)S(1)}, u32[]{:S(2)}, u32[]{:S(2)}) collective-permute-start(bf16[6,64]{1,0:T(8,128)(2,1)S(1)} %get-tuple-element.480), channel_id=1, source_target_pairs={{0,4},{4,8},{8,12},{12,16},{16,20},{20,24},{24,28},{28,32},{32,36}... | collective-permute-start | bytes 2312 | tf_op jit(solution)/shard_map/ppermute | solution.py:19
  611.7 22.0 %collective-permute-start.22 = (bf16[6,64,256]{2,0,1:T(8,128)(2,1)S(1)}, bf16[6,64,256]{2,0,1:T(8,128)(2,1)S(1)}, u32[]{:S(2)}, u32[]{:S(2)}) collective-permute-start(bf16[6,64,256]{2,0,1:T(8,128)(2,1)S(1)} %copy.251), channel_id=1, source_target_pairs={{0,12},{4,16},{8,20},{12,24},{16,28},{20,32},{24,36},{28,40},{32,4... | collective-permute-start | bytes 589832 | tf_op jit(solution)/shard_map/ppermute | solution.py:19
  614.5 24.6 %collective-permute-start.21 = (bf16[6,64,256]{2,0,1:T(8,128)(2,1)S(1)}, bf16[6,64,256]{2,0,1:T(8,128)(2,1)S(1)}, u32[]{:S(2)}, u32[]{:S(2)}) collective-permute-start(bf16[6,64,256]{2,0,1:T(8,128)(2,1)S(1)} %copy.250), channel_id=1, source_target_pairs={{0,504},{4,508},{8,0},{12,4},{16,8},{20,12},{24,16},{28,20},{32,24... | collective-permute-start | bytes 589832 | tf_op jit(solution)/shard_map/ppermute | solution.py:19
  624.6 14.7 %collective-permute-start.20 = (bf16[6,64,256]{2,0,1:T(8,128)(2,1)S(1)}, bf16[6,64,256]{2,0,1:T(8,128)(2,1)S(1)}, u32[]{:S(2)}, u32[]{:S(2)}) collective-permute-start(bf16[6,64,256]{2,0,1:T(8,128)(2,1)S(1)} %copy.249), channel_id=1, source_target_pairs={{0,8},{4,12},{8,16},{12,20},{16,24},{20,28},{24,32},{28,36},{32,40... | collective-permute-start | bytes 589832 | tf_op jit(solution)/shard_map/ppermute | solution.py:19
  626.6 12.9 %collective-permute-start.19 = (bf16[6,64,256]{2,0,1:T(8,128)(2,1)S(1)}, bf16[6,64,256]{2,0,1:T(8,128)(2,1)S(1)}, u32[]{:S(2)}, u32[]{:S(2)}) collective-permute-start(bf16[6,64,256]{2,0,1:T(8,128)(2,1)S(1)} %copy.248), channel_id=1, source_target_pairs={{0,508},{4,0},{8,4},{12,8},{16,12},{20,16},{24,20},{28,24},{32,28}... | collective-permute-start | bytes 589832 | tf_op jit(solution)/shard_map/ppermute | solution.py:19
  628.7 12.5 %collective-permute-start.23 = (bf16[6,64,256]{2,0,1:T(8,128)(2,1)S(1)}, bf16[6,64,256]{2,0,1:T(8,128)(2,1)S(1)}, u32[]{:S(2)}, u32[]{:S(2)}) collective-permute-start(bf16[6,64,256]{2,0,1:T(8,128)(2,1)S(1)} %copy.252), channel_id=1, source_target_pairs={{0,500},{4,504},{8,508},{12,0},{16,4},{20,8},{24,12},{28,16},{32,2... | collective-permute-start | bytes 589832 | tf_op jit(solution)/shard_map/ppermute | solution.py:19
  633.6 8.5 %collective-permute-start.18 = (bf16[6,64,256]{2,0,1:T(8,128)(2,1)S(1)}, bf16[6,64,256]{2,0,1:T(8,128)(2,1)S(1)}, u32[]{:S(2)}, u32[]{:S(2)}) collective-permute-start(bf16[6,64,256]{2,0,1:T(8,128)(2,1)S(1)} %copy.247), channel_id=1, source_target_pairs={{0,4},{4,8},{8,12},{12,16},{16,20},{20,24},{24,28},{28,32},{32,36}... | collective-permute-start | bytes 589832 | tf_op jit(solution)/shard_map/ppermute | solution.py:19
Sparse Core Ops, SparseCore 0:
  33.8 29.6 all-gather.2
  572.4 24.9 reduce-scatter.6
  600.4 31.1 reduce-scatter.4
where the time goes:
time: 660 us; the launch traced here: 651 us
  other arithmetic  276 us (42%)
  starting transfers between devices  152 us (23%)
  matrix products  104 us (16%)
  loops' own time  40.8 us (6%)
  local copies, waits for them, and re-layouts  40.1 us (6%)
  between operations  15.2 us (2%)
  blocking collectives  12.9 us (2%)
  waiting for transfers between devices  9.89 us (1%)
    ppermute x30, starting transfers between devices, shifted(): lax.ppermute(shard, axis, [(i, (i + by) % size) for i in range(size)])  135 us
    reduce_sum x80, other arithmetic, entropic_transport_iterate(): col_pot = log_cols - jax.nn.logsumexp(coupling + row_pot[:, None], axis=0)  71 us
    reduce_sum x80, other arithmetic, entropic_transport_iterate(): row_pot = log_rows - jax.nn.logsumexp(coupling + col_pot[None, :], axis=1)  63.8 us
    reduce_max x80, other arithmetic, entropic_transport_iterate(): col_pot = log_cols - jax.nn.logsumexp(coupling + row_pot[:, None], axis=0)  63.4 us
    reduce_max x80, other arithmetic, entropic_transport_iterate(): row_pot = log_rows - jax.nn.logsumexp(coupling + col_pot[None, :], axis=1)  60.8 us
    dot_general x56, matrix products, project(): jnp.dot(features, weight, preferred_element_type=jnp.float32)  59.3 us
    another operation x1, loops' own time, local(): lax.map(one_pair, (partner_full, partner_mask, mine_local))  40.8 us
  transfers between devices with their start and end apart: 37, of which 3 were waited for; matrix products, arithmetic and copies ran while one was open for 3% of the time, Pallas kernels for 0%

commit v1 on v0

v1 whole, which is shorter than its diff:
```python
import math

import jax, jax.numpy as jnp
from jax import lax
from jax.experimental import pallas as pl
from jax.experimental.pallas import tpu as pltpu
from jax.sharding import PartitionSpec as P

BF=jnp.bfloat16; F32=jnp.float32
LOG2E=1.4426950408889634
HEADS=4; ITERS=10; K=256; D=256; SLAB=272; KEYS=256

def nn(a,b): return lax.dot_general(a,b,(((1,),(0,)),((),())),preferred_element_type=F32)
def nt(a,b): return lax.dot_general(a,b,(((1,),(1,)),((),())),preferred_element_type=F32)

def eye(n,dt=BF):
    return (lax.broadcasted_iota(jnp.int32,(n,n),0)==lax.broadcasted_iota(jnp.int32,(n,n),1)).astype(dt)

def to_col(row, id_ref):
    return nt(id_ref[...], jnp.broadcast_to(row,(128,row.shape[1])))

def prologue(wa,wv,wo,wh,gain,wd,wm, wvT,woT,whT,wdT,wmT,gcol,ident):
    ident[...]=eye(256)
    I=ident[...]
    wvT[...]=nt(I,wv[...]).astype(BF)
    woT[...]=nt(I,wo[...]).astype(BF)
    wmT[...]=nt(I,wm[...]).astype(BF)
    for a in range(2):
        for b in range(2):
            whT[a*256:a*256+256,b*256:b*256+256]=nt(I,wh[b*256:b*256+256,a*256:a*256+256]).astype(BF)
    for b in range(2):
        wdT[:,b*256:b*256+256]=nt(I,wd[b*256:b*256+256,:]).astype(BF)
    e=lax.broadcasted_iota(jnp.int32,(128,128),0)==lax.broadcasted_iota(jnp.int32,(128,128),1)
    for q in range(4):
        g=jnp.sum(jnp.where(e,jnp.broadcast_to(gain[:,q*128:q*128+128],(128,128)),0.0),axis=1,keepdims=True)
        gcol[q*128:q*128+128,:]=jnp.broadcast_to(g,(128,128))

def gelu(y):
    return 0.5*y*(1.0+lax.erf(y*math.sqrt(0.5)))

def attention(a_other, a_self, vT_other, bias):
    outs=[]
    ones=jnp.ones((16,K),BF)
    for h in range(HEADS):
        sl=slice(h*64,h*64+64)
        s=nt(a_other[:,sl],a_self[:,sl])*(LOG2E/8.0)+bias
        m=jnp.max(s,axis=0,keepdims=True)
        e=jnp.exp2(s-m).astype(BF)
        r=nn(jnp.concatenate([vT_other[sl,:],ones],axis=0),e)
        outs.append((r[:64]*(1.0/r[64:65])).astype(BF))
    return jnp.concatenate(outs,axis=0)

def refine(x, msgT, W):
    sentT=nn(W['woT'][...],msgT).astype(BF)
    hid=nt(W['whT'][:,:256],x)+nn(W['whT'][:,256:],sentT)
    mean=jnp.sum(hid,axis=0,keepdims=True)*(1.0/512)
    cen=hid-mean
    var=jnp.sum(cen*cen,axis=0,keepdims=True)*(1.0/512)
    g=W['gcol'][...]
    normed=cen*lax.rsqrt(var+1e-5)*jnp.concatenate([g,g],axis=1)
    act=gelu(normed).astype(BF)
    return nn(W['wdT'][...],act).astype(BF)

def phase_a(xi,ki,xj,kj,W):
    big=1e30
    bi=(to_col(ki,W['ident'])-1.0)*big; bi=jnp.concatenate([bi,bi],axis=1)
    bj=(to_col(kj,W['ident'])-1.0)*big; bj=jnp.concatenate([bj,bj],axis=1)
    ai=nn(xi,W['wa'][...]).astype(BF); aj=nn(xj,W['wa'][...]).astype(BF)
    viT=nt(W['wvT'][...],xi).astype(BF); vjT=nt(W['wvT'][...],xj).astype(BF)
    miT=attention(aj,ai,vjT,bj)
    mjT=attention(ai,aj,viT,bi)
    diT=refine(xi,miT,W); djT=refine(xj,mjT,W)
    I=W['ident'][...]
    riT=(nt(I,xi)+diT.astype(F32)).astype(BF)
    rjT=(nt(I,xj)+djT.astype(F32)).astype(BF)
    mi=nn(W['wmT'][...],riT).astype(BF); mj=nn(W['wmT'][...],rjT).astype(BF)
    mi=nt(I,mi).astype(BF)
    sc=nn(mi,mj)*(LOG2E/16.0)
    return diT,djT,sc

def marginals(ki,kj,W):
    ki32=ki.astype(F32); kj32=kj.astype(F32)
    m=jnp.sum(ki32,axis=1,keepdims=True); n=jnp.sum(kj32,axis=1,keepdims=True)
    tot=m+n
    off=-jnp.log2(jnp.maximum(tot,1.0))
    fg=30.0*LOG2E
    kic=to_col(ki,W['ident'])[:,:1]
    lr=off-fg*(1.0-kic)
    lc=off-fg*(1.0-kj32)
    lrb=jnp.log2(jnp.maximum(n,1.0))+off
    lcb=jnp.log2(jnp.maximum(m,1.0))+off
    return tot,kic,lr,lc,lrb,lcb

def sink_init(c_ref,p,binv,lr,lc,lrb,lcb):
    c=c_ref[p]
    mx=jnp.maximum(jnp.max(c,axis=1,keepdims=True),binv)
    s=jnp.sum(jnp.exp2(c-mx),axis=1,keepdims=True)+jnp.exp2(binv-mx)
    f=lr-mx-jnp.log2(s)
    fb=lrb-binv-math.log2(257.0)
    t=jnp.sum(jnp.exp2(c+f),axis=0,keepdims=True)+jnp.exp2(binv+fb)
    g=lc-jnp.log2(t)
    tb=jnp.sum(jnp.exp2(binv+f),axis=0,keepdims=True)+jnp.exp2(binv+fb)
    gb=lcb-jnp.log2(tb)
    return f,fb,g,gb

CH=256
def sink_iter(c_ref,p,binv,lr,lc,lrb,lcb,r,rb,st):
    f,fb,g,gb=st
    eb=jnp.exp2(binv+fb+g); ebb=jnp.exp2(binv+fb+gb)
    ub=rb/(jnp.sum(eb,axis=1,keepdims=True)+ebb)
    t=eb*ub
    tb=ebb*ub
    nf=[]
    for q in range(0,K,CH):
        fq=f[q:q+CH]
        pq=jnp.exp2(c_ref[p,q:q+CH,:]+g+fq)
        bq=jnp.exp2((binv+gb)+fq)
        s=jnp.sum(pq,axis=1,keepdims=True)+bq
        u=r[q:q+CH]/s
        nf.append(fq+jnp.log2(u))
        t=t+jnp.sum(pq*u,axis=0,keepdims=True)
        tb=tb+jnp.sum(bq*u,axis=0,keepdims=True)
    f=jnp.concatenate(nf,axis=0) if len(nf)>1 else nf[0]
    return f,fb+jnp.log2(ub),g+lc-jnp.log2(t),gb+lcb-jnp.log2(tb)

def sink_out(c_ref,p,tot,kic,kj32,st,W):
    f,fb,g,gb=st
    plan=jnp.exp2(c_ref[p]+f+g)
    mi=(jnp.sum(plan,axis=1,keepdims=True)*tot*kic).astype(BF)
    mj=(jnp.sum(plan,axis=0,keepdims=True)*tot*kj32).astype(BF)
    e0=(lax.broadcasted_iota(jnp.int32,(16,128),1)==0).astype(BF)
    mirow=nt(e0,jnp.broadcast_to(mi,(256,128)))[:1]
    return mirow, mj.astype(F32)

WIN = 3
REACH = 2 * WIN
PER = 2
SLOTS = REACH * PER
OWN = 8
ROWS = 64
SUBS = 4
MESH = pl.DeviceIdType.MESH


def step_of(turn):
    return (turn // 2 + 1) * (1 - 2 * (turn % 2))


def places():
    n = lax.axis_size("img")
    me = lax.axis_index("img")
    sub = lax.axis_index("sub")
    others = [lax.rem(me + step_of(t) + n, n) for t in range(REACH)]
    peers = [lax.rem(sub + d, SUBS) for d in range(1, SUBS)]
    return me, sub, others, peers


def greet(others, peers):
    barrier = pltpu.get_barrier_semaphore()
    for h in others:
        pl.semaphore_signal(barrier, inc=1, device_id={"img": h}, device_id_type=MESH)
    for s in peers:
        pl.semaphore_signal(barrier, inc=1, device_id={"sub": s}, device_id_type=MESH)
    pl.semaphore_wait(barrier, len(others) + len(peers))


def job_table(pairs, live_count, me, img_count):
    first = pairs[:, 0:1]
    second = pairs[:, 1:2]
    slots = pairs.shape[0]
    row_ids = lax.broadcasted_iota(jnp.int32, (slots, 1), 0)
    holder = second >> 3
    ahead = holder - me
    ahead = jnp.where(ahead < 0, ahead + img_count, ahead)
    turn = jnp.where(ahead <= WIN, 2 * (ahead - 1), 2 * (img_count - ahead - 1) + 1)
    live = row_ids < live_count
    key = jnp.where(live, turn, REACH)
    code = 1 + (first & 7) * 8 + (second & 7)
    up = lax.broadcasted_iota(jnp.int32, (slots, slots), 0)
    across = lax.broadcasted_iota(jnp.int32, (slots, slots), 1)
    key_row = jnp.sum(jnp.where(up == across, key, 0), axis=0, keepdims=True)
    below = (key_row < key).astype(jnp.int32)
    base = jnp.sum(below, axis=1, keepdims=True)
    rank = jnp.sum(((key_row == key) & (across < up)).astype(jnp.int32), axis=1, keepdims=True)
    place = base + rank
    lane_of = jnp.where(live, key * 8 + (place & 3) * 2 + (rank >> 2), -1)
    lanes = lax.broadcasted_iota(jnp.int32, (slots, 128), 1)
    row = jnp.sum(jnp.where(lanes == lane_of, code, 0), axis=0, keepdims=True)
    return jnp.broadcast_to(row, (8, 128))


def gather_kernel(
    desc, counts, visible, pairs, pair_count, full, tables, masks, table, send_sem, recv_sem, tsend, trecv
):
    me, sub, others, peers = places()
    rows = pl.ds(pl.multiple_of(sub * ROWS, ROWS), ROWS)
    full[:, rows, :] = desc[...]
    image = lax.broadcasted_iota(jnp.int32, (OWN, ROWS), 0)
    found = jnp.zeros((OWN, ROWS), jnp.int32)
    for a in range(OWN):
        found = jnp.where(image == a, counts[a], found)
    spot = lax.broadcasted_iota(jnp.int32, (OWN, ROWS), 1) + sub * ROWS
    kept = jnp.where((spot < found) & (visible[...] > 0), 1.0, 0.0)
    wide = jnp.concatenate([kept] * SUBS, axis=1)
    lane = lax.broadcasted_iota(jnp.int32, (OWN, KEYS), 1)
    wide = jnp.where((lane >= sub * ROWS) & (lane < sub * ROWS + ROWS), wide, 0.0)
    masks[0] = jnp.concatenate([wide, jnp.zeros_like(wide)], axis=0).astype(BF)
    greet(others, peers)
    copies = []
    for d in range(1, SUBS):
        to = {"sub": peers[d - 1]}
        copies.append(
            pltpu.make_async_remote_copy(
                src_ref=full.at[:, rows, :],
                dst_ref=full.at[:, rows, :],
                send_sem=send_sem.at[0, d - 1],
                recv_sem=recv_sem.at[0, d - 1],
                device_id=to,
                device_id_type=MESH,
            )
        )
        copies.append(
            pltpu.make_async_remote_copy(
                src_ref=masks.at[0],
                dst_ref=masks.at[d],
                send_sem=send_sem.at[1, d - 1],
                recv_sem=recv_sem.at[1, d - 1],
                device_id=to,
                device_id_type=MESH,
            )
        )
    for copy in copies:
        copy.start()
    mine = job_table(pairs[...], pair_count[0], me, lax.axis_size("img"))
    table[...] = mine
    tables[REACH] = mine
    tells = []
    for t in range(REACH):
        tells.append(
            pltpu.make_async_remote_copy(
                src_ref=table,
                dst_ref=tables.at[t ^ 1],
                send_sem=tsend.at[t],
                recv_sem=trecv.at[t ^ 1],
                device_id={"img": others[t]},
                device_id_type=MESH,
            )
        )
    for copy in tells:
        copy.start()
    for copy in tells:
        copy.wait_send()
    for t in range(REACH):
        tells[t].wait_recv()
    for copy in copies:
        copy.wait()
    whole = masks[0].astype(F32)
    for d in range(1, SUBS):
        whole = whole + masks[d].astype(F32)
    for a in range(OWN):
        full[a, KEYS:, :] = jnp.broadcast_to(whole[a : a + 1], (SLAB - KEYS, KEYS)).astype(BF)


def asked(tables, t, c, sub):
    return tables[t, 0, (t ^ 1) * 8 + sub * 2 + c]


def fetch_kernel(tables, full, landed, stage, send_sem, recv_sem):
    me, sub, others, peers = places()
    greet(others, [])
    copies = []
    for t in (4, 5, 2, 3, 0, 1):
        for c in range(PER):
            which = jnp.maximum(asked(tables, t, c, sub) - 1, 0) & 7
            stage[t, c] = full[which]
        copy = pltpu.make_async_remote_copy(
            src_ref=stage.at[t],
            dst_ref=landed.at[t ^ 1],
            send_sem=send_sem.at[t],
            recv_sem=recv_sem.at[t ^ 1],
            device_id={"img": others[t]},
            device_id_type=MESH,
        )
        copy.start()
        copies.append(copy)
    for copy in copies:
        copy.wait()


def give_kernel(tables, own, slots, upd, mass, back, total, parts, got, mparts, mgot, zsend, zrecv, ysend, yrecv):
    me, sub, others, peers = places()
    greet(others, peers)
    copies = []
    for t in (4, 5, 2, 3, 0, 1):
        copy = pltpu.make_async_remote_copy(
            src_ref=slots.at[t],
            dst_ref=back.at[t ^ 1],
            send_sem=zsend.at[t],
            recv_sem=zrecv.at[t ^ 1],
            device_id={"img": others[t]},
            device_id_type=MESH,
        )
        copy.start()
        copies.append(copy)
    for copy in copies:
        copy.wait()
    wants = []
    for t in range(REACH):
        for c in range(PER):
            code = asked(tables, t, c, sub)
            wants.append((t, c, jnp.where(code > 0, (code - 1) & 7, -1)))
    ident = eye(KEYS)
    for a in range(OWN):
        def add(r, _):
            at = pl.ds(pl.multiple_of(r * 64, 64), 64)
            value = own[a, at, :]
            for t, c, which in wants:
                value = value + back[t, c, at, :].astype(F32) * jnp.where(which == a, 1.0, 0.0)
            total[at, :] = value.astype(BF)
            return 0
        lax.fori_loop(0, 4, add, 0)
        turned = nt(ident, total[...]).astype(BF)
        for s in range(SUBS):
            parts[s, a] = turned[s * ROWS : s * ROWS + ROWS]
        value = own[a, KEYS : KEYS + 16, :]
        for t, c, which in wants:
            value = value + back[t, c, KEYS:, :].astype(F32) * jnp.where(which == a, 1.0, 0.0)
        mparts[a : a + 1, :] = value[:1]
    sends = []
    for d in range(1, SUBS):
        to = {"sub": peers[d - 1]}
        sends.append(
            pltpu.make_async_remote_copy(
                src_ref=parts.at[peers[d - 1]],
                dst_ref=got.at[d - 1],
                send_sem=ysend.at[0, d - 1],
                recv_sem=yrecv.at[0, d - 1],
                device_id=to,
                device_id_type=MESH,
            )
        )
        sends.append(
            pltpu.make_async_remote_copy(
                src_ref=mparts,
                dst_ref=mgot.at[d - 1],
                send_sem=ysend.at[1, d - 1],
                recv_sem=yrecv.at[1, d - 1],
                device_id=to,
                device_id_type=MESH,
            )
        )
    for copy in sends:
        copy.start()
    for copy in sends:
        copy.wait()
    for a in range(OWN):
        value = parts[sub, a].astype(F32)
        for d in range(SUBS - 1):
            value = value + got[d, a].astype(F32)
        upd[a] = value.astype(BF)
    value = mparts[...]
    for d in range(SUBS - 1):
        value = value + mgot[d]
    out = jnp.zeros((OWN, ROWS), F32)
    for s in range(SUBS):
        out = jnp.where(sub == s, value[:, s * ROWS : s * ROWS + ROWS], out)
    mass[...] = out


def work_kernel(tables, full, landed, binr, wa, wv, wo, wh, gain, wd, wm, own, slots, wvT, woT, whT, wdT, wmT, gcol, ident, sc, jobs):
    sub = lax.axis_index("sub")
    prologue(wa, wv, wo, wh, gain, wd, wm, wvT, woT, whT, wdT, wmT, gcol, ident)
    W = dict(wa=wa, wvT=wvT, woT=woT, whT=whT, wdT=wdT, wmT=wmT, gcol=gcol, ident=ident)
    binv = binr[...] * LOG2E
    own[...] = jnp.zeros_like(own)
    n = jnp.int32(0)
    for t in range(REACH):
        for c in range(PER):
            code = tables[REACH, 0, t * 8 + sub * 2 + c]
            jobs[0, n] = (code - 1) >> 3
            jobs[1, n] = t * PER + c
            n = n + jnp.where(code > 0, 1, 0)

            @pl.when(code == 0)
            def _():
                slots[t, c] = jnp.zeros((SLAB, KEYS), BF)
    jobs[0, n] = jobs[0, jnp.maximum(n - 1, 0)]
    jobs[1, n] = jobs[1, jnp.maximum(n - 1, 0)]
    @pl.loop(0, n)
    def _(p):
        a = jobs[0, p]
        z = jobs[1, p]
        tz, cz = z >> 1, z & 1
        di, dj, s = phase_a(full[a, :KEYS], full[a, KEYS : KEYS + 1], landed[tz, cz, :KEYS], landed[tz, cz, KEYS : KEYS + 1], W)
        own[a, :KEYS] = own[a, :KEYS] + di.astype(F32)
        slots[tz, cz, :KEYS] = dj
        sc[p] = s

    @pl.loop(0, (n + 1) >> 1)
    def _(q):
        P = [q * 2 + i for i in range(2)]
        A = [jobs[0, p] for p in P]
        Z = [(jobs[1, p] >> 1, jobs[1, p] & 1) for p in P]
        KI = [full[a, KEYS : KEYS + 1] for a in A]
        KJ = [landed[z[0], z[1], KEYS : KEYS + 1] for z in Z]
        M = [marginals(ki, kj, W) for ki, kj in zip(KI, KJ)]
        RR = [(jnp.exp2(m[2]), jnp.exp2(m[4])) for m in M]
        S = [jnp.minimum(p, n - 1) for p in P]
        st = [sink_init(sc, p, binv, *m[2:]) for p, m in zip(S, M)]
        def body(_, st):
            return [sink_iter(sc, p, binv, *m[2:], *r, s) for p, m, r, s in zip(S, M, RR, st)]
        st = lax.fori_loop(0, ITERS - 1, body, st)
        for i, (p, m, s) in enumerate(zip(S, M, st)):
            x, y = sink_out(sc, p, m[0], m[1], KJ[i].astype(F32), s, W)
            fresh = jnp.where(P[i] < n, 1.0, 0.0)
            own[A[i], KEYS:] = own[A[i], KEYS:] + jnp.broadcast_to(x * fresh, (SLAB - KEYS, KEYS))
            slots[Z[i][0], Z[i][1], KEYS:] = jnp.broadcast_to(y, (SLAB - KEYS, KEYS)).astype(BF)


VM = pl.BlockSpec(memory_space=pltpu.VMEM)
SM = pl.BlockSpec(memory_space=pltpu.SMEM)
DMA = pltpu.SemaphoreType.DMA
LIMIT = 56 * 2**20


def local(descriptors, counts, visible, pair_list, pair_count, w_attend, w_value, w_output, w_hidden, norm_gain, w_down, w_match, unassigned_bucket):
    V = pltpu.VMEM
    full, tables = pl.pallas_call(
        gather_kernel,
        out_shape=(jax.ShapeDtypeStruct((OWN, SLAB, D), BF), jax.ShapeDtypeStruct((REACH + 1, 8, 128), jnp.int32)),
        in_specs=[VM, SM, VM, VM, SM],
        out_specs=(VM, VM),
        scratch_shapes=[V((SUBS, 16, KEYS), BF), V((8, 128), jnp.int32), DMA((2, SUBS - 1)), DMA((2, SUBS - 1)), DMA((REACH,)), DMA((REACH,))],
        compiler_params=pltpu.CompilerParams(collective_id=0, has_side_effects=True, vmem_limit_bytes=LIMIT),
    )(descriptors, counts, visible, pair_list, pair_count)
    landed = pl.pallas_call(
        fetch_kernel,
        out_shape=jax.ShapeDtypeStruct((REACH, PER, SLAB, D), BF),
        in_specs=[SM, VM],
        out_specs=VM,
        scratch_shapes=[V((REACH, PER, SLAB, D), BF), DMA((REACH,)), DMA((REACH,))],
        compiler_params=pltpu.CompilerParams(collective_id=1, has_side_effects=True, vmem_limit_bytes=LIMIT),
    )(tables, full)
    own, slots = pl.pallas_call(
        work_kernel,
        out_shape=(jax.ShapeDtypeStruct((OWN, SLAB, D), F32), jax.ShapeDtypeStruct((REACH, PER, SLAB, D), BF)),
        in_specs=[SM] + [VM] * 10,
        out_specs=(VM, VM),
        scratch_shapes=[V((256, 256), BF), V((256, 256), BF), V((512, 512), BF), V((256, 512), BF), V((256, 256), BF), V((512, 128), F32), V((256, 256), BF), V((8, 256, 256), F32), pltpu.SMEM((2, 16), jnp.int32)],
        compiler_params=pltpu.CompilerParams(vmem_limit_bytes=LIMIT),
    )(tables, full, landed, unassigned_bucket.reshape(1, 1), w_attend, w_value, w_output, w_hidden, norm_gain.reshape(1, -1), w_down, w_match)
    return pl.pallas_call(
        give_kernel,
        out_shape=(jax.ShapeDtypeStruct((OWN, ROWS, D), BF), jax.ShapeDtypeStruct((OWN, ROWS), F32)),
        in_specs=[SM, VM, VM],
        out_specs=(VM, VM),
        scratch_shapes=[
            V((REACH, PER, SLAB, D), BF), V((KEYS, D), BF), V((SUBS, OWN, ROWS, D), BF), V((SUBS - 1, OWN, ROWS, D), BF),
            V((OWN, KEYS), F32), V((SUBS - 1, OWN, KEYS), F32),
            DMA((REACH,)), DMA((REACH,)), DMA((2, SUBS - 1)), DMA((2, SUBS - 1)),
        ],
        compiler_params=pltpu.CompilerParams(collective_id=2, has_side_effects=True, vmem_limit_bytes=LIMIT),
    )(tables, own, slots)


def solution(mesh):
    placed = (P("img", "sub", None), P("img"), P("img", "sub"), P("img", None), P("img")) + (P(),) * 8
    return jax.shard_map(local, mesh=mesh, in_specs=placed, out_specs=(P("img", "sub", None), P("img", "sub")), check_vma=False)
```

time: 660 us -> 173 us (0.26); the launches traced: 651 us -> 171 us
  other arithmetic: 276 us -> 0 us
  Pallas kernels: 0 us -> 165 us
  starting transfers between devices: 152 us -> 0 us
  matrix products: 104 us -> 0 us
  loops' own time: 40.8 us -> 0 us
  local copies, waits for them, and re-layouts: 40.1 us -> 4.3 us
  between operations: 15.2 us -> 1.95 us
  blocking collectives: 12.9 us -> 0 us
  waiting for transfers between devices: 9.89 us -> 0 us
    pallas_call x0 -> x4, Pallas kernels: none -> 165 us  [the longest x1 59.9 us: local(): pl.pallas_call(give_kernel, out_shape=(jax.ShapeDtypeStruct((OWN, ROWS, D...]
    reduce_sum x192 -> x0, other arithmetic: 145 us -> none  [the longest x80 71 us: entropic_transport_iterate(): col_pot = log_cols - jax.nn.logsumexp(coupling + row_pot[:, None], axis=0)]
    ppermute x30 -> x0, starting transfers between devices: 135 us -> none  [shifted(): lax.ppermute(shard, axis, [(i, (i + by) % size) for i in range(size)])]
    reduce_max x160 -> x0, other arithmetic: 124 us -> none  [the longest x80 63.4 us: entropic_transport_iterate(): col_pot = log_cols - jax.nn.logsumexp(coupling + row_pot[:, None], axis=0)]
    dot_general x125 -> x0, matrix products: 94.3 us -> none  [the longest x56 59.3 us: project(): jnp.dot(features, weight, preferred_element_type=jnp.float32)]
    another operation x1 -> x0, loops' own time: 40.8 us -> none  [local(): lax.map(one_pair, (partner_full, partner_mask, mine_local))]
    dynamic_slice x57 -> x0, local copies, waits for them, and re-layouts: 23.3 us -> none  [the longest x24 12.9 us: local(): lax.map(one_pair, (partner_full, partner_mask, mine_local))]
    all_to_all x4 -> x0, starting transfers between devices: 16.8 us -> none  [the longest x1 4.31 us: local(): lax.all_to_all(target_marginal_weight, 'sub', split_axis=1, concat_axis=0...]
  transfers between devices with their start and end apart: 37 -> 0, of which waited for: 3 -> 0; matrix products, arithmetic and copies ran while one was open for 3% -> 0% of each run, Pallas kernels for 0% -> 0%
where the time goes in v1:
time: 173 us; the launch traced here: 171 us
  Pallas kernels  165 us (95%)
  local copies, waits for them, and re-layouts  4.3 us (2%)
  between operations  1.95 us (1%)
    pallas_call x1, Pallas kernels, local(): pl.pallas_call(give_kernel, out_shape=(jax.ShapeDtypeStruct((OWN, ROWS, D...  59.9 us
    pallas_call x1, Pallas kernels, local(): pl.pallas_call(work_kernel, out_shape=(jax.ShapeDtypeStruct((OWN, SLAB, D...  49.5 us
    pallas_call x1, Pallas kernels, local(): pl.pallas_call(gather_kernel, out_shape=(jax.ShapeDtypeStruct((OWN, SLAB,...  31.1 us
    pallas_call x1, Pallas kernels, local(): pl.pallas_call(fetch_kernel, out_shape=jax.ShapeDtypeStruct((REACH, PER,...  24.7 us
    unnamed x3, local copies, waits for them, and re-layouts  4.3 us

profile of v1, /device:TPU:1, one launch (start us, length us, event | category | flops | bytes accessed | tf_op | source)
XLA Modules:
  0.0 171.5 jit_solution(15598477960667825282)
XLA Ops:
  1.9 1.4 copy.15.pairs
  3.3 31.1 %shard_map.140 = (bf16[8,272,256]{2,1,0:T(8,128)(2,1)}, s32[7,8,128]{2,1,0:T(8,128)}) custom-call(bf16[8,64,256]{2,1,0:T(8,128)(2,1)} %desc.1, s32[8]{0:T(128)} %counts.1, s32[8,64]{1,0:T(8,128)} %visible.1, s32[32,2]{1,0:T(8,128)} %copy.15.pairs, s32[1]{0:T(128)S(6)} %copy.18.pair_count), custom_call_target="tpu_custom_call" | custom-call | tf_op jit(solution)/shard_map/pallas_call | solution.py:428
  34.4 24.7 %shard_map.141.landed = bf16[6,2,272,256]{3,2,1,0:T(8,128)(2,1)} custom-call(s32[7,8,128]{2,1,0:T(8,128)} %get-tuple-element.6.tables, bf16[8,272,256]{2,1,0:T(8,128)(2,1)} %get-tuple-element.7.full), custom_call_target="tpu_custom_call" | custom-call | tf_op jit(solution)/shard_map/pallas_call | solution.py:436
  59.1 49.5 %shard_map.142 = (f32[8,272,256]{2,1,0:T(8,128)}, bf16[6,2,272,256]{3,2,1,0:T(8,128)(2,1)}) custom-call(s32[7,8,128]{2,1,0:T(8,128)} %get-tuple-element.6.tables, bf16[8,272,256]{2,1,0:T(8,128)(2,1)} %get-tuple-element.7.full, bf16[6,2,272,256]{3,2,1,0:T(8,128)(2,1)} %shard_map.141.landed, f32[1,1]{1,0:T(1,128)} %bitcast.2.binr, bf16[256,256]{1,0:T(8,128)(2,1)} %wa.1, ...), custom_call_target="tpu_custom_call" | custom-call | tf_op jit(solution)/shard_map/pallas_call | solution.py:444
  108.6 59.9 %shard_map.143 = (bf16[8,64,256]{2,1,0:T(8,128)(2,1)}, f32[8,64]{1,0:T(8,128)}) custom-call(s32[7,8,128]{2,1,0:T(8,128)} %get-tuple-element.6.tables, f32[8,272,256]{2,1,0:T(8,128)} %get-tuple-element.8.own, bf16[6,2,272,256]{3,2,1,0:T(8,128)(2,1)} %get-tuple-element.9.slots), custom_call_target="tpu_custom_call" | custom-call | tf_op jit(solution)/shard_map/pallas_call | solution.py:452
  168.5 1.7 copy.20
  170.2 1.3 copy.21

commit v2 on v1

v2 whole, which is shorter than its diff:
```python
import math

import jax
import jax.numpy as jnp
from jax import lax
from jax.experimental import pallas as pl
from jax.experimental.pallas import tpu as pltpu
from jax.sharding import PartitionSpec as P

BF = jnp.bfloat16
F32 = jnp.float32
I32 = jnp.int32
LOG2E = 1.4426950408889634
FORGET = 30.0 * LOG2E
HEADS = 4
ITERS = 10
KEYS = 256
D = 256
WIN = 3
REACH = 2 * WIN
MOST = 6
OWN = 8
ROWS = 64
SUBS = 4
JOBS = 8
MESH = pl.DeviceIdType.MESH
LIMIT = 56 * 2**20


def nn(a, b):
    return lax.dot_general(a, b, (((1,), (0,)), ((), ())), preferred_element_type=F32)


def nt(a, b):
    return lax.dot_general(a, b, (((1,), (1,)), ((), ())), preferred_element_type=F32)


def eye(n):
    up = lax.broadcasted_iota(I32, (n, n), 0)
    return (up == lax.broadcasted_iota(I32, (n, n), 1)).astype(BF)


def to_col(row, ident):
    return nt(ident, jnp.broadcast_to(row, (128, row.shape[1])))


def prepare(wv, wo, wh, gain, wd, wm, wvT, woT, whT, wdT, wmT, gcol):
    ident = eye(256)
    wvT[...] = nt(ident, wv[...]).astype(BF)
    woT[...] = nt(ident, wo[...]).astype(BF)
    wmT[...] = nt(ident, wm[...]).astype(BF)
    for a in range(0, 512, 256):
        for b in range(0, 512, 256):
            whT[a : a + 256, b : b + 256] = nt(ident, wh[b : b + 256, a : a + 256]).astype(BF)
    for b in range(0, 512, 256):
        wdT[:, b : b + 256] = nt(ident, wd[b : b + 256, :]).astype(BF)
    same = lax.broadcasted_iota(I32, (128, 128), 0) == lax.broadcasted_iota(I32, (128, 128), 1)
    for q in range(0, 512, 128):
        spread = jnp.broadcast_to(gain[:, q : q + 128], (128, 128))
        column = jnp.sum(jnp.where(same, spread, 0.0), axis=1, keepdims=True)
        gcol[q : q + 128, :] = jnp.broadcast_to(column, (128, 128))


def attention(a_other, a_self, vT_other, bias, ident):
    outs = []
    ones = jnp.ones((16, KEYS), BF)
    aT = nt(ident, a_self).astype(BF)
    for h in range(HEADS):
        sl = slice(h * 64, h * 64 + 64)
        s = nn(a_other[:, sl], aT[sl]) * (LOG2E / 8.0) + bias
        top = jnp.max(s, axis=0, keepdims=True)
        e = jnp.exp2(s - top).astype(BF)
        r = nn(jnp.concatenate([vT_other[sl, :], ones], axis=0), e)
        outs.append((r[:64] * (1.0 / r[64:65])).astype(BF))
    return jnp.concatenate(outs, axis=0)


def refine(x, msgT, w):
    outs = []
    gain = w["gcol"][...]
    sentT = nn(w["woT"][...], msgT).astype(BF)
    for c in range(0, KEYS, 128):
        hid = nt(w["whT"][:, :256], x[c : c + 128]) + nn(w["whT"][:, 256:], sentT[:, c : c + 128])
        mean = jnp.sum(hid, axis=0, keepdims=True) * (1.0 / 512)
        cen = hid - mean
        var = jnp.sum(cen * cen, axis=0, keepdims=True) * (1.0 / 512)
        normed = cen * lax.rsqrt(var + 1e-5) * gain
        outs.append((0.5 * normed * (1.0 + lax.erf(normed * math.sqrt(0.5)))).astype(BF))
    return nn(w["wdT"][...], jnp.concatenate(outs, axis=1)).astype(BF)


def pair_scores(xi, ki, xj, kj, w):
    ident = w["ident"][...]
    bi = (to_col(ki, ident) - 1.0) * 1e30
    bj = (to_col(kj, ident) - 1.0) * 1e30
    bi = jnp.concatenate([bi, bi], axis=1)
    bj = jnp.concatenate([bj, bj], axis=1)
    ai = nn(xi, w["wa"][...]).astype(BF)
    aj = nn(xj, w["wa"][...]).astype(BF)
    viT = nt(w["wvT"][...], xi).astype(BF)
    vjT = nt(w["wvT"][...], xj).astype(BF)
    diT = refine(xi, attention(aj, ai, vjT, bj, ident), w)
    djT = refine(xj, attention(ai, aj, viT, bi, ident), w)
    riT = (nt(ident, xi) + diT.astype(F32)).astype(BF)
    rjT = (nt(ident, xj) + djT.astype(F32)).astype(BF)
    mi = nn(w["wmT"][...], riT).astype(BF)
    mj = nn(w["wmT"][...], rjT).astype(BF)
    scores = nn(nt(ident, mi).astype(BF), mj) * (LOG2E / 16.0)
    return nt(ident, diT).astype(BF), nt(ident, djT).astype(BF), scores


def marginals(ki, kj, ident):
    m = jnp.sum(ki, axis=1, keepdims=True)
    n = jnp.sum(kj, axis=1, keepdims=True)
    total = m + n
    off = -jnp.log2(jnp.maximum(total, 1.0))
    kic = to_col(ki.astype(BF), ident)[:, :1]
    lr = off - FORGET * (1.0 - kic)
    lc = off - FORGET * (1.0 - kj)
    lrb = jnp.log2(jnp.maximum(n, 1.0)) + off
    lcb = jnp.log2(jnp.maximum(m, 1.0)) + off
    return total, kic, lr, lc, lrb, lcb


def sink_first(c, bucket, lr, lc, lrb, lcb):
    top = jnp.maximum(jnp.max(c, axis=1, keepdims=True), bucket)
    s = jnp.sum(jnp.exp2(c - top), axis=1, keepdims=True) + jnp.exp2(bucket - top)
    f = lr - top - jnp.log2(s)
    fb = lrb - bucket - math.log2(257.0)
    t = jnp.sum(jnp.exp2(c + f), axis=0, keepdims=True) + jnp.exp2(bucket + fb)
    tb = jnp.sum(jnp.exp2(bucket + f), axis=0, keepdims=True) + jnp.exp2(bucket + fb)
    return f, fb, lc - jnp.log2(t), lcb - jnp.log2(tb)


def sink_next(c, bucket, lr, lc, lrb, lcb, r, rb, state):
    f, fb, g, gb = state
    eb = jnp.exp2(bucket + fb + g)
    ebb = jnp.exp2(bucket + fb + gb)
    ub = rb / (jnp.sum(eb, axis=1, keepdims=True) + ebb)
    p = jnp.exp2(c + g + f)
    b = jnp.exp2((bucket + gb) + f)
    u = r / (jnp.sum(p, axis=1, keepdims=True) + b)
    t = eb * ub + jnp.sum(p * u, axis=0, keepdims=True)
    tb = ebb * ub + jnp.sum(b * u, axis=0, keepdims=True)
    return f + jnp.log2(u), fb + jnp.log2(ub), g + lc - jnp.log2(t), gb + lcb - jnp.log2(tb)


def sink_out(c, total, kic, kj, state):
    f, fb, g, gb = state
    plan = jnp.exp2(c + f + g)
    mi = (jnp.sum(plan, axis=1, keepdims=True) * total * kic).astype(BF)
    mj = (jnp.sum(plan, axis=0, keepdims=True) * total * kj).astype(BF)
    first = (lax.broadcasted_iota(I32, (16, 128), 1) == 0).astype(BF)
    return nt(first, jnp.broadcast_to(mi, (KEYS, 128)))[:1], mj.astype(F32)


def row_of(block, index):
    at = lax.broadcasted_iota(I32, block.shape, 0)
    return jnp.sum(jnp.where(at == index, block, 0.0), axis=0, keepdims=True)


def job_of(tab, q, sub):
    code = tab[0, q * SUBS + sub]
    return (code >> 8) & 7, (code >> 12) & 1


def do_scores(q, tab, sub, allx, okeep, jkeep, w, dmine, dother, sc):
    mine, swap = job_of(tab, q, sub)
    first = jnp.where(swap == 1, OWN + q, mine)
    second = jnp.where(swap == 1, mine, OWN + q)
    km = row_of(okeep[...], mine)
    ko = row_of(jkeep[...], q)
    ki = jnp.where(swap == 1, ko, km).astype(BF)
    kj = jnp.where(swap == 1, km, ko).astype(BF)
    di, dj, s = pair_scores(allx[first], ki, allx[second], kj, w)
    dmine[q] = jnp.where(swap == 1, dj, di)
    dother[q] = jnp.where(swap == 1, di, dj)
    sc[q] = s


def do_masses(jobs, tab, sub, okeep, jkeep, bucket, w, mm, mo, sc):
    ident = w["ident"][...]
    swaps, margs, states, kjs = [], [], [], []
    for q in jobs:
        mine, swap = job_of(tab, q, sub)
        km = row_of(okeep[...], mine)
        ko = row_of(jkeep[...], q)
        ki = jnp.where(swap == 1, ko, km)
        kj = jnp.where(swap == 1, km, ko)
        marg = marginals(ki, kj, ident)
        swaps.append(swap)
        kjs.append(kj)
        margs.append(marg)
        states.append(sink_first(sc[q], bucket, *marg[2:]))
    sums = [(jnp.exp2(m[2]), jnp.exp2(m[4])) for m in margs]

    def sweep(_, states):
        return [sink_next(sc[q], bucket, *m[2:], *r, s) for q, m, r, s in zip(jobs, margs, sums, states)]

    states = lax.fori_loop(0, ITERS - 1, sweep, states)
    for q, m, s, kj, swap in zip(jobs, margs, states, kjs, swaps):
        a, b = sink_out(sc[q], m[0], m[1], kj, s)
        mm[q] = jnp.broadcast_to(jnp.where(swap == 1, b, a), (8, KEYS))
        mo[q] = jnp.broadcast_to(jnp.where(swap == 1, a, b), (8, KEYS))


def step_of(turn):
    return (turn // 2 + 1) * (1 - 2 * (turn % 2))


def places():
    n = lax.axis_size("img")
    me = lax.axis_index("img")
    sub = lax.axis_index("sub")
    others = [lax.rem(me + step_of(t) + n, n) for t in range(REACH)]
    peers = [lax.rem(sub + d, SUBS) for d in range(1, SUBS)]
    return me, sub, others, peers


def greet(others, peers):
    barrier = pltpu.get_barrier_semaphore()
    for h in others:
        pl.semaphore_signal(barrier, inc=1, device_id={"img": h}, device_id_type=MESH)
    for s in peers:
        pl.semaphore_signal(barrier, inc=1, device_id={"sub": s}, device_id_type=MESH)
    pl.semaphore_wait(barrier, len(others) + len(peers))


def send(src, dst, ssem, rsem, to):
    return pltpu.make_async_remote_copy(
        src_ref=src, dst_ref=dst, send_sem=ssem, recv_sem=rsem, device_id=to, device_id_type=MESH
    )


def own_rows(pairs, live_count, me, img_count):
    first = pairs[:, 0:1]
    second = pairs[:, 1:2]
    slots = pairs.shape[0]
    row_ids = lax.broadcasted_iota(I32, (slots, 1), 0)
    ahead = (second >> 3) - me
    ahead = jnp.where(ahead < 0, ahead + img_count, ahead)
    turn = jnp.where(ahead <= WIN, 2 * (ahead - 1), 2 * (img_count - ahead - 1) + 1)
    live = row_ids < live_count
    key = jnp.where(live, turn, 15)
    code = 1 + (first & 7) * 8 + (second & 7)
    up = lax.broadcasted_iota(I32, (slots, slots), 0)
    across = lax.broadcasted_iota(I32, (slots, slots), 1)
    key_row = jnp.sum(jnp.where(up == across, key, 0), axis=0, keepdims=True)
    rank = jnp.sum(jnp.where((key_row == key) & (across < up), 1, 0), axis=1, keepdims=True)
    lanes = lax.broadcasted_iota(I32, (slots, 128), 1)
    lane = lax.broadcasted_iota(I32, (1, 128), 1)
    rows = []
    for k in (key, key ^ 1):
        at = jnp.where(live, k * 8 + rank, -1)
        codes = jnp.sum(jnp.where(lanes == at, code, 0), axis=0, keepdims=True)
        counts = jnp.sum(jnp.where((lanes == 64 + k) & live, 1, 0), axis=0, keepdims=True)
        row = codes + counts
        rows.append(jnp.where((lane >= 80) & (lane < 88), live_count, row))
    return rows


def plan_rows(own, near, live_count):
    r8 = lax.broadcasted_iota(I32, (8, 128), 0)
    l8 = lax.broadcasted_iota(I32, (8, 128), 1)
    mine = jnp.where(l8 < 64, l8 >> 3, l8 & 7)
    from_near = jnp.sum(jnp.where((mine == r8) & (r8 < REACH), near, 0), axis=0, keepdims=True)
    slots = 64
    lanes = lax.broadcasted_iota(I32, (slots, 128), 1)
    slot = lax.broadcasted_iota(I32, (slots, 1), 0)
    turn = slot >> 3
    u = slot & 7
    own_all = jnp.broadcast_to(own, (slots, 128))
    near_all = jnp.broadcast_to(from_near, (slots, 128))

    def pick(table, lane):
        return jnp.sum(jnp.where(lanes == lane, table, 0), axis=1, keepdims=True)

    n_own = pick(own_all, 64 + turn)
    n_near = pick(near_all, 64 + turn)
    l_near = pick(near_all, 80 + turn)

    def sixth(value):
        return (jnp.maximum(value, 0) * 43) >> 8

    give = jnp.maximum(jnp.minimum(jnp.minimum(sixth(live_count - l_near), n_own), MOST - n_near), 0)
    take = jnp.maximum(jnp.minimum(jnp.minimum(sixth(l_near - live_count), n_near), MOST - n_own), 0)
    kept = n_own - give
    near_kept = n_near - take
    own_code = pick(own_all, turn * 8 + u) - 1
    near_code = pick(near_all, turn * 8 + u) - 1
    taken_code = pick(near_all, turn * 8 + near_kept + u - kept) - 1
    given_code = pick(own_all, turn * 8 + kept + u - near_kept) - 1
    live = (u < kept + take) & (turn < REACH)
    image = jnp.where(u < kept, own_code >> 3, taken_code & 7)
    swap = jnp.where(u < kept, 0, 1)
    asked = (u < near_kept + give) & (turn < REACH)
    sends = jnp.where(u < near_kept, near_code & 7, given_code >> 3)
    eye64 = lax.broadcasted_iota(I32, (slots, slots), 0) == lax.broadcasted_iota(I32, (slots, slots), 1)
    live_row = jnp.sum(jnp.where(eye64, jnp.where(live, 1, 0), 0), axis=0, keepdims=True)
    short = lax.broadcasted_iota(I32, (slots, slots), 1)
    place = jnp.sum(jnp.where(short < slot, live_row, 0), axis=1, keepdims=True)
    count = jnp.sum(live_row, axis=1, keepdims=True)

    def put(lane, value):
        return jnp.sum(jnp.where(lanes == lane, value, 0), axis=0, keepdims=True)

    by_place = put(jnp.where(live, place, -1), 1 + slot + image * 256 + swap * 4096)
    by_slot = put(slot, jnp.where(asked, 1 + sends, 0))
    places_row = put(slot, jnp.where(live, place, 0))
    row = lax.broadcasted_iota(I32, (8, 128), 0)
    out = jnp.where(row == 0, by_place, jnp.where(row == 1, by_slot, jnp.where(row == 2, places_row, count)))
    return out


def meet_kernel(pairs, pair_count, wv, wo, wh, gain, wd, wm, tab, wvT, woT, whT, wdT, wmT, gcol, told, near, ssem, rsem):
    me, sub, others, peers = places()
    own, out = own_rows(pairs[...], pair_count[0], me, lax.axis_size("img"))
    told[...] = jnp.broadcast_to(out, (8, 128))
    greet(others, [])
    copies = [send(told, near.at[t ^ 1], ssem.at[t], rsem.at[t ^ 1], {"img": others[t]}) for t in range(REACH)]
    for copy in copies:
        copy.start()
    prepare(wv, wo, wh, gain, wd, wm, wvT, woT, whT, wdT, wmT, gcol)
    for copy in copies:
        copy.wait()
    row = lax.broadcasted_iota(I32, (8, 128), 0)
    table = jnp.zeros((8, 128), I32)
    for t in range(REACH):
        table = jnp.where(row == t, near[t], table)
    tab[...] = plan_rows(own, table, pair_count[0])


def sent_image(tab, t, u):
    return tab[1, t * 8 + u]


def fetch_kernel(tab, desc, counts, visible, allx, okeep, jkeep, zst, zland, zms, zml, yst, yms, yml, omask, zsem, zrem, ysem, yrem, osem, orem):
    me, sub, others, peers = places()
    rows = pl.ds(pl.multiple_of(sub * ROWS, ROWS), ROWS)
    for a in range(OWN):
        allx[a, rows, :] = desc[a]
    image = lax.broadcasted_iota(I32, (OWN, ROWS), 0)
    found = jnp.zeros((OWN, ROWS), I32)
    for a in range(OWN):
        found = jnp.where(image == a, counts[a], found)
    spot = lax.broadcasted_iota(I32, (OWN, ROWS), 1) + sub * ROWS
    kept = jnp.where((spot < found) & (visible[...] > 0), 1.0, 0.0)
    wide = jnp.concatenate([kept] * SUBS, axis=1)
    lane = lax.broadcasted_iota(I32, (OWN, KEYS), 1)
    wide = jnp.where((lane >= sub * ROWS) & (lane < sub * ROWS + ROWS), wide, 0.0)
    omask[0] = wide
    greet(others, peers)
    zcopies = []
    for t in (4, 5, 2, 3, 0, 1):
        line = lax.broadcasted_iota(I32, (8, KEYS), 0)
        masks = jnp.zeros((8, KEYS), F32)
        for u in range(MOST):
            which = jnp.maximum(sent_image(tab, t, u) - 1, 0)
            zst[t, u] = desc[which]
            masks = jnp.where(line == u, row_of(wide, which), masks)
        zms[t] = masks
        to = {"img": others[t]}
        zcopies.append(send(zst.at[t], zland.at[t ^ 1], zsem.at[0, t], zrem.at[0, t ^ 1], to))
        zcopies.append(send(zms.at[t], zml.at[t ^ 1], zsem.at[1, t], zrem.at[1, t ^ 1], to))
        zcopies[-2].start()
        zcopies[-1].start()
    ocopies = []
    for d in range(1, SUBS):
        to = {"sub": peers[d - 1]}
        mine = allx.at[0:OWN, rows, :]
        ocopies.append(send(mine, mine, osem.at[0, d - 1], orem.at[0, d - 1], to))
        ocopies.append(send(omask.at[0], omask.at[d], osem.at[1, d - 1], orem.at[1, d - 1], to))
    for copy in ocopies:
        copy.start()
    for copy in zcopies:
        copy.wait()
    ycopies = []
    line = lax.broadcasted_iota(I32, (JOBS, KEYS), 0)
    zmasks = jnp.concatenate([zml[t] for t in range(REACH)], axis=0)
    for q in range(JOBS):
        for d in range(SUBS):
            worker = sub if d == 0 else peers[d - 1]
            slot = jnp.maximum((tab[0, q * SUBS + worker] & 255) - 1, 0)
            t, u = slot >> 3, slot & 7
            masks = jnp.where(line == q, row_of(zmasks, slot), 0.0 if q == 0 else yms[d])
            yms[d] = masks
            if d == 0:
                allx[OWN + q, rows, :] = zland[t, u]
            else:
                yst[d - 1, q] = zland[t, u]
                copy = send(
                    yst.at[d - 1, q],
                    allx.at[OWN + q, rows, :],
                    ysem.at[q, d - 1],
                    yrem.at[q, d - 1],
                    {"sub": worker},
                )
                copy.start()
                ycopies.append(copy)
    for d in range(1, SUBS):
        copy = send(yms.at[d], yml.at[d - 1], ysem.at[JOBS, d - 1], yrem.at[JOBS, d - 1], {"sub": peers[d - 1]})
        copy.start()
        ycopies.append(copy)
    for copy in ocopies:
        copy.wait()
    okeep[...] = omask[0] + omask[1] + omask[2] + omask[3]
    for copy in ycopies:
        copy.wait()
    jkeep[...] = yms[0] + yml[0] + yml[1] + yml[2]


def work_kernel(tab, allx, okeep, jkeep, bucket, wa, wvT, woT, whT, wdT, wmT, gcol, dmine, dother, mm, mo, ident, sc):
    sub = lax.axis_index("sub")
    ident[...] = eye(256)
    w = dict(wa=wa, wvT=wvT, woT=woT, whT=whT, wdT=wdT, wmT=wmT, gcol=gcol, ident=ident)
    n = (tab[3, 0] + (SUBS - 1) - sub) >> 2
    binv = bucket[...] * LOG2E

    @pl.loop(0, n)
    def _(q):
        do_scores(q, tab, sub, allx, okeep, jkeep, w, dmine, dother, sc)

    @pl.loop(0, n >> 1)
    def _(p):
        do_masses([2 * p, 2 * p + 1], tab, sub, okeep, jkeep, binv, w, mm, mo, sc)

    @pl.when((n & 1) == 1)
    def _():
        do_masses([n - 1], tab, sub, okeep, jkeep, binv, w, mm, mo, sc)


def give_kernel(tab, dmine, dother, mm, mo, upd, mass, yb, ymst, yml, zst, zms, zret, zmr, parts, got, mparts, mgot, ysem, yrem, zsem, zrem, osem, orem):
    me, sub, others, peers = places()
    rows = pl.ds(pl.multiple_of(sub * ROWS, ROWS), ROWS)
    mline = lax.broadcasted_iota(I32, (JOBS, KEYS), 0)
    masks = jnp.zeros((JOBS, KEYS), F32)
    for q in range(JOBS):
        masks = jnp.where(mline == q, mo[q], masks)
    ymst[...] = masks
    greet(others, peers)
    ycopies = []
    for q in range(JOBS):
        for d in range(1, SUBS):
            p = peers[d - 1]
            part = dother.at[q, pl.ds(pl.multiple_of(p * ROWS, ROWS), ROWS), :]
            ycopies.append(send(part, yb.at[q, sub], ysem.at[q, d - 1], yrem.at[q, d - 1], {"sub": p}))
    for d in range(1, SUBS):
        ycopies.append(send(ymst, yml.at[sub], ysem.at[JOBS, d - 1], yrem.at[JOBS, d - 1], {"sub": peers[d - 1]}))
    for copy in ycopies:
        copy.start()
    for q in range(JOBS):
        yb[q, sub] = dother[q, rows, :]
    yml[sub] = masks
    for copy in ycopies:
        copy.wait()
    ymasses = jnp.concatenate([yml[s] for s in range(SUBS)], axis=0)
    zcopies = [None] * REACH
    for t in (4, 5, 2, 3, 0, 1):
        line = lax.broadcasted_iota(I32, (8, KEYS), 0)
        back = jnp.zeros((8, KEYS), F32)
        for u in range(MOST):
            place = tab[2, t * 8 + u]
            zst[t, u] = yb[place >> 2, place & 3]
            back = jnp.where(line == u, row_of(ymasses, (place & 3) * JOBS + (place >> 2)), back)
        zms[t] = back
        to = {"img": others[t]}
        zcopies[t] = [
            send(zst.at[t], zret.at[t ^ 1], zsem.at[0, t], zrem.at[0, t ^ 1], to),
            send(zms.at[t], zmr.at[t ^ 1], zsem.at[1, t], zrem.at[1, t ^ 1], to),
        ]
        for copy in zcopies[t]:
            copy.start()
    n = (tab[3, 0] + (SUBS - 1) - sub) >> 2
    owners = [jnp.where(q < n, job_of(tab, q, sub)[0], -1) for q in range(JOBS)]
    for a in range(OWN):
        for s in range(SUBS):
            value = jnp.zeros((ROWS, D), F32)
            for q in range(JOBS):
                value = value + jnp.where(owners[q] == a, dmine[q, s * ROWS : s * ROWS + ROWS, :].astype(F32), 0.0)
            parts[s, a] = value.astype(BF)
        value = jnp.zeros((1, KEYS), F32)
        for q in range(JOBS):
            value = value + jnp.where(owners[q] == a, mm[q, 0:1, :], 0.0)
        mparts[a : a + 1, :] = value
    ocopies = []
    for d in range(1, SUBS):
        to = {"sub": peers[d - 1]}
        ocopies.append(send(parts.at[peers[d - 1]], got.at[d - 1], osem.at[0, d - 1], orem.at[0, d - 1], to))
        ocopies.append(send(mparts, mgot.at[d - 1], osem.at[1, d - 1], orem.at[1, d - 1], to))
    for copy in ocopies:
        copy.start()
    for copy in ocopies:
        copy.wait()
    for t in range(REACH):
        for copy in zcopies[t]:
            copy.wait()
    masses = mparts[...] + mgot[0] + mgot[1] + mgot[2]
    wants = [(t, u, sent_image(tab, t, u) - 1) for t in range(REACH) for u in range(MOST)]
    for a in range(OWN):
        value = parts[sub, a].astype(F32)
        for d in range(SUBS - 1):
            value = value + got[d, a].astype(F32)
        extra = jnp.zeros((1, KEYS), F32)
        for t, u, which in wants:
            value = value + jnp.where(which == a, zret[t, u].astype(F32), 0.0)
            extra = extra + jnp.where(which == a, zmr[t, u : u + 1, :], 0.0)
        upd[a] = value.astype(BF)
        masses = masses + jnp.where(mline == a, extra, 0.0)
    out = jnp.zeros((OWN, ROWS), F32)
    for s in range(SUBS):
        out = jnp.where(sub == s, masses[:, s * ROWS : s * ROWS + ROWS], out)
    mass[...] = out


VM = pl.BlockSpec(memory_space=pltpu.VMEM)
SM = pl.BlockSpec(memory_space=pltpu.SMEM)
DMA = pltpu.SemaphoreType.DMA


def shape(dims, kind=BF):
    return jax.ShapeDtypeStruct(dims, kind)


def talk(number):
    return pltpu.CompilerParams(collective_id=number, has_side_effects=True, vmem_limit_bytes=LIMIT)


def local(descriptors, counts, visible, pair_list, pair_count, w_attend, w_value, w_output, w_hidden, norm_gain, w_down, w_match, unassigned_bucket):
    V = pltpu.VMEM
    tab, *ready = pl.pallas_call(
        meet_kernel,
        out_shape=(shape((8, 128), I32), shape((256, 256)), shape((256, 256)), shape((512, 512)), shape((256, 512)), shape((256, 256)), shape((512, 128), F32)),
        in_specs=[VM, SM] + [VM] * 6,
        out_specs=(VM,) * 7,
        scratch_shapes=[V((8, 128), I32), V((REACH, 8, 128), I32), DMA((REACH,)), DMA((REACH,))],
        compiler_params=talk(0),
    )(pair_list, pair_count, w_value, w_output, w_hidden, norm_gain.reshape(1, -1), w_down, w_match)
    allx, okeep, jkeep = pl.pallas_call(
        fetch_kernel,
        out_shape=(shape((OWN + JOBS, KEYS, D)), shape((OWN, KEYS), F32), shape((JOBS, KEYS), F32)),
        in_specs=[SM, VM, SM, VM],
        out_specs=(VM,) * 3,
        scratch_shapes=[
            V((REACH, MOST, ROWS, D), BF), V((REACH, MOST, ROWS, D), BF), V((REACH, 8, KEYS), F32), V((REACH, 8, KEYS), F32),
            V((SUBS - 1, JOBS, ROWS, D), BF), V((SUBS, JOBS, KEYS), F32), V((SUBS - 1, JOBS, KEYS), F32), V((SUBS, OWN, KEYS), F32),
            DMA((2, REACH)), DMA((2, REACH)), DMA((JOBS + 1, SUBS - 1)), DMA((JOBS + 1, SUBS - 1)), DMA((2, SUBS - 1)), DMA((2, SUBS - 1)),
        ],
        compiler_params=talk(1),
    )(tab, descriptors, counts, visible)
    done = pl.pallas_call(
        work_kernel,
        out_shape=(shape((JOBS, KEYS, D)), shape((JOBS, KEYS, D)), shape((JOBS, 8, KEYS), F32), shape((JOBS, 8, KEYS), F32)),
        in_specs=[SM] + [VM] * 11,
        out_specs=(VM,) * 4,
        scratch_shapes=[V((256, 256), BF), V((JOBS, KEYS, KEYS), F32)],
        compiler_params=pltpu.CompilerParams(vmem_limit_bytes=LIMIT),
    )(tab, allx, okeep, jkeep, unassigned_bucket.reshape(1, 1), w_attend, *ready)
    return pl.pallas_call(
        give_kernel,
        out_shape=(shape((OWN, ROWS, D)), shape((OWN, ROWS), F32)),
        in_specs=[SM] + [VM] * 4,
        out_specs=(VM, VM),
        scratch_shapes=[
            V((JOBS, SUBS, ROWS, D), BF), V((JOBS, KEYS), F32), V((SUBS, JOBS, KEYS), F32),
            V((REACH, MOST, ROWS, D), BF), V((REACH, 8, KEYS), F32), V((REACH, MOST, ROWS, D), BF), V((REACH, 8, KEYS), F32),
            V((SUBS, OWN, ROWS, D), BF), V((SUBS - 1, OWN, ROWS, D), BF), V((OWN, KEYS), F32), V((SUBS - 1, OWN, KEYS), F32),
            DMA((JOBS + 1, SUBS - 1)), DMA((JOBS + 1, SUBS - 1)), DMA((2, REACH)), DMA((2, REACH)), DMA((2, SUBS - 1)), DMA((2, SUBS - 1)),
        ],
        compiler_params=talk(2),
    )(tab, *done)


def solution(mesh):
    placed = (P("img", "sub", None), P("img"), P("img", "sub"), P("img", None), P("img")) + (P(),) * 8
    return jax.shard_map(
        local, mesh=mesh, in_specs=placed, out_specs=(P("img", "sub", None), P("img", "sub")), check_vma=False
    )
```

time: 173 us -> 147 us (0.85)
  Pallas kernels: 165 us -> 140 us
    pallas_call x4, Pallas kernels: 165 us -> 140 us  [the longest x1 51.6 us: local(): pl.pallas_call(give_kernel, out_shape=(shape((OWN, ROWS, D)), shape((OWN,...]
where the time goes in v2:
time: 147 us; the launch traced here: 146 us
  Pallas kernels  140 us (95%)
  local copies, waits for them, and re-layouts  4.31 us (3%)
  between operations  1.95 us (1%)
    pallas_call x1, Pallas kernels, local(): pl.pallas_call(give_kernel, out_shape=(shape((OWN, ROWS, D)), shape((OWN,...  51.6 us
    pallas_call x1, Pallas kernels, local(): pl.pallas_call(work_kernel, out_shape=(shape((JOBS, KEYS, D)), shape((JOB...  35.7 us
    pallas_call x1, Pallas kernels, local(): pl.pallas_call(fetch_kernel, out_shape=(shape((OWN + JOBS, KEYS, D)), sha...  33.9 us
    pallas_call x1, Pallas kernels, local(): pl.pallas_call(meet_kernel, out_shape=(shape((8, 128), I32), shape((256,...  18.9 us
    unnamed x3, local copies, waits for them, and re-layouts  4.31 us

profile of v2, /device:TPU:1, one launch (start us, length us, event | category | flops | bytes accessed | tf_op | source)
XLA Modules:
  0.0 146.4 jit_solution(2495591869729947224)
XLA Ops:
  1.9 1.4 copy.15.pairs
  3.3 18.9 %shard_map.140 = (s32[8,128]{1,0:T(8,128)}, bf16[256,256]{1,0:T(8,128)(2,1)}, bf16[256,256]{1,0:T(8,128)(2,1)}, bf16[512,512]{1,0:T(8,128)(2,1)}, bf16[256,512]{...) custom-call(s32[32,2]{1,0:T(8,128)} %copy.15.pairs, s32[1]{0:T(128)S(6)} %copy.18.pair_count, ...), custom_call_target="tpu_custom_call" | custom-call | tf_op jit(solution)/shard_map/pallas_call | solution.py:530
  22.2 33.9 %shard_map.141 = (bf16[16,256,256]{2,1,0:T(8,128)(2,1)}, f32[8,256]{1,0:T(8,128)}, f32[8,256]{1,0:T(8,128)}) custom-call(s32[8,128]{1,0:T(8,128)} %get-tuple-element.16.tab, bf16[8,64,256]{2,1,0:T(8,128)(2,1)} %desc.1, s32[8]{0:T(128)} %counts.1, s32[8,64]{1,0:T(8,128)} %visible.1), custom_call_target="tpu_custom_call" | custom-call | tf_op jit(solution)/shard_map/pallas_call | solution.py:538
  56.1 35.7 %shard_map.142 = (bf16[8,256,256]{2,1,0:T(8,128)(2,1)}, bf16[8,256,256]{2,1,0:T(8,128)(2,1)}, f32[8,8,256]{2,1,0:T(8,128)}, f32[8,8,256]{2,1,0:T(8,128)}) custom-call(s32[8,128]{1,0:T(8,128)} %get-tuple-element.16.tab, bf16[16,256,256]{2,1,0:T(8,128)(2,1)} %get-tuple-element.17.allx, f32[8,256]{1,0:T(8,128)} %get-tuple-element.18.okeep, ...), custom_call_target="tpu_custom_call" | custom-call | tf_op jit(solution)/shard_map/pallas_call | solution.py:550
  91.8 51.6 %shard_map.143 = (bf16[8,64,256]{2,1,0:T(8,128)(2,1)}, f32[8,64]{1,0:T(8,128)}) custom-call(s32[8,128]{1,0:T(8,128)} %get-tuple-element.16.tab, bf16[8,256,256]{2,1,0:T(8,128)(2,1)} %get-tuple-element.26.dmine, bf16[8,256,256]{2,1,0:T(8,128)(2,1)} %get-tuple-element.27.dother, f32[8,8,256]{2,1,0:T(8,128)} %get-tuple-element.28.mm, ...), custom_call_target="tpu_custom_call" | custom-call | tf_op jit(solution)/shard_map/pallas_call | solution.py:558
  143.5 1.7 %copy.20 = bf16[8,64,256]{2,1,0:T(8,128)(2,1)} copy(bf16[8,64,256]{2,1,0:T(8,128)(2,1)} %get-tuple-element.32) | data formatting | bytes 524288
  145.2 1.3 copy.21

commit v3 on v2

--- a/solution.py
+++ b/solution.py
@@ -23,6 +23,8 @@
 ROWS = 64
 SUBS = 4
 JOBS = 8
+FIXED = 4
+EARLY = 2
 MESH = pl.DeviceIdType.MESH
 LIMIT = 56 * 2**20
 
@@ -164,24 +166,20 @@
     return (code >> 8) & 7, (code >> 12) & 1
 
 
-def do_scores(q, tab, sub, allx, okeep, jkeep, w, dmine, dother, sc):
+def do_scores(q, tab, sub, own, xo, okeep, jkeep, w):
     mine, swap = job_of(tab, q, sub)
-    first = jnp.where(swap == 1, OWN + q, mine)
-    second = jnp.where(swap == 1, mine, OWN + q)
+    xm = own[mine]
     km = row_of(okeep[...], mine)
     ko = row_of(jkeep[...], q)
     ki = jnp.where(swap == 1, ko, km).astype(BF)
     kj = jnp.where(swap == 1, km, ko).astype(BF)
-    di, dj, s = pair_scores(allx[first], ki, allx[second], kj, w)
-    dmine[q] = jnp.where(swap == 1, dj, di)
-    dother[q] = jnp.where(swap == 1, di, dj)
-    sc[q] = s
-
-
-def do_masses(jobs, tab, sub, okeep, jkeep, bucket, w, mm, mo, sc):
-    ident = w["ident"][...]
+    di, dj, scores = pair_scores(jnp.where(swap == 1, xo, xm), ki, jnp.where(swap == 1, xm, xo), kj, w)
+    return jnp.where(swap == 1, dj, di), jnp.where(swap == 1, di, dj), scores
+
+
+def do_masses(jobs, sc, tab, sub, okeep, jkeep, bucket, ident):
     swaps, margs, states, kjs = [], [], [], []
-    for q in jobs:
+    for q, (ref, at) in zip(jobs, sc):
         mine, swap = job_of(tab, q, sub)
         km = row_of(okeep[...], mine)
         ko = row_of(jkeep[...], q)
@@ -191,17 +189,18 @@
         swaps.append(swap)
         kjs.append(kj)
         margs.append(marg)
-        states.append(sink_first(sc[q], bucket, *marg[2:]))
+        states.append(sink_first(ref[at], bucket, *marg[2:]))
     sums = [(jnp.exp2(m[2]), jnp.exp2(m[4])) for m in margs]
 
     def sweep(_, states):
-        return [sink_next(sc[q], bucket, *m[2:], *r, s) for q, m, r, s in zip(jobs, margs, sums, states)]
+        return [sink_next(ref[at], bucket, *m[2:], *r, s) for (ref, at), m, r, s in zip(sc, margs, sums, states)]
 
     states = lax.fori_loop(0, ITERS - 1, sweep, states)
-    for q, m, s, kj, swap in zip(jobs, margs, states, kjs, swaps):
-        a, b = sink_out(sc[q], m[0], m[1], kj, s)
-        mm[q] = jnp.broadcast_to(jnp.where(swap == 1, b, a), (8, KEYS))
-        mo[q] = jnp.broadcast_to(jnp.where(swap == 1, a, b), (8, KEYS))
+    outs = []
+    for (ref, at), m, s, kj, swap in zip(sc, margs, states, kjs, swaps):
+        a, b = sink_out(ref[at], m[0], m[1], kj, s)
+        outs.append((jnp.where(swap == 1, b, a), jnp.where(swap == 1, a, b)))
+    return outs
 
 
 def step_of(turn):
@@ -334,11 +333,13 @@
     return tab[1, t * 8 + u]
 
 
-def fetch_kernel(tab, desc, counts, visible, allx, okeep, jkeep, zst, zland, zms, zml, yst, yms, yml, omask, zsem, zrem, ysem, yrem, osem, orem):
+def fetch_kernel(tab, desc, counts, visible, wa, wvT, woT, whT, wdT, wmT, gcol, own, xj, okeep, jkeep, dmine, dother, sc, ident, zst, zland, zms, zml, yst, yms, yml, omask, zsem, zrem, ysem, yrem, osem, orem):
     me, sub, others, peers = places()
     rows = pl.ds(pl.multiple_of(sub * ROWS, ROWS), ROWS)
+    ident[...] = eye(256)
+    w = dict(wa=wa, wvT=wvT, woT=woT, whT=whT, wdT=wdT, wmT=wmT, gcol=gcol, ident=ident)
     for a in range(OWN):
-        allx[a, rows, :] = desc[a]
+        own[a, rows, :] = desc[a]
     image = lax.broadcasted_iota(I32, (OWN, ROWS), 0)
     found = jnp.zeros((OWN, ROWS), I32)
     for a in range(OWN):
@@ -367,7 +368,7 @@
     ocopies = []
     for d in range(1, SUBS):
         to = {"sub": peers[d - 1]}
-        mine = allx.at[0:OWN, rows, :]
+        mine = own.at[:, rows, :]
         ocopies.append(send(mine, mine, osem.at[0, d - 1], orem.at[0, d - 1], to))
         ocopies.append(send(omask.at[0], omask.at[d], osem.at[1, d - 1], orem.at[1, d - 1], to))
     for copy in ocopies:
@@ -377,138 +378,188 @@
     ycopies = []
     line = lax.broadcasted_iota(I32, (JOBS, KEYS), 0)
     zmasks = jnp.concatenate([zml[t] for t in range(REACH)], axis=0)
+    slots = [[None] * SUBS for _ in range(JOBS)]
+    for d in range(SUBS):
+        worker = sub if d == 0 else peers[d - 1]
+        masks = jnp.zeros((JOBS, KEYS), F32)
+        for q in range(JOBS):
+            slots[q][d] = jnp.maximum((tab[0, q * SUBS + worker] & 255) - 1, 0)
+            masks = jnp.where(line == q, row_of(zmasks, slots[q][d]), masks)
+        yms[d] = masks
+    mcopies = []
+    for d in range(1, SUBS):
+        mcopies.append(send(yms.at[d], yml.at[d - 1], ysem.at[JOBS, d - 1], yrem.at[JOBS, d - 1], {"sub": peers[d - 1]}))
+        mcopies[-1].start()
     for q in range(JOBS):
-        for d in range(SUBS):
-            worker = sub if d == 0 else peers[d - 1]
-            slot = jnp.maximum((tab[0, q * SUBS + worker] & 255) - 1, 0)
-            t, u = slot >> 3, slot & 7
-            masks = jnp.where(line == q, row_of(zmasks, slot), 0.0 if q == 0 else yms[d])
-            yms[d] = masks
-            if d == 0:
-                allx[OWN + q, rows, :] = zland[t, u]
-            else:
-                yst[d - 1, q] = zland[t, u]
-                copy = send(
-                    yst.at[d - 1, q],
-                    allx.at[OWN + q, rows, :],
-                    ysem.at[q, d - 1],
-                    yrem.at[q, d - 1],
-                    {"sub": worker},
-                )
-                copy.start()
-                ycopies.append(copy)
-    for d in range(1, SUBS):
-        copy = send(yms.at[d], yml.at[d - 1], ysem.at[JOBS, d - 1], yrem.at[JOBS, d - 1], {"sub": peers[d - 1]})
-        copy.start()
-        ycopies.append(copy)
+        for d in range(1, SUBS):
+            yst[d - 1, q] = zland[slots[q][d] >> 3, slots[q][d] & 7]
+            copy = send(yst.at[d - 1, q], xj.at[q, rows, :], ysem.at[q, d - 1], yrem.at[q, d - 1], {"sub": peers[d - 1]})
+            copy.start()
+            ycopies.append(copy)
+        xj[q, rows, :] = zland[slots[q][0] >> 3, slots[q][0] & 7]
     for copy in ocopies:
         copy.wait()
     okeep[...] = omask[0] + omask[1] + omask[2] + omask[3]
-    for copy in ycopies:
+    for copy in mcopies:
         copy.wait()
     jkeep[...] = yms[0] + yml[0] + yml[1] + yml[2]
-
-
-def work_kernel(tab, allx, okeep, jkeep, bucket, wa, wvT, woT, whT, wdT, wmT, gcol, dmine, dother, mm, mo, ident, sc):
+    for q in range(EARLY):
+        for copy in ycopies[3 * q : 3 * q + 3]:
+            copy.wait()
+        dmine[q], dother[q], sc[q] = do_scores(q, tab, sub, own, xj[q], okeep, jkeep, w)
+    for copy in ycopies[3 * EARLY :]:
+        copy.wait()
+
+
+def work_kernel(tab, own, xj, okeep, jkeep, bucket, wa, wvT, woT, whT, wdT, wmT, gcol, dmine, dother, mm, mo, ident, sc):
     sub = lax.axis_index("sub")
     ident[...] = eye(256)
     w = dict(wa=wa, wvT=wvT, woT=woT, whT=whT, wdT=wdT, wmT=wmT, gcol=gcol, ident=ident)
-    n = (tab[3, 0] + (SUBS - 1) - sub) >> 2
+    n = ((tab[3, 0] + (SUBS - 1) - sub) >> 2) - FIXED
     binv = bucket[...] * LOG2E
 
     @pl.loop(0, n)
-    def _(q):
-        do_scores(q, tab, sub, allx, okeep, jkeep, w, dmine, dother, sc)
+    def _(p):
+        q = FIXED + p
+        dmine[p], dother[p], sc[p] = do_scores(q, tab, sub, own, xj[q], okeep, jkeep, w)
+
+    def masses(ps):
+        outs = do_masses([FIXED + p for p in ps], [(sc, p) for p in ps], tab, sub, okeep, jkeep, binv, ident[...])
+        for p, (a, b) in zip(ps, outs):
+            mm[p] = jnp.broadcast_to(a, (8, KEYS))
+            mo[p] = jnp.broadcast_to(b, (8, KEYS))
 
     @pl.loop(0, n >> 1)
     def _(p):
-        do_masses([2 * p, 2 * p + 1], tab, sub, okeep, jkeep, binv, w, mm, mo, sc)
+        masses([2 * p, 2 * p + 1])
 
     @pl.when((n & 1) == 1)
     def _():
-        do_masses([n - 1], tab, sub, okeep, jkeep, binv, w, mm, mo, sc)
-
-
-def give_kernel(tab, dmine, dother, mm, mo, upd, mass, yb, ymst, yml, zst, zms, zret, zmr, parts, got, mparts, mgot, ysem, yrem, zsem, zrem, osem, orem):
+        masses([n - 1])
+
+
+def give_kernel(
+    tab, own, xj, okeep, jkeep, bucket, wa, wvT, woT, whT, wdT, wmT, gcol, dmine0, dother0, sc0, dmine2, dother2, mm2, mo2,
+    upd, mass, ident, dmine1, dother1, sc1, yb, ymst, yml, zst, zms, zret, zmr, parts, got, mparts, mgot,
+    ysem, yrem, zsem, zrem, osem, orem,
+):
     me, sub, others, peers = places()
     rows = pl.ds(pl.multiple_of(sub * ROWS, ROWS), ROWS)
+    ident[...] = eye(256)
+    w = dict(wa=wa, wvT=wvT, woT=woT, whT=whT, wdT=wdT, wmT=wmT, gcol=gcol, ident=ident)
+    binv = bucket[...] * LOG2E
     mline = lax.broadcasted_iota(I32, (JOBS, KEYS), 0)
-    masks = jnp.zeros((JOBS, KEYS), F32)
-    for q in range(JOBS):
-        masks = jnp.where(mline == q, mo[q], masks)
-    ymst[...] = masks
+
+    def held(q, parts):
+        if q < EARLY:
+            return parts[0], q
+        if q < FIXED:
+            return parts[1], q - EARLY
+        return parts[2], q - FIXED
+
     greet(others, peers)
     ycopies = []
-    for q in range(JOBS):
+
+    def hand_back(q):
+        ref, at = held(q, (dother0, dother1, dother2))
         for d in range(1, SUBS):
             p = peers[d - 1]
-            part = dother.at[q, pl.ds(pl.multiple_of(p * ROWS, ROWS), ROWS), :]
+            part = ref.at[at, pl.ds(pl.multiple_of(p * ROWS, ROWS), ROWS), :]
             ycopies.append(send(part, yb.at[q, sub], ysem.at[q, d - 1], yrem.at[q, d - 1], {"sub": p}))
-    for d in range(1, SUBS):
-        ycopies.append(send(ymst, yml.at[sub], ysem.at[JOBS, d - 1], yrem.at[JOBS, d - 1], {"sub": peers[d - 1]}))
+            ycopies[-1].start()
+        yb[q, sub] = ref[at, rows, :]
+
+    for q in list(range(EARLY)) + list(range(FIXED, JOBS)):
+        hand_back(q)
+    for q in range(EARLY, FIXED):
+        dmine1[q - EARLY], dother1[q - EARLY], sc1[q - EARLY] = do_scores(q, tab, sub, own, xj[q], okeep, jkeep, w)
+        hand_back(q)
+    masses = [None] * FIXED
+    halves = (list(range(FIXED // 2)), list(range(FIXED // 2, FIXED)))
+    outs = do_masses(halves[0], [held(q, (sc0, sc1)) for q in halves[0]], tab, sub, okeep, jkeep, binv, ident[...])
+    for q, out in zip(halves[0], outs):
+        masses[q] = out
     for copy in ycopies:
-        copy.start()
-    for q in range(JOBS):
-        yb[q, sub] = dother[q, rows, :]
-    yml[sub] = masks
-    for copy in ycopies:
-        copy.wait()
-    ymasses = jnp.concatenate([yml[s] for s in range(SUBS)], axis=0)
+        copy.wait()
     zcopies = [None] * REACH
     for t in (4, 5, 2, 3, 0, 1):
-        line = lax.broadcasted_iota(I32, (8, KEYS), 0)
-        back = jnp.zeros((8, KEYS), F32)
         for u in range(MOST):
             place = tab[2, t * 8 + u]
             zst[t, u] = yb[place >> 2, place & 3]
-            back = jnp.where(line == u, row_of(ymasses, (place & 3) * JOBS + (place >> 2)), back)
-        zms[t] = back
-        to = {"img": others[t]}
-        zcopies[t] = [
-            send(zst.at[t], zret.at[t ^ 1], zsem.at[0, t], zrem.at[0, t ^ 1], to),
-            send(zms.at[t], zmr.at[t ^ 1], zsem.at[1, t], zrem.at[1, t ^ 1], to),
-        ]
-        for copy in zcopies[t]:
-            copy.start()
+        zcopies[t] = send(zst.at[t], zret.at[t ^ 1], zsem.at[0, t], zrem.at[0, t ^ 1], {"img": others[t]})
+        zcopies[t].start()
     n = (tab[3, 0] + (SUBS - 1) - sub) >> 2
     owners = [jnp.where(q < n, job_of(tab, q, sub)[0], -1) for q in range(JOBS)]
     for a in range(OWN):
         for s in range(SUBS):
             value = jnp.zeros((ROWS, D), F32)
             for q in range(JOBS):
-                value = value + jnp.where(owners[q] == a, dmine[q, s * ROWS : s * ROWS + ROWS, :].astype(F32), 0.0)
+                ref, at = held(q, (dmine0, dmine1, dmine2))
+                value = value + jnp.where(owners[q] == a, ref[at, s * ROWS : s * ROWS + ROWS, :].astype(F32), 0.0)
             parts[s, a] = value.astype(BF)
-        value = jnp.zeros((1, KEYS), F32)
-        for q in range(JOBS):
-            value = value + jnp.where(owners[q] == a, mm[q, 0:1, :], 0.0)
-        mparts[a : a + 1, :] = value
     ocopies = []
     for d in range(1, SUBS):
         to = {"sub": peers[d - 1]}
         ocopies.append(send(parts.at[peers[d - 1]], got.at[d - 1], osem.at[0, d - 1], orem.at[0, d - 1], to))
-        ocopies.append(send(mparts, mgot.at[d - 1], osem.at[1, d - 1], orem.at[1, d - 1], to))
+        ocopies[-1].start()
+    outs = do_masses(halves[1], [held(q, (sc0, sc1)) for q in halves[1]], tab, sub, okeep, jkeep, binv, ident[...])
+    for q, out in zip(halves[1], outs):
+        masses[q] = out
+    mine = [masses[q][0] if q < FIXED else mm2[q - FIXED, 0:1, :] for q in range(JOBS)]
+    away = [masses[q][1] if q < FIXED else mo2[q - FIXED, 0:1, :] for q in range(JOBS)]
+    table = jnp.zeros((JOBS, KEYS), F32)
+    for q in range(JOBS):
+        table = jnp.where(mline == q, away[q], table)
+    ymst[...] = table
+    yml[sub] = table
+    ymcopies = []
+    for d in range(1, SUBS):
+        ymcopies.append(send(ymst, yml.at[sub], ysem.at[JOBS, d - 1], yrem.at[JOBS, d - 1], {"sub": peers[d - 1]}))
+        ymcopies[-1].start()
+    table = jnp.zeros((OWN, KEYS), F32)
+    for a in range(OWN):
+        for q in range(JOBS):
+            table = table + jnp.where((mline == a) & (owners[q] == a), mine[q], 0.0)
+    mparts[...] = table
+    for d in range(1, SUBS):
+        copy = send(mparts, mgot.at[d - 1], osem.at[1, d - 1], orem.at[1, d - 1], {"sub": peers[d - 1]})
+        copy.start()
+        ocopies.append(copy)
+    for copy in ymcopies:
+        copy.wait()
+    ymasses = jnp.concatenate([yml[s] for s in range(SUBS)], axis=0)
+    zmcopies = []
+    for t in (4, 5, 2, 3, 0, 1):
+        back = jnp.zeros((8, KEYS), F32)
+        for u in range(MOST):
+            place = tab[2, t * 8 + u]
+            back = jnp.where(mline == u, row_of(ymasses, (place & 3) * JOBS + (place >> 2)), back)
+        zms[t] = back
+        zmcopies.append(send(zms.at[t], zmr.at[t ^ 1], zsem.at[1, t], zrem.at[1, t ^ 1], {"img": others[t]}))
+        zmcopies[-1].start()
     for copy in ocopies:
-        copy.start()
-    for copy in ocopies:
         copy.wait()
     for t in range(REACH):
-        for copy in zcopies[t]:
-            copy.wait()
-    masses = mparts[...] + mgot[0] + mgot[1] + mgot[2]
+        zcopies[t].wait()
     wants = [(t, u, sent_image(tab, t, u) - 1) for t in range(REACH) for u in range(MOST)]
     for a in range(OWN):
         value = parts[sub, a].astype(F32)
         for d in range(SUBS - 1):
             value = value + got[d, a].astype(F32)
+        for t, u, which in wants:
+            value = value + jnp.where(which == a, zret[t, u].astype(F32), 0.0)
+        upd[a] = value.astype(BF)
+    for copy in zmcopies:
+        copy.wait()
+    total = mparts[...] + mgot[0] + mgot[1] + mgot[2]
+    for a in range(OWN):
         extra = jnp.zeros((1, KEYS), F32)
         for t, u, which in wants:
-            value = value + jnp.where(which == a, zret[t, u].astype(F32), 0.0)
             extra = extra + jnp.where(which == a, zmr[t, u : u + 1, :], 0.0)
-        upd[a] = value.astype(BF)
-        masses = masses + jnp.where(mline == a, extra, 0.0)
+        total = total + jnp.where(mline == a, extra, 0.0)
     out = jnp.zeros((OWN, ROWS), F32)
     for s in range(SUBS):
-        out = jnp.where(sub == s, masses[:, s * ROWS : s * ROWS + ROWS], out)
+        out = jnp.where(sub == s, total[:, s * ROWS : s * ROWS + ROWS], out)
     mass[...] = out
 
 
@@ -535,39 +586,47 @@
         scratch_shapes=[V((8, 128), I32), V((REACH, 8, 128), I32), DMA((REACH,)), DMA((REACH,))],
         compiler_params=talk(0),
     )(pair_list, pair_count, w_value, w_output, w_hidden, norm_gain.reshape(1, -1), w_down, w_match)
-    allx, okeep, jkeep = pl.pallas_call(
+    own, xj, okeep, jkeep, *early = pl.pallas_call(
         fetch_kernel,
-        out_shape=(shape((OWN + JOBS, KEYS, D)), shape((OWN, KEYS), F32), shape((JOBS, KEYS), F32)),
-        in_specs=[SM, VM, SM, VM],
-        out_specs=(VM,) * 3,
+        out_shape=(
+            shape((OWN, KEYS, D)), shape((JOBS, KEYS, D)), shape((OWN, KEYS), F32), shape((JOBS, KEYS), F32),
+            shape((EARLY, KEYS, D)), shape((EARLY, KEYS, D)), shape((EARLY, KEYS, KEYS), F32),
+        ),
+        in_specs=[SM, VM, SM, VM] + [VM] * 7,
+        out_specs=(VM,) * 7,
         scratch_shapes=[
+            V((256, 256), BF),
             V((REACH, MOST, ROWS, D), BF), V((REACH, MOST, ROWS, D), BF), V((REACH, 8, KEYS), F32), V((REACH, 8, KEYS), F32),
             V((SUBS - 1, JOBS, ROWS, D), BF), V((SUBS, JOBS, KEYS), F32), V((SUBS - 1, JOBS, KEYS), F32), V((SUBS, OWN, KEYS), F32),
             DMA((2, REACH)), DMA((2, REACH)), DMA((JOBS + 1, SUBS - 1)), DMA((JOBS + 1, SUBS - 1)), DMA((2, SUBS - 1)), DMA((2, SUBS - 1)),
         ],
         compiler_params=talk(1),
-    )(tab, descriptors, counts, visible)
-    done = pl.pallas_call(
+    )(tab, descriptors, counts, visible, w_attend, *ready)
+    common = (tab, own, xj, okeep, jkeep, unassigned_bucket.reshape(1, 1), w_attend, *ready)
+    late = JOBS - FIXED
+    rest = pl.pallas_call(
         work_kernel,
-        out_shape=(shape((JOBS, KEYS, D)), shape((JOBS, KEYS, D)), shape((JOBS, 8, KEYS), F32), shape((JOBS, 8, KEYS), F32)),
-        in_specs=[SM] + [VM] * 11,
+        out_shape=(shape((late, KEYS, D)), shape((late, KEYS, D)), shape((late, 8, KEYS), F32), shape((late, 8, KEYS), F32)),
+        in_specs=[SM] + [VM] * 12,
         out_specs=(VM,) * 4,
-        scratch_shapes=[V((256, 256), BF), V((JOBS, KEYS, KEYS), F32)],
+        scratch_shapes=[V((256, 256), BF), V((late, KEYS, KEYS), F32)],
         compiler_params=pltpu.CompilerParams(vmem_limit_bytes=LIMIT),
-    )(tab, allx, okeep, jkeep, unassigned_bucket.reshape(1, 1), w_attend, *ready)
+    )(*common)
+    mid = FIXED - EARLY
     return pl.pallas_call(
         give_kernel,
         out_shape=(shape((OWN, ROWS, D)), shape((OWN, ROWS), F32)),
-        in_specs=[SM] + [VM] * 4,
+        in_specs=[SM] + [VM] * 19,
         out_specs=(VM, VM),
         scratch_shapes=[
+            V((256, 256), BF), V((mid, KEYS, D), BF), V((mid, KEYS, D), BF), V((mid, KEYS, KEYS), F32),
             V((JOBS, SUBS, ROWS, D), BF), V((JOBS, KEYS), F32), V((SUBS, JOBS, KEYS), F32),
             V((REACH, MOST, ROWS, D), BF), V((REACH, 8, KEYS), F32), V((REACH, MOST, ROWS, D), BF), V((REACH, 8, KEYS), F32),
             V((SUBS, OWN, ROWS, D), BF), V((SUBS - 1, OWN, ROWS, D), BF), V((OWN, KEYS), F32), V((SUBS - 1, OWN, KEYS), F32),
             DMA((JOBS + 1, SUBS - 1)), DMA((JOBS + 1, SUBS - 1)), DMA((2, REACH)), DMA((2, REACH)), DMA((2, SUBS - 1)), DMA((2, SUBS - 1)),
         ],
         compiler_params=talk(2),
-    )(tab, *done)
+    )(*common, *early, *rest)
 
 
 def solution(mesh):

time: 147 us -> 119 us (0.81)
  Pallas kernels: 140 us -> 113 us
    pallas_call x2, Pallas kernels: 69.6 us -> 49.4 us  [the longest x1 37.5 us: local(): pl.pallas_call(fetch_kernel, out_shape=(shape((OWN, KEYS, D)), shape((JOB...]
    pallas_call x1, Pallas kernels: 51.6 us -> 44.3 us  [local(): pl.pallas_call(give_kernel, out_shape=(shape((OWN, ROWS, D)), shape((OWN,...]
    unnamed x3 -> x7, local copies, waits for them, and re-layouts: 4.31 us -> 3.63 us
where the time goes in v3:
time: 119 us; the launch traced here: 118 us
  Pallas kernels  113 us (95%)
  local copies, waits for them, and re-layouts  3.63 us (3%)
  between operations  1.97 us (2%)
    pallas_call x1, Pallas kernels, local(): pl.pallas_call(give_kernel, out_shape=(shape((OWN, ROWS, D)), shape((OWN,...  44.3 us
    pallas_call x1, Pallas kernels, local(): pl.pallas_call(fetch_kernel, out_shape=(shape((OWN, KEYS, D)), shape((JOB...  37.5 us
    pallas_call x1, Pallas kernels, local(): pl.pallas_call(meet_kernel, out_shape=(shape((8, 128), I32), shape((256,...  18.9 us
    pallas_call x1, Pallas kernels, local(): pl.pallas_call(work_kernel, out_shape=(shape((late, KEYS, D)), shape((lat...  11.8 us
    unnamed x7, local copies, waits for them, and re-layouts  3.63 us

profile of v3, /device:TPU:1, one launch (start us, length us, event | category | flops | bytes accessed | tf_op | source)
XLA Modules:
  0.0 118.2 jit_solution(13410130125315097763)
XLA Ops:
  1.9 0.0 copy-start.1
  1.9 0.7 copy-done.1
  2.6 0.7 copy.15.pairs
  3.3 18.9 %shard_map.140 = (s32[8,128]{1,0:T(8,128)}, bf16[256,256]{1,0:T(8,128)(2,1)}, bf16[256,256]{1,0:T(8,128)(2,1)}, bf16[512,512]{1,0:T(8,128)(2,1)}, bf16[256,512]{...) custom-call(s32[32,2]{1,0:T(8,128)} %copy.15.pairs, s32[1]{0:T(128)S(6)} %copy.18.pair_count, ...), custom_call_target="tpu_custom_call" | custom-call | tf_op jit(solution)/shard_map/pallas_call | solution.py:581
  22.2 37.5 %shard_map.141 = (bf16[8,256,256]{2,1,0:T(8,128)(2,1)}, bf16[8,256,256]{2,1,0:T(8,128)(2,1)}, f32[8,256]{1,0:T(8,128)}, f32[8,256]{1,0:T(8,128)}, bf16[2,256,256...) custom-call(s32[8,128]{1,0:T(8,128)} %get-tuple-element.20.tab, bf16[8,64,256]{2,1,0:T(8,128)(2,1)} %desc.1, ...), custom_call_target="tpu_custom_call" | custom-call | tf_op jit(solution)/shard_map/pallas_call | solution.py:589
  59.8 11.8 %shard_map.142 = (bf16[4,256,256]{2,1,0:T(8,128)(2,1)}, bf16[4,256,256]{2,1,0:T(8,128)(2,1)}, f32[4,8,256]{2,1,0:T(8,128)}, f32[4,8,256]{2,1,0:T(8,128)}) custom-call(s32[8,128]{1,0:T(8,128)} %get-tuple-element.20.tab, bf16[8,256,256]{2,1,0:T(8,128)(2,1)} %get-tuple-element.27.own, bf16[8,256,256]{2,1,0:T(8,128)(2,1)} %get-tuple-element.28.xj, ...), custom_call_target="tpu_custom_call" | custom-call | tf_op jit(solution)/shard_map/pallas_call | solution.py:607
  71.6 44.3 %shard_map.143 = (bf16[8,64,256]{2,1,0:T(8,128)(2,1)}, f32[8,64]{1,0:T(8,128)}) custom-call(s32[8,128]{1,0:T(8,128)} %get-tuple-element.20.tab, bf16[8,256,256]{2,1,0:T(8,128)(2,1)} %get-tuple-element.27.own, bf16[8,256,256]{2,1,0:T(8,128)(2,1)} %get-tuple-element.28.xj, f32[8,256]{1,0:T(8,128)} %get-tuple-element.29.okeep, ...), custom_call_target="tpu_custom_call" | custom-call | tf_op jit(solution)/shard_map/pallas_call | solution.py:616
  116.0 0.0 copy-start
  116.0 1.7 %copy.20 = bf16[8,64,256]{2,1,0:T(8,128)(2,1)} copy(bf16[8,64,256]{2,1,0:T(8,128)(2,1)} %get-tuple-element.40) | data formatting | bytes 524288
  117.6 0.0 copy-done
  117.6 0.6 copy.21
Async XLA Ops:
  1.9 0.7 copy-start.1
  116.0 1.7 %copy-start = (f32[8,64]{1,0:T(8,128)S(1)}, f32[8,64]{1,0:T(8,128)}, u32[]{:S(2)}) copy-start(f32[8,64]{1,0:T(8,128)} %get-tuple-element.41) | copy-start | bytes 6148

commit v4 on v3

--- a/solution.py
+++ b/solution.py
@@ -46,11 +46,11 @@
     return nt(ident, jnp.broadcast_to(row, (128, row.shape[1])))
 
 
-def prepare(wv, wo, wh, gain, wd, wm, wvT, woT, whT, wdT, wmT, gcol):
+def prepare(wa, wv, wo, wh, gain, wd, waT, wvT, woT, whT, wdT, gcol):
     ident = eye(256)
+    waT[...] = nt(ident, wa[...]).astype(BF)
     wvT[...] = nt(ident, wv[...]).astype(BF)
     woT[...] = nt(ident, wo[...]).astype(BF)
-    wmT[...] = nt(ident, wm[...]).astype(BF)
     for a in range(0, 512, 256):
         for b in range(0, 512, 256):
             whT[a : a + 256, b : b + 256] = nt(ident, wh[b : b + 256, a : a + 256]).astype(BF)
@@ -63,52 +63,77 @@
         gcol[q : q + 128, :] = jnp.broadcast_to(column, (128, 128))
 
 
-def attention(a_other, a_self, vT_other, bias, ident):
+def attention(sides, ahead=4, behind=2):
+    ones = jnp.ones((16, KEYS), BF)
+    steps = [(h, s) for h in range(HEADS) for s in range(len(sides))]
+
+    def similarity(h, s):
+        a_other, aT_self, _, bias = sides[s]
+        sl = slice(h * 64, h * 64 + 64)
+        value = nn(a_other[:, sl], aT_self[sl]) * (LOG2E / 8.0) + bias
+        return value, jnp.max(value, axis=0, keepdims=True)
+
+    def finish(r):
+        return (r[:64] * (1.0 / r[64:65])).astype(BF)
+
+    waiting = [similarity(*step) for step in steps[:ahead]]
+    late = []
+    outs = {}
+    for i, (h, s) in enumerate(steps):
+        if i + ahead < len(steps):
+            waiting.append(similarity(*steps[i + ahead]))
+        value, top = waiting.pop(0)
+        e = jnp.exp2(value - top).astype(BF)
+        late.append(((h, s), nn(jnp.concatenate([sides[s][2][h * 64 : h * 64 + 64], ones], axis=0), e)))
+        if len(late) > behind:
+            step, r = late.pop(0)
+            outs[step] = finish(r)
+    for step, r in late:
+        outs[step] = finish(r)
+    return [jnp.concatenate([outs[h, s] for h in range(HEADS)], axis=0) for s in range(len(sides))]
+
+
+def refine(xs, msgs, w):
+    half = math.sqrt(0.5)
+    gain = jnp.concatenate([w["gcol"][...]] * 2, axis=1) * half
+
+    def hidden(i):
+        sentT = nn(w["woT"][...], msgs[i]).astype(BF)
+        return nt(w["whT"][:, :256], xs[i]) + nn(w["whT"][:, 256:], sentT)
+
     outs = []
-    ones = jnp.ones((16, KEYS), BF)
-    aT = nt(ident, a_self).astype(BF)
-    for h in range(HEADS):
-        sl = slice(h * 64, h * 64 + 64)
-        s = nn(a_other[:, sl], aT[sl]) * (LOG2E / 8.0) + bias
-        top = jnp.max(s, axis=0, keepdims=True)
-        e = jnp.exp2(s - top).astype(BF)
-        r = nn(jnp.concatenate([vT_other[sl, :], ones], axis=0), e)
-        outs.append((r[:64] * (1.0 / r[64:65])).astype(BF))
-    return jnp.concatenate(outs, axis=0)
-
-
-def refine(x, msgT, w):
-    outs = []
-    gain = w["gcol"][...]
-    sentT = nn(w["woT"][...], msgT).astype(BF)
-    for c in range(0, KEYS, 128):
-        hid = nt(w["whT"][:, :256], x[c : c + 128]) + nn(w["whT"][:, 256:], sentT[:, c : c + 128])
+    later = hidden(0)
+    for i in range(len(xs)):
+        hid = later
+        if i + 1 < len(xs):
+            later = hidden(i + 1)
         mean = jnp.sum(hid, axis=0, keepdims=True) * (1.0 / 512)
         cen = hid - mean
         var = jnp.sum(cen * cen, axis=0, keepdims=True) * (1.0 / 512)
-        normed = cen * lax.rsqrt(var + 1e-5) * gain
-        outs.append((0.5 * normed * (1.0 + lax.erf(normed * math.sqrt(0.5)))).astype(BF))
-    return nn(w["wdT"][...], jnp.concatenate(outs, axis=1)).astype(BF)
-
-
-def pair_scores(xi, ki, xj, kj, w):
+        z = cen * lax.rsqrt(var + 1e-5) * gain
+        outs.append(nn(w["wdT"][...], ((half * z) * (1.0 + lax.erf(z))).astype(BF)).astype(BF))
+    return outs
+
+
+def pair_scores(pairs, w):
     ident = w["ident"][...]
-    bi = (to_col(ki, ident) - 1.0) * 1e30
-    bj = (to_col(kj, ident) - 1.0) * 1e30
-    bi = jnp.concatenate([bi, bi], axis=1)
-    bj = jnp.concatenate([bj, bj], axis=1)
-    ai = nn(xi, w["wa"][...]).astype(BF)
-    aj = nn(xj, w["wa"][...]).astype(BF)
-    viT = nt(w["wvT"][...], xi).astype(BF)
-    vjT = nt(w["wvT"][...], xj).astype(BF)
-    diT = refine(xi, attention(aj, ai, vjT, bj, ident), w)
-    djT = refine(xj, attention(ai, aj, viT, bi, ident), w)
-    riT = (nt(ident, xi) + diT.astype(F32)).astype(BF)
-    rjT = (nt(ident, xj) + djT.astype(F32)).astype(BF)
-    mi = nn(w["wmT"][...], riT).astype(BF)
-    mj = nn(w["wmT"][...], rjT).astype(BF)
-    scores = nn(nt(ident, mi).astype(BF), mj) * (LOG2E / 16.0)
-    return nt(ident, diT).astype(BF), nt(ident, djT).astype(BF), scores
+    xs, biases = [], []
+    for xi, ki, xj, kj in pairs:
+        xs += [xi, xj]
+        for keep in (ki, kj):
+            bias = (to_col(keep, ident) - 1.0) * 1e30
+            biases.append(jnp.concatenate([bias, bias], axis=1))
+    attend = [nn(x, w["wa"][...]).astype(BF) for x in xs]
+    attendT = [nt(w["waT"][...], x).astype(BF) for x in xs]
+    valueT = [nt(w["wvT"][...], x).astype(BF) for x in xs]
+    msgs = attention([(attend[i ^ 1], attendT[i], valueT[i ^ 1], biases[i ^ 1]) for i in range(len(xs))])
+    deltas = [nt(ident, d).astype(BF) for d in refine(xs, msgs, w)]
+    match = [
+        nn((x.astype(F32) + d.astype(F32)).astype(BF), w["wm"][...]).astype(BF) for x, d in zip(xs, deltas)
+    ]
+    return [
+        (deltas[i], deltas[i + 1], nt(match[i], match[i + 1]) * (LOG2E / 16.0)) for i in range(0, len(xs), 2)
+    ]
 
 
 def marginals(ki, kj, ident):
@@ -116,7 +141,7 @@
     n = jnp.sum(kj, axis=1, keepdims=True)
     total = m + n
     off = -jnp.log2(jnp.maximum(total, 1.0))
-    kic = to_col(ki.astype(BF), ident)[:, :1]
+    kic = to_col(ki.astype(BF), ident)
     lr = off - FORGET * (1.0 - kic)
     lc = off - FORGET * (1.0 - kj)
     lrb = jnp.log2(jnp.maximum(n, 1.0)) + off
@@ -129,31 +154,38 @@
     s = jnp.sum(jnp.exp2(c - top), axis=1, keepdims=True) + jnp.exp2(bucket - top)
     f = lr - top - jnp.log2(s)
     fb = lrb - bucket - math.log2(257.0)
-    t = jnp.sum(jnp.exp2(c + f), axis=0, keepdims=True) + jnp.exp2(bucket + fb)
-    tb = jnp.sum(jnp.exp2(bucket + f), axis=0, keepdims=True) + jnp.exp2(bucket + fb)
+    halves = [jnp.sum(jnp.exp2(c[:, at : at + 128] + f), axis=0, keepdims=True) for at in (0, 128)]
+    t = jnp.concatenate(halves, axis=1) + jnp.exp2(bucket + fb)
+    tb = jnp.sum(jnp.exp2(bucket + f), axis=0, keepdims=True)[:, :1] + jnp.exp2(bucket + fb)
     return f, fb, lc - jnp.log2(t), lcb - jnp.log2(tb)
 
 
-def sink_next(c, bucket, lr, lc, lrb, lcb, r, rb, state):
+def sink_next(c, at, bucket, lr, lc, lrb, lcb, state):
     f, fb, g, gb = state
     eb = jnp.exp2(bucket + fb + g)
     ebb = jnp.exp2(bucket + fb + gb)
-    ub = rb / (jnp.sum(eb, axis=1, keepdims=True) + ebb)
-    p = jnp.exp2(c + g + f)
+    dub = lrb - jnp.log2(jnp.sum(eb, axis=1, keepdims=True) + ebb)
+    ub = jnp.exp2(dub)
+    p0 = jnp.exp2(c[at, :, :128] + g[:, :128] + f)
+    p1 = jnp.exp2(c[at, :, 128:] + g[:, 128:] + f)
     b = jnp.exp2((bucket + gb) + f)
-    u = r / (jnp.sum(p, axis=1, keepdims=True) + b)
-    t = eb * ub + jnp.sum(p * u, axis=0, keepdims=True)
-    tb = ebb * ub + jnp.sum(b * u, axis=0, keepdims=True)
-    return f + jnp.log2(u), fb + jnp.log2(ub), g + lc - jnp.log2(t), gb + lcb - jnp.log2(tb)
+    du = lr - jnp.log2(jnp.sum(p0 + p1, axis=1, keepdims=True) + b)
+    u = jnp.exp2(du)
+    t = [jnp.sum(p * u, axis=0, keepdims=True) for p in (p0, p1)]
+    t = eb * ub + jnp.concatenate(t, axis=1)
+    tb = ebb * ub + jnp.sum(b * u, axis=0, keepdims=True)[:, :1]
+    return f + du, fb + dub, g + lc - jnp.log2(t), gb + lcb - jnp.log2(tb)
 
 
 def sink_out(c, total, kic, kj, state):
     f, fb, g, gb = state
-    plan = jnp.exp2(c + f + g)
-    mi = (jnp.sum(plan, axis=1, keepdims=True) * total * kic).astype(BF)
-    mj = (jnp.sum(plan, axis=0, keepdims=True) * total * kj).astype(BF)
+    p0 = jnp.exp2(c[:, :128] + g[:, :128] + f)
+    p1 = jnp.exp2(c[:, 128:] + g[:, 128:] + f)
+    mi = (jnp.sum(p0 + p1, axis=1, keepdims=True) * total * kic).astype(BF)
+    halves = [jnp.sum(p, axis=0, keepdims=True) for p in (p0, p1)]
+    mj = (jnp.concatenate(halves, axis=1) * total * kj).astype(BF)
     first = (lax.broadcasted_iota(I32, (16, 128), 1) == 0).astype(BF)
-    return nt(first, jnp.broadcast_to(mi, (KEYS, 128)))[:1], mj.astype(F32)
+    return nt(first, mi)[:1], mj.astype(F32)
 
 
 def row_of(block, index):
@@ -166,15 +198,21 @@
     return (code >> 8) & 7, (code >> 12) & 1
 
 
-def do_scores(q, tab, sub, own, xo, okeep, jkeep, w):
-    mine, swap = job_of(tab, q, sub)
-    xm = own[mine]
-    km = row_of(okeep[...], mine)
-    ko = row_of(jkeep[...], q)
-    ki = jnp.where(swap == 1, ko, km).astype(BF)
-    kj = jnp.where(swap == 1, km, ko).astype(BF)
-    di, dj, scores = pair_scores(jnp.where(swap == 1, xo, xm), ki, jnp.where(swap == 1, xm, xo), kj, w)
-    return jnp.where(swap == 1, dj, di), jnp.where(swap == 1, di, dj), scores
+def do_scores(jobs, tab, sub, own, xj, okeep, jkeep, w):
+    pairs, swaps = [], []
+    for q in jobs:
+        mine, swap = job_of(tab, q, sub)
+        xm, xo = own[mine], xj[q]
+        km = row_of(okeep[...], mine)
+        ko = row_of(jkeep[...], q)
+        ki = jnp.where(swap == 1, ko, km).astype(BF)
+        kj = jnp.where(swap == 1, km, ko).astype(BF)
+        pairs.append((jnp.where(swap == 1, xo, xm), ki, jnp.where(swap == 1, xm, xo), kj))
+        swaps.append(swap)
+    return [
+        (jnp.where(swap == 1, dj, di), jnp.where(swap == 1, di, dj), scores)
+        for swap, (di, dj, scores) in zip(swaps, pair_scores(pairs, w))
+    ]
 
 
 def do_masses(jobs, sc, tab, sub, okeep, jkeep, bucket, ident):
@@ -190,10 +228,9 @@
         kjs.append(kj)
         margs.append(marg)
         states.append(sink_first(ref[at], bucket, *marg[2:]))
-    sums = [(jnp.exp2(m[2]), jnp.exp2(m[4])) for m in margs]
 
     def sweep(_, states):
-        return [sink_next(ref[at], bucket, *m[2:], *r, s) for (ref, at), m, r, s in zip(sc, margs, sums, states)]
+        return [sink_next(ref, at, bucket, *m[2:], s) for (ref, at), m, s in zip(sc, margs, states)]
 
     states = lax.fori_loop(0, ITERS - 1, sweep, states)
     outs = []
@@ -311,7 +348,7 @@
     return out
 
 
-def meet_kernel(pairs, pair_count, wv, wo, wh, gain, wd, wm, tab, wvT, woT, whT, wdT, wmT, gcol, told, near, ssem, rsem):
+def meet_kernel(pairs, pair_count, wa, wv, wo, wh, gain, wd, tab, waT, wvT, woT, whT, wdT, gcol, told, near, ssem, rsem):
     me, sub, others, peers = places()
     own, out = own_rows(pairs[...], pair_count[0], me, lax.axis_size("img"))
     told[...] = jnp.broadcast_to(out, (8, 128))
@@ -319,7 +356,7 @@
     copies = [send(told, near.at[t ^ 1], ssem.at[t], rsem.at[t ^ 1], {"img": others[t]}) for t in range(REACH)]
     for copy in copies:
         copy.start()
-    prepare(wv, wo, wh, gain, wd, wm, wvT, woT, whT, wdT, wmT, gcol)
+    prepare(wa, wv, wo, wh, gain, wd, waT, wvT, woT, whT, wdT, gcol)
     for copy in copies:
         copy.wait()
     row = lax.broadcasted_iota(I32, (8, 128), 0)
@@ -333,11 +370,11 @@
     return tab[1, t * 8 + u]
 
 
-def fetch_kernel(tab, desc, counts, visible, wa, wvT, woT, whT, wdT, wmT, gcol, own, xj, okeep, jkeep, dmine, dother, sc, ident, zst, zland, zms, zml, yst, yms, yml, omask, zsem, zrem, ysem, yrem, osem, orem):
+def fetch_kernel(tab, desc, counts, visible, wa, wm, waT, wvT, woT, whT, wdT, gcol, own, xj, okeep, jkeep, dmine, dother, sc, ident, zst, zland, zms, zml, yst, yms, yml, omask, zsem, zrem, ysem, yrem, osem, orem):
     me, sub, others, peers = places()
     rows = pl.ds(pl.multiple_of(sub * ROWS, ROWS), ROWS)
     ident[...] = eye(256)
-    w = dict(wa=wa, wvT=wvT, woT=woT, whT=whT, wdT=wdT, wmT=wmT, gcol=gcol, ident=ident)
+    w = dict(wa=wa, wm=wm, waT=waT, wvT=wvT, woT=woT, whT=whT, wdT=wdT, gcol=gcol, ident=ident)
     for a in range(OWN):
         own[a, rows, :] = desc[a]
     image = lax.broadcasted_iota(I32, (OWN, ROWS), 0)
@@ -390,38 +427,44 @@
     for d in range(1, SUBS):
         mcopies.append(send(yms.at[d], yml.at[d - 1], ysem.at[JOBS, d - 1], yrem.at[JOBS, d - 1], {"sub": peers[d - 1]}))
         mcopies[-1].start()
-    for q in range(JOBS):
+    def hand_out(q):
         for d in range(1, SUBS):
             yst[d - 1, q] = zland[slots[q][d] >> 3, slots[q][d] & 7]
             copy = send(yst.at[d - 1, q], xj.at[q, rows, :], ysem.at[q, d - 1], yrem.at[q, d - 1], {"sub": peers[d - 1]})
             copy.start()
             ycopies.append(copy)
         xj[q, rows, :] = zland[slots[q][0] >> 3, slots[q][0] & 7]
+
+    for q in range(EARLY):
+        hand_out(q)
     for copy in ocopies:
         copy.wait()
     okeep[...] = omask[0] + omask[1] + omask[2] + omask[3]
     for copy in mcopies:
         copy.wait()
     jkeep[...] = yms[0] + yml[0] + yml[1] + yml[2]
-    for q in range(EARLY):
-        for copy in ycopies[3 * q : 3 * q + 3]:
-            copy.wait()
-        dmine[q], dother[q], sc[q] = do_scores(q, tab, sub, own, xj[q], okeep, jkeep, w)
+    for copy in ycopies:
+        copy.wait()
+    for q in range(EARLY, JOBS):
+        hand_out(q)
+    outs = do_scores(list(range(EARLY)), tab, sub, own, xj, okeep, jkeep, w)
+    for q, out in enumerate(outs):
+        dmine[q], dother[q], sc[q] = out
     for copy in ycopies[3 * EARLY :]:
         copy.wait()
 
 
-def work_kernel(tab, own, xj, okeep, jkeep, bucket, wa, wvT, woT, whT, wdT, wmT, gcol, dmine, dother, mm, mo, ident, sc):
+def work_kernel(tab, own, xj, okeep, jkeep, bucket, wa, wm, waT, wvT, woT, whT, wdT, gcol, dmine, dother, mm, mo, ident, sc):
     sub = lax.axis_index("sub")
     ident[...] = eye(256)
-    w = dict(wa=wa, wvT=wvT, woT=woT, whT=whT, wdT=wdT, wmT=wmT, gcol=gcol, ident=ident)
+    w = dict(wa=wa, wm=wm, waT=waT, wvT=wvT, woT=woT, whT=whT, wdT=wdT, gcol=gcol, ident=ident)
     n = ((tab[3, 0] + (SUBS - 1) - sub) >> 2) - FIXED
     binv = bucket[...] * LOG2E
 
-    @pl.loop(0, n)
-    def _(p):
-        q = FIXED + p
-        dmine[p], dother[p], sc[p] = do_scores(q, tab, sub, own, xj[q], okeep, jkeep, w)
+    def scores(ps):
+        outs = do_scores([FIXED + p for p in ps], tab, sub, own, xj, okeep, jkeep, w)
+        for p, out in zip(ps, outs):
+            dmine[p], dother[p], sc[p] = out
 
     def masses(ps):
         outs = do_masses([FIXED + p for p in ps], [(sc, p) for p in ps], tab, sub, okeep, jkeep, binv, ident[...])
@@ -431,22 +474,24 @@
 
     @pl.loop(0, n >> 1)
     def _(p):
+        scores([2 * p, 2 * p + 1])
         masses([2 * p, 2 * p + 1])
 
     @pl.when((n & 1) == 1)
     def _():
+        scores([n - 1])
         masses([n - 1])
 
 
 def give_kernel(
-    tab, own, xj, okeep, jkeep, bucket, wa, wvT, woT, whT, wdT, wmT, gcol, dmine0, dother0, sc0, dmine2, dother2, mm2, mo2,
+    tab, own, xj, okeep, jkeep, bucket, wa, wm, waT, wvT, woT, whT, wdT, gcol, dmine0, dother0, sc0, dmine2, dother2, mm2, mo2,
     upd, mass, ident, dmine1, dother1, sc1, yb, ymst, yml, zst, zms, zret, zmr, parts, got, mparts, mgot,
     ysem, yrem, zsem, zrem, osem, orem,
 ):
     me, sub, others, peers = places()
     rows = pl.ds(pl.multiple_of(sub * ROWS, ROWS), ROWS)
     ident[...] = eye(256)
-    w = dict(wa=wa, wvT=wvT, woT=woT, whT=whT, wdT=wdT, wmT=wmT, gcol=gcol, ident=ident)
+    w = dict(wa=wa, wm=wm, waT=waT, wvT=wvT, woT=woT, whT=whT, wdT=wdT, gcol=gcol, ident=ident)
     binv = bucket[...] * LOG2E
     mline = lax.broadcasted_iota(I32, (JOBS, KEYS), 0)
 
@@ -471,23 +516,10 @@
 
     for q in list(range(EARLY)) + list(range(FIXED, JOBS)):
         hand_back(q)
-    for q in range(EARLY, FIXED):
-        dmine1[q - EARLY], dother1[q - EARLY], sc1[q - EARLY] = do_scores(q, tab, sub, own, xj[q], okeep, jkeep, w)
-        hand_back(q)
-    masses = [None] * FIXED
-    halves = (list(range(FIXED // 2)), list(range(FIXED // 2, FIXED)))
-    outs = do_masses(halves[0], [held(q, (sc0, sc1)) for q in halves[0]], tab, sub, okeep, jkeep, binv, ident[...])
-    for q, out in zip(halves[0], outs):
-        masses[q] = out
-    for copy in ycopies:
-        copy.wait()
-    zcopies = [None] * REACH
-    for t in (4, 5, 2, 3, 0, 1):
-        for u in range(MOST):
-            place = tab[2, t * 8 + u]
-            zst[t, u] = yb[place >> 2, place & 3]
-        zcopies[t] = send(zst.at[t], zret.at[t ^ 1], zsem.at[0, t], zrem.at[0, t ^ 1], {"img": others[t]})
-        zcopies[t].start()
+    outs = do_scores(list(range(EARLY, FIXED)), tab, sub, own, xj, okeep, jkeep, w)
+    for at, out in enumerate(outs):
+        dmine1[at], dother1[at], sc1[at] = out
+        hand_back(EARLY + at)
     n = (tab[3, 0] + (SUBS - 1) - sub) >> 2
     owners = [jnp.where(q < n, job_of(tab, q, sub)[0], -1) for q in range(JOBS)]
     for a in range(OWN):
@@ -497,14 +529,22 @@
                 ref, at = held(q, (dmine0, dmine1, dmine2))
                 value = value + jnp.where(owners[q] == a, ref[at, s * ROWS : s * ROWS + ROWS, :].astype(F32), 0.0)
             parts[s, a] = value.astype(BF)
+    for copy in ycopies:
+        copy.wait()
+    zcopies = [None] * REACH
+    for t in (4, 5, 2, 3, 0, 1):
+        for u in range(MOST):
+            place = tab[2, t * 8 + u]
+            zst[t, u] = yb[place >> 2, place & 3]
+        zcopies[t] = send(zst.at[t], zret.at[t ^ 1], zsem.at[0, t], zrem.at[0, t ^ 1], {"img": others[t]})
+        zcopies[t].start()
     ocopies = []
     for d in range(1, SUBS):
         to = {"sub": peers[d - 1]}
         ocopies.append(send(parts.at[peers[d - 1]], got.at[d - 1], osem.at[0, d - 1], orem.at[0, d - 1], to))
         ocopies[-1].start()
-    outs = do_masses(halves[1], [held(q, (sc0, sc1)) for q in halves[1]], tab, sub, okeep, jkeep, binv, ident[...])
-    for q, out in zip(halves[1], outs):
-        masses[q] = out
+    fixed = list(range(FIXED))
+    masses = do_masses(fixed, [held(q, (sc0, sc1)) for q in fixed], tab, sub, okeep, jkeep, binv, ident[...])
     mine = [masses[q][0] if q < FIXED else mm2[q - FIXED, 0:1, :] for q in range(JOBS)]
     away = [masses[q][1] if q < FIXED else mo2[q - FIXED, 0:1, :] for q in range(JOBS)]
     table = jnp.zeros((JOBS, KEYS), F32)
@@ -525,6 +565,18 @@
         copy = send(mparts, mgot.at[d - 1], osem.at[1, d - 1], orem.at[1, d - 1], {"sub": peers[d - 1]})
         copy.start()
         ocopies.append(copy)
+    for copy in ocopies[: SUBS - 1]:
+        copy.wait()
+    for t in range(REACH):
+        zcopies[t].wait()
+    wants = [(t, u, sent_image(tab, t, u) - 1) for t in range(REACH) for u in range(MOST)]
+    for a in range(OWN):
+        value = parts[sub, a].astype(F32)
+        for d in range(SUBS - 1):
+            value = value + got[d, a].astype(F32)
+        for t, u, which in wants:
+            value = value + jnp.where(which == a, zret[t, u].astype(F32), 0.0)
+        upd[a] = value.astype(BF)
     for copy in ymcopies:
         copy.wait()
     ymasses = jnp.concatenate([yml[s] for s in range(SUBS)], axis=0)
@@ -537,18 +589,8 @@
         zms[t] = back
         zmcopies.append(send(zms.at[t], zmr.at[t ^ 1], zsem.at[1, t], zrem.at[1, t ^ 1], {"img": others[t]}))
         zmcopies[-1].start()
-    for copy in ocopies:
-        copy.wait()
-    for t in range(REACH):
-        zcopies[t].wait()
-    wants = [(t, u, sent_image(tab, t, u) - 1) for t in range(REACH) for u in range(MOST)]
-    for a in range(OWN):
-        value = parts[sub, a].astype(F32)
-        for d in range(SUBS - 1):
-            value = value + got[d, a].astype(F32)
-        for t, u, which in wants:
-            value = value + jnp.where(which == a, zret[t, u].astype(F32), 0.0)
-        upd[a] = value.astype(BF)
+    for copy in ocopies[SUBS - 1 :]:
+        copy.wait()
     for copy in zmcopies:
         copy.wait()
     total = mparts[...] + mgot[0] + mgot[1] + mgot[2]
@@ -580,19 +622,19 @@
     V = pltpu.VMEM
     tab, *ready = pl.pallas_call(
         meet_kernel,
-        out_shape=(shape((8, 128), I32), shape((256, 256)), shape((256, 256)), shape((512, 512)), shape((256, 512)), shape((256, 256)), shape((512, 128), F32)),
+        out_shape=(shape((8, 128), I32), *[shape((256, 256))] * 3, shape((512, 512)), shape((256, 512)), shape((512, 128), F32)),
         in_specs=[VM, SM] + [VM] * 6,
         out_specs=(VM,) * 7,
         scratch_shapes=[V((8, 128), I32), V((REACH, 8, 128), I32), DMA((REACH,)), DMA((REACH,))],
         compiler_params=talk(0),
-    )(pair_list, pair_count, w_value, w_output, w_hidden, norm_gain.reshape(1, -1), w_down, w_match)
+    )(pair_list, pair_count, w_attend, w_value, w_output, w_hidden, norm_gain.reshape(1, -1), w_down)
     own, xj, okeep, jkeep, *early = pl.pallas_call(
         fetch_kernel,
         out_shape=(
             shape((OWN, KEYS, D)), shape((JOBS, KEYS, D)), shape((OWN, KEYS), F32), shape((JOBS, KEYS), F32),
             shape((EARLY, KEYS, D)), shape((EARLY, KEYS, D)), shape((EARLY, KEYS, KEYS), F32),
         ),
-        in_specs=[SM, VM, SM, VM] + [VM] * 7,
+        in_specs=[SM, VM, SM, VM] + [VM] * 8,
         out_specs=(VM,) * 7,
         scratch_shapes=[
             V((256, 256), BF),
@@ -601,13 +643,13 @@
             DMA((2, REACH)), DMA((2, REACH)), DMA((JOBS + 1, SUBS - 1)), DMA((JOBS + 1, SUBS - 1)), DMA((2, SUBS - 1)), DMA((2, SUBS - 1)),
         ],
         compiler_params=talk(1),
-    )(tab, descriptors, counts, visible, w_attend, *ready)
-    common = (tab, own, xj, okeep, jkeep, unassigned_bucket.reshape(1, 1), w_attend, *ready)
+    )(tab, descriptors, counts, visible, w_attend, w_match, *ready)
+    common = (tab, own, xj, okeep, jkeep, unassigned_bucket.reshape(1, 1), w_attend, w_match, *ready)
     late = JOBS - FIXED
     rest = pl.pallas_call(
         work_kernel,
         out_shape=(shape((late, KEYS, D)), shape((late, KEYS, D)), shape((late, 8, KEYS), F32), shape((late, 8, KEYS), F32)),
-        in_specs=[SM] + [VM] * 12,
+        in_specs=[SM] + [VM] * 13,
         out_specs=(VM,) * 4,
         scratch_shapes=[V((256, 256), BF), V((late, KEYS, KEYS), F32)],
         compiler_params=pltpu.CompilerParams(vmem_limit_bytes=LIMIT),
@@ -616,7 +658,7 @@
     return pl.pallas_call(
         give_kernel,
         out_shape=(shape((OWN, ROWS, D)), shape((OWN, ROWS), F32)),
-        in_specs=[SM] + [VM] * 19,
+        in_specs=[SM] + [VM] * 20,
         out_specs=(VM, VM),
         scratch_shapes=[
             V((256, 256), BF), V((mid, KEYS, D), BF), V((mid, KEYS, D), BF), V((mid, KEYS, KEYS), F32),

time: 119 us -> 118 us (level)
    pallas_call x1, Pallas kernels: 44.3 us -> 49 us  [local(): pl.pallas_call(give_kernel, out_shape=(shape((OWN, ROWS, D)), shape((OWN,...]
    pallas_call x1, Pallas kernels: 11.8 us -> 9.04 us  [local(): pl.pallas_call(work_kernel, out_shape=(shape((late, KEYS, D)), shape((lat...]
    pallas_call x1, Pallas kernels: 37.5 us -> 35.3 us  [local(): pl.pallas_call(fetch_kernel, out_shape=(shape((OWN, KEYS, D)), shape((JOB...]
where the time goes in v4:
time: 118 us
  Pallas kernels  112 us (95%)
  local copies, waits for them, and re-layouts  3.63 us (3%)
  between operations  1.97 us (2%)
    pallas_call x1, Pallas kernels, local(): pl.pallas_call(give_kernel, out_shape=(shape((OWN, ROWS, D)), shape((OWN,...  49 us
    pallas_call x1, Pallas kernels, local(): pl.pallas_call(fetch_kernel, out_shape=(shape((OWN, KEYS, D)), shape((JOB...  35.3 us
    pallas_call x1, Pallas kernels, local(): pl.pallas_call(meet_kernel, out_shape=(shape((8, 128), I32), *[shape((256...  19 us
    pallas_call x1, Pallas kernels, local(): pl.pallas_call(work_kernel, out_shape=(shape((late, KEYS, D)), shape((lat...  9.04 us
    unnamed x7, local copies, waits for them, and re-layouts  3.63 us

profile of v4, /device:TPU:1, one launch (start us, length us, event | category | flops | bytes accessed | tf_op | source)
XLA Modules:
  0.0 117.9 jit_solution(7806693074748423868)
XLA Ops:
  1.9 0.0 copy-start.1
  1.9 0.7 copy-done.1
  2.6 0.7 copy.15.pairs
  3.3 19.0 %shard_map.140 = (s32[8,128]{1,0:T(8,128)}, bf16[256,256]{1,0:T(8,128)(2,1)}, bf16[256,256]{1,0:T(8,128)(2,1)}, bf16[256,256]{1,0:T(8,128)(2,1)}, bf16[512,512]{...) custom-call(s32[32,2]{1,0:T(8,128)} %copy.15.pairs, s32[1]{0:T(128)S(6)} %copy.18.pair_count, ...), custom_call_target="tpu_custom_call" | custom-call | tf_op jit(solution)/shard_map/pallas_call | solution.py:623
  22.3 35.3 %shard_map.141 = (bf16[8,256,256]{2,1,0:T(8,128)(2,1)}, bf16[8,256,256]{2,1,0:T(8,128)(2,1)}, f32[8,256]{1,0:T(8,128)}, f32[8,256]{1,0:T(8,128)}, bf16[2,256,256...) custom-call(s32[8,128]{1,0:T(8,128)} %get-tuple-element.20.tab, bf16[8,64,256]{2,1,0:T(8,128)(2,1)} %desc.1, ...), custom_call_target="tpu_custom_call" | custom-call | tf_op jit(solution)/shard_map/pallas_call | solution.py:631
  57.6 9.0 %shard_map.142 = (bf16[4,256,256]{2,1,0:T(8,128)(2,1)}, bf16[4,256,256]{2,1,0:T(8,128)(2,1)}, f32[4,8,256]{2,1,0:T(8,128)}, f32[4,8,256]{2,1,0:T(8,128)}) custom-call(s32[8,128]{1,0:T(8,128)} %get-tuple-element.20.tab, bf16[8,256,256]{2,1,0:T(8,128)(2,1)} %get-tuple-element.27.own, bf16[8,256,256]{2,1,0:T(8,128)(2,1)} %get-tuple-element.28.xj, ...), custom_call_target="tpu_custom_call" | custom-call | tf_op jit(solution)/shard_map/pallas_call | solution.py:649
  66.7 49.0 %shard_map.143 = (bf16[8,64,256]{2,1,0:T(8,128)(2,1)}, f32[8,64]{1,0:T(8,128)}) custom-call(s32[8,128]{1,0:T(8,128)} %get-tuple-element.20.tab, bf16[8,256,256]{2,1,0:T(8,128)(2,1)} %get-tuple-element.27.own, bf16[8,256,256]{2,1,0:T(8,128)(2,1)} %get-tuple-element.28.xj, f32[8,256]{1,0:T(8,128)} %get-tuple-element.29.okeep, ...), custom_call_target="tpu_custom_call" | custom-call | tf_op jit(solution)/shard_map/pallas_call | solution.py:658
  115.7 0.0 copy-start
  115.7 1.7 %copy.20 = bf16[8,64,256]{2,1,0:T(8,128)(2,1)} copy(bf16[8,64,256]{2,1,0:T(8,128)(2,1)} %get-tuple-element.40) | data formatting | bytes 524288
  117.3 0.0 copy-done
  117.3 0.6 copy.21
Async XLA Ops:
  1.9 0.7 copy-start.1
  115.7 1.7 %copy-start = (f32[8,64]{1,0:T(8,128)S(1)}, f32[8,64]{1,0:T(8,128)}, u32[]{:S(2)}) copy-start(f32[8,64]{1,0:T(8,128)} %get-tuple-element.41) | copy-start | bytes 6148

commit v5 on v4

--- a/solution.py
+++ b/solution.py
@@ -24,7 +24,9 @@
 SUBS = 4
 JOBS = 8
 FIXED = 4
-EARLY = 2
+PARTS = 4
+PART = ROWS // PARTS
+HALF = ROWS // 2
 MESH = pl.DeviceIdType.MESH
 LIMIT = 56 * 2**20
 
@@ -348,14 +350,39 @@
     return out
 
 
-def meet_kernel(pairs, pair_count, wa, wv, wo, wh, gain, wd, tab, waT, wvT, woT, whT, wdT, gcol, told, near, ssem, rsem):
+def own_mask(counts, visible, sub):
+    image = lax.broadcasted_iota(I32, (OWN, ROWS), 0)
+    found = jnp.zeros((OWN, ROWS), I32)
+    for a in range(OWN):
+        found = jnp.where(image == a, counts[a], found)
+    spot = lax.broadcasted_iota(I32, (OWN, ROWS), 1) + sub * ROWS
+    kept = jnp.where((spot < found) & (visible[...] > 0), 1.0, 0.0)
+    return my_lanes(jnp.concatenate([kept] * SUBS, axis=1), sub)
+
+
+def my_lanes(wide, sub):
+    lane = lax.broadcasted_iota(I32, wide.shape, 1)
+    return jnp.where((lane >= sub * ROWS) & (lane < sub * ROWS + ROWS), wide, 0.0)
+
+
+def meet_kernel(
+    pairs, pair_count, desc, counts, visible, wa, wv, wo, wh, gain, wd,
+    tab, waT, wvT, woT, whT, wdT, gcol, upper, okeep, told, near, omask, ssem, rsem, osem, orem,
+):
     me, sub, others, peers = places()
+    omask[0] = own_mask(counts, visible, sub)
+    greet(others, peers)
+    ocopies = []
+    for d in range(1, SUBS):
+        to = {"sub": peers[d - 1]}
+        ocopies.append(send(omask.at[0], omask.at[d], osem.at[1, d - 1], orem.at[1, d - 1], to))
+        ocopies.append(send(desc.at[:, 0:HALF, :], upper.at[sub], osem.at[0, d - 1], orem.at[0, d - 1], to))
     own, out = own_rows(pairs[...], pair_count[0], me, lax.axis_size("img"))
     told[...] = jnp.broadcast_to(out, (8, 128))
-    greet(others, [])
     copies = [send(told, near.at[t ^ 1], ssem.at[t], rsem.at[t ^ 1], {"img": others[t]}) for t in range(REACH)]
-    for copy in copies:
+    for copy in copies + ocopies:
         copy.start()
+    upper[sub] = desc[:, 0:HALF, :]
     prepare(wa, wv, wo, wh, gain, wd, waT, wvT, woT, whT, wdT, gcol)
     for copy in copies:
         copy.wait()
@@ -364,187 +391,188 @@
     for t in range(REACH):
         table = jnp.where(row == t, near[t], table)
     tab[...] = plan_rows(own, table, pair_count[0])
-
-
-def sent_image(tab, t, u):
-    return tab[1, t * 8 + u]
-
-
-def fetch_kernel(tab, desc, counts, visible, wa, wm, waT, wvT, woT, whT, wdT, gcol, own, xj, okeep, jkeep, dmine, dother, sc, ident, zst, zland, zms, zml, yst, yms, yml, omask, zsem, zrem, ysem, yrem, osem, orem):
-    me, sub, others, peers = places()
-    rows = pl.ds(pl.multiple_of(sub * ROWS, ROWS), ROWS)
-    ident[...] = eye(256)
-    w = dict(wa=wa, wm=wm, waT=waT, wvT=wvT, woT=woT, whT=whT, wdT=wdT, gcol=gcol, ident=ident)
-    for a in range(OWN):
-        own[a, rows, :] = desc[a]
-    image = lax.broadcasted_iota(I32, (OWN, ROWS), 0)
-    found = jnp.zeros((OWN, ROWS), I32)
-    for a in range(OWN):
-        found = jnp.where(image == a, counts[a], found)
-    spot = lax.broadcasted_iota(I32, (OWN, ROWS), 1) + sub * ROWS
-    kept = jnp.where((spot < found) & (visible[...] > 0), 1.0, 0.0)
-    wide = jnp.concatenate([kept] * SUBS, axis=1)
-    lane = lax.broadcasted_iota(I32, (OWN, KEYS), 1)
-    wide = jnp.where((lane >= sub * ROWS) & (lane < sub * ROWS + ROWS), wide, 0.0)
-    omask[0] = wide
-    greet(others, peers)
-    zcopies = []
-    for t in (4, 5, 2, 3, 0, 1):
-        line = lax.broadcasted_iota(I32, (8, KEYS), 0)
-        masks = jnp.zeros((8, KEYS), F32)
-        for u in range(MOST):
-            which = jnp.maximum(sent_image(tab, t, u) - 1, 0)
-            zst[t, u] = desc[which]
-            masks = jnp.where(line == u, row_of(wide, which), masks)
-        zms[t] = masks
-        to = {"img": others[t]}
-        zcopies.append(send(zst.at[t], zland.at[t ^ 1], zsem.at[0, t], zrem.at[0, t ^ 1], to))
-        zcopies.append(send(zms.at[t], zml.at[t ^ 1], zsem.at[1, t], zrem.at[1, t ^ 1], to))
-        zcopies[-2].start()
-        zcopies[-1].start()
-    ocopies = []
-    for d in range(1, SUBS):
-        to = {"sub": peers[d - 1]}
-        mine = own.at[:, rows, :]
-        ocopies.append(send(mine, mine, osem.at[0, d - 1], orem.at[0, d - 1], to))
-        ocopies.append(send(omask.at[0], omask.at[d], osem.at[1, d - 1], orem.at[1, d - 1], to))
-    for copy in ocopies:
-        copy.start()
-    for copy in zcopies:
-        copy.wait()
-    ycopies = []
-    line = lax.broadcasted_iota(I32, (JOBS, KEYS), 0)
-    zmasks = jnp.concatenate([zml[t] for t in range(REACH)], axis=0)
-    slots = [[None] * SUBS for _ in range(JOBS)]
-    for d in range(SUBS):
-        worker = sub if d == 0 else peers[d - 1]
-        masks = jnp.zeros((JOBS, KEYS), F32)
-        for q in range(JOBS):
-            slots[q][d] = jnp.maximum((tab[0, q * SUBS + worker] & 255) - 1, 0)
-            masks = jnp.where(line == q, row_of(zmasks, slots[q][d]), masks)
-        yms[d] = masks
-    mcopies = []
-    for d in range(1, SUBS):
-        mcopies.append(send(yms.at[d], yml.at[d - 1], ysem.at[JOBS, d - 1], yrem.at[JOBS, d - 1], {"sub": peers[d - 1]}))
-        mcopies[-1].start()
-    def hand_out(q):
-        for d in range(1, SUBS):
-            yst[d - 1, q] = zland[slots[q][d] >> 3, slots[q][d] & 7]
-            copy = send(yst.at[d - 1, q], xj.at[q, rows, :], ysem.at[q, d - 1], yrem.at[q, d - 1], {"sub": peers[d - 1]})
-            copy.start()
-            ycopies.append(copy)
-        xj[q, rows, :] = zland[slots[q][0] >> 3, slots[q][0] & 7]
-
-    for q in range(EARLY):
-        hand_out(q)
     for copy in ocopies:
         copy.wait()
     okeep[...] = omask[0] + omask[1] + omask[2] + omask[3]
-    for copy in mcopies:
+
+
+def sent_image(tab, t, u):
+    return tab[1, t * 8 + u]
+
+
+def fetch_kernel(
+    tab, desc, upper, okeep, own, xj, jkeep, zst, zl0, zl1, zl2, zl3, zms, zml, yst, yl, yms, yml, lower,
+    zsem, zrem, ysem, yrem, osem, orem,
+):
+    me, sub, others, peers = places()
+    zland = (zl0, zl1, zl2, zl3)
+    wide = my_lanes(okeep[...], sub)
+    greet(others, peers)
+    order = (4, 5, 2, 3, 0, 1)
+    line = lax.broadcasted_iota(I32, (8, KEYS), 0)
+    zmcopies = []
+    for t in order:
+        masks = jnp.zeros((8, KEYS), F32)
+        for u in range(MOST):
+            masks = jnp.where(line == u, row_of(wide, jnp.maximum(sent_image(tab, t, u) - 1, 0)), masks)
+        zms[t] = masks
+        zmcopies.append(
+            send(zms.at[t], zml.at[t ^ 1], zsem.at[PARTS, t], zrem.at[PARTS, t ^ 1], {"img": others[t]})
+        )
+        zmcopies[-1].start()
+    zcopies = []
+    for c in range(PARTS):
+        zcopies.append([])
+        for t in order:
+            for u in range(MOST):
+                which = jnp.maximum(sent_image(tab, t, u) - 1, 0)
+                zst[c, t, u] = desc[which, c * PART : c * PART + PART, :]
+            copy = send(zst.at[c, t], zland[c].at[t ^ 1], zsem.at[c, t], zrem.at[c, t ^ 1], {"img": others[t]})
+            copy.start()
+            zcopies[c].append(copy)
+    ocopies = []
+    for d in range(1, SUBS):
+        copy = send(desc.at[:, HALF:ROWS, :], lower.at[sub], osem.at[d - 1], orem.at[d - 1], {"sub": peers[d - 1]})
+        copy.start()
+        ocopies.append(copy)
+    lower[sub] = desc[:, HALF:ROWS, :]
+    for copy in zmcopies:
         copy.wait()
-    jkeep[...] = yms[0] + yml[0] + yml[1] + yml[2]
+    zmasks = jnp.concatenate([zml[t] for t in range(REACH)], axis=0)
+    slots = []
+    for d in range(SUBS):
+        worker = sub if d == 0 else peers[d - 1]
+        slots.append([jnp.maximum((tab[0, q * SUBS + worker] & 255) - 1, 0) for q in range(JOBS)])
+        masks = jnp.zeros((JOBS, KEYS), F32)
+        for q in range(JOBS):
+            masks = jnp.where(line == q, row_of(zmasks, slots[d][q]), masks)
+        yms[d] = masks
+    ycopies = []
+    for d in range(1, SUBS):
+        to = {"sub": peers[d - 1]}
+        ycopies.append(send(yms.at[d], yml.at[d - 1], ysem.at[PARTS, d - 1], yrem.at[PARTS, d - 1], to))
+        ycopies[-1].start()
+    for c in range(PARTS):
+        for copy in zcopies[c]:
+            copy.wait()
+        for d in range(1, SUBS):
+            for q in range(JOBS):
+                yst[c, d - 1, q] = zland[c][slots[d][q] >> 3, slots[d][q] & 7]
+            copy = send(yst.at[c, d - 1], yl.at[c, sub], ysem.at[c, d - 1], yrem.at[c, d - 1], {"sub": peers[d - 1]})
+            copy.start()
+            ycopies.append(copy)
+        for q in range(JOBS):
+            yl[c, sub, q] = zland[c][slots[0][q] >> 3, slots[0][q] & 7]
+    for copy in ocopies:
+        copy.wait()
+    for s in range(SUBS):
+        own[:, s * ROWS : s * ROWS + HALF, :] = upper[s]
+        own[:, s * ROWS + HALF : s * ROWS + ROWS, :] = lower[s]
     for copy in ycopies:
         copy.wait()
-    for q in range(EARLY, JOBS):
-        hand_out(q)
-    outs = do_scores(list(range(EARLY)), tab, sub, own, xj, okeep, jkeep, w)
-    for q, out in enumerate(outs):
-        dmine[q], dother[q], sc[q] = out
-    for copy in ycopies[3 * EARLY :]:
-        copy.wait()
-
-
-def work_kernel(tab, own, xj, okeep, jkeep, bucket, wa, wm, waT, wvT, woT, whT, wdT, gcol, dmine, dother, mm, mo, ident, sc):
+    for s in range(SUBS):
+        for c in range(PARTS):
+            at = s * ROWS + c * PART
+            xj[:, at : at + PART, :] = yl[c, s]
+    jkeep[...] = yms[0] + yml[0] + yml[1] + yml[2]
+
+
+def work_kernel(
+    tab, own, xj, okeep, jkeep, bucket, wa, wm, waT, wvT, woT, whT, wdT, gcol, dmine, dother, sc, mm, mo, ident, sclate
+):
     sub = lax.axis_index("sub")
     ident[...] = eye(256)
     w = dict(wa=wa, wm=wm, waT=waT, wvT=wvT, woT=woT, whT=whT, wdT=wdT, gcol=gcol, ident=ident)
     n = ((tab[3, 0] + (SUBS - 1) - sub) >> 2) - FIXED
     binv = bucket[...] * LOG2E
 
-    def scores(ps):
-        outs = do_scores([FIXED + p for p in ps], tab, sub, own, xj, okeep, jkeep, w)
-        for p, out in zip(ps, outs):
-            dmine[p], dother[p], sc[p] = out
-
-    def masses(ps):
-        outs = do_masses([FIXED + p for p in ps], [(sc, p) for p in ps], tab, sub, okeep, jkeep, binv, ident[...])
+    def scores(qs, ref, first):
+        outs = do_scores(qs, tab, sub, own, xj, okeep, jkeep, w)
+        for q, out in zip(qs, outs):
+            dmine[q], dother[q], ref[q - first] = out
+
+    def late(ps):
+        scores([FIXED + p for p in ps], sclate, FIXED)
+        outs = do_masses([FIXED + p for p in ps], [(sclate, p) for p in ps], tab, sub, okeep, jkeep, binv, ident[...])
         for p, (a, b) in zip(ps, outs):
             mm[p] = jnp.broadcast_to(a, (8, KEYS))
             mo[p] = jnp.broadcast_to(b, (8, KEYS))
 
+    @pl.loop(0, FIXED // 2)
+    def _(p):
+        scores([2 * p, 2 * p + 1], sc, 0)
+
     @pl.loop(0, n >> 1)
     def _(p):
-        scores([2 * p, 2 * p + 1])
-        masses([2 * p, 2 * p + 1])
+        late([2 * p, 2 * p + 1])
 
     @pl.when((n & 1) == 1)
     def _():
-        scores([n - 1])
-        masses([n - 1])
+        late([n - 1])
 
 
 def give_kernel(
-    tab, own, xj, okeep, jkeep, bucket, wa, wm, waT, wvT, woT, whT, wdT, gcol, dmine0, dother0, sc0, dmine2, dother2, mm2, mo2,
-    upd, mass, ident, dmine1, dother1, sc1, yb, ymst, yml, zst, zms, zret, zmr, parts, got, mparts, mgot,
+    tab, okeep, jkeep, bucket, dmine, dother, sc, mm2, mo2,
+    upd, mass, ident, yb0, yb1, yb2, yb3, ymst, yml, zst, zms, zret, zmr, parts, got, mparts, mgot,
     ysem, yrem, zsem, zrem, osem, orem,
 ):
     me, sub, others, peers = places()
-    rows = pl.ds(pl.multiple_of(sub * ROWS, ROWS), ROWS)
+    yb = (yb0, yb1, yb2, yb3)
     ident[...] = eye(256)
-    w = dict(wa=wa, wm=wm, waT=waT, wvT=wvT, woT=woT, whT=whT, wdT=wdT, gcol=gcol, ident=ident)
     binv = bucket[...] * LOG2E
     mline = lax.broadcasted_iota(I32, (JOBS, KEYS), 0)
-
-    def held(q, parts):
-        if q < EARLY:
-            return parts[0], q
-        if q < FIXED:
-            return parts[1], q - EARLY
-        return parts[2], q - FIXED
+    order = (4, 5, 2, 3, 0, 1)
+
+    def rows_of(p, c):
+        return pl.ds(pl.multiple_of(p * ROWS + c * PART, PART), PART)
 
     greet(others, peers)
     ycopies = []
-
-    def hand_back(q):
-        ref, at = held(q, (dother0, dother1, dother2))
+    for c in range(PARTS):
+        ycopies.append([])
         for d in range(1, SUBS):
             p = peers[d - 1]
-            part = ref.at[at, pl.ds(pl.multiple_of(p * ROWS, ROWS), ROWS), :]
-            ycopies.append(send(part, yb.at[q, sub], ysem.at[q, d - 1], yrem.at[q, d - 1], {"sub": p}))
-            ycopies[-1].start()
-        yb[q, sub] = ref[at, rows, :]
-
-    for q in list(range(EARLY)) + list(range(FIXED, JOBS)):
-        hand_back(q)
-    outs = do_scores(list(range(EARLY, FIXED)), tab, sub, own, xj, okeep, jkeep, w)
-    for at, out in enumerate(outs):
-        dmine1[at], dother1[at], sc1[at] = out
-        hand_back(EARLY + at)
+            copy = send(
+                dother.at[:, rows_of(p, c), :], yb[c].at[sub], ysem.at[c, d - 1], yrem.at[c, d - 1], {"sub": p}
+            )
+            copy.start()
+            ycopies[c].append(copy)
+    for c in range(PARTS):
+        yb[c][sub] = dother[:, rows_of(sub, c), :]
     n = (tab[3, 0] + (SUBS - 1) - sub) >> 2
     owners = [jnp.where(q < n, job_of(tab, q, sub)[0], -1) for q in range(JOBS)]
     for a in range(OWN):
         for s in range(SUBS):
             value = jnp.zeros((ROWS, D), F32)
             for q in range(JOBS):
-                ref, at = held(q, (dmine0, dmine1, dmine2))
-                value = value + jnp.where(owners[q] == a, ref[at, s * ROWS : s * ROWS + ROWS, :].astype(F32), 0.0)
+                value = value + jnp.where(owners[q] == a, dmine[q, s * ROWS : s * ROWS + ROWS, :].astype(F32), 0.0)
             parts[s, a] = value.astype(BF)
-    for copy in ycopies:
-        copy.wait()
-    zcopies = [None] * REACH
-    for t in (4, 5, 2, 3, 0, 1):
-        for u in range(MOST):
-            place = tab[2, t * 8 + u]
-            zst[t, u] = yb[place >> 2, place & 3]
-        zcopies[t] = send(zst.at[t], zret.at[t ^ 1], zsem.at[0, t], zrem.at[0, t ^ 1], {"img": others[t]})
-        zcopies[t].start()
+    places_of = [[tab[2, t * 8 + u] for u in range(MOST)] for t in range(REACH)]
+    zcopies = [[] for _ in range(PARTS)]
+
+    def pass_on(c):
+        for copy in ycopies[c]:
+            copy.wait()
+        for t in order:
+            for u in range(MOST):
+                zst[c, t, u] = yb[c][places_of[t][u] & 3, places_of[t][u] >> 2]
+            copy = send(zst.at[c, t], zret.at[c, t ^ 1], zsem.at[c, t], zrem.at[c, t ^ 1], {"img": others[t]})
+            copy.start()
+            zcopies[c].append(copy)
+
+    def some_masses(qs):
+        return do_masses(qs, [(sc, q) for q in qs], tab, sub, okeep, jkeep, binv, ident[...])
+
+    pass_on(0)
+    masses = some_masses([0, 1])
+    pass_on(1)
+    pass_on(2)
     ocopies = []
     for d in range(1, SUBS):
         to = {"sub": peers[d - 1]}
         ocopies.append(send(parts.at[peers[d - 1]], got.at[d - 1], osem.at[0, d - 1], orem.at[0, d - 1], to))
         ocopies[-1].start()
-    fixed = list(range(FIXED))
-    masses = do_masses(fixed, [held(q, (sc0, sc1)) for q in fixed], tab, sub, okeep, jkeep, binv, ident[...])
+    masses += some_masses([2, 3])
     mine = [masses[q][0] if q < FIXED else mm2[q - FIXED, 0:1, :] for q in range(JOBS)]
     away = [masses[q][1] if q < FIXED else mo2[q - FIXED, 0:1, :] for q in range(JOBS)]
     table = jnp.zeros((JOBS, KEYS), F32)
@@ -554,8 +582,10 @@
     yml[sub] = table
     ymcopies = []
     for d in range(1, SUBS):
-        ymcopies.append(send(ymst, yml.at[sub], ysem.at[JOBS, d - 1], yrem.at[JOBS, d - 1], {"sub": peers[d - 1]}))
+        to = {"sub": peers[d - 1]}
+        ymcopies.append(send(ymst, yml.at[sub], ysem.at[PARTS, d - 1], yrem.at[PARTS, d - 1], to))
         ymcopies[-1].start()
+    pass_on(3)
     table = jnp.zeros((OWN, KEYS), F32)
     for a in range(OWN):
         for q in range(JOBS):
@@ -565,33 +595,35 @@
         copy = send(mparts, mgot.at[d - 1], osem.at[1, d - 1], orem.at[1, d - 1], {"sub": peers[d - 1]})
         copy.start()
         ocopies.append(copy)
-    for copy in ocopies[: SUBS - 1]:
-        copy.wait()
-    for t in range(REACH):
-        zcopies[t].wait()
-    wants = [(t, u, sent_image(tab, t, u) - 1) for t in range(REACH) for u in range(MOST)]
-    for a in range(OWN):
-        value = parts[sub, a].astype(F32)
-        for d in range(SUBS - 1):
-            value = value + got[d, a].astype(F32)
-        for t, u, which in wants:
-            value = value + jnp.where(which == a, zret[t, u].astype(F32), 0.0)
-        upd[a] = value.astype(BF)
     for copy in ymcopies:
         copy.wait()
     ymasses = jnp.concatenate([yml[s] for s in range(SUBS)], axis=0)
     zmcopies = []
-    for t in (4, 5, 2, 3, 0, 1):
+    for t in order:
         back = jnp.zeros((8, KEYS), F32)
         for u in range(MOST):
-            place = tab[2, t * 8 + u]
+            place = places_of[t][u]
             back = jnp.where(mline == u, row_of(ymasses, (place & 3) * JOBS + (place >> 2)), back)
         zms[t] = back
-        zmcopies.append(send(zms.at[t], zmr.at[t ^ 1], zsem.at[1, t], zrem.at[1, t ^ 1], {"img": others[t]}))
+        to = {"img": others[t]}
+        zmcopies.append(send(zms.at[t], zmr.at[t ^ 1], zsem.at[PARTS, t], zrem.at[PARTS, t ^ 1], to))
         zmcopies[-1].start()
-    for copy in ocopies[SUBS - 1 :]:
+    wants = [(t, u, sent_image(tab, t, u) - 1) for t in range(REACH) for u in range(MOST)]
+    for copy in ocopies[: SUBS - 1]:
         copy.wait()
-    for copy in zmcopies:
+    for c in (0, 2):
+        for copy in zcopies[c] + zcopies[c + 1]:
+            copy.wait()
+        part = slice(c * PART, c * PART + 2 * PART)
+        for a in range(OWN):
+            value = parts[sub, a, part].astype(F32)
+            for d in range(SUBS - 1):
+                value = value + got[d, a, part].astype(F32)
+            for t, u, which in wants:
+                come = zret[c : c + 2, t, u].reshape(2 * PART, D)
+                value = value + jnp.where(which == a, come.astype(F32), 0.0)
+            upd[a, part] = value.astype(BF)
+    for copy in ocopies[SUBS - 1 :] + zmcopies:
         copy.wait()
     total = mparts[...] + mgot[0] + mgot[1] + mgot[2]
     for a in range(OWN):
@@ -620,55 +652,60 @@
 
 def local(descriptors, counts, visible, pair_list, pair_count, w_attend, w_value, w_output, w_hidden, norm_gain, w_down, w_match, unassigned_bucket):
     V = pltpu.VMEM
-    tab, *ready = pl.pallas_call(
+    peer = (SUBS - 1,)
+    tab, *ready, upper, okeep = pl.pallas_call(
         meet_kernel,
-        out_shape=(shape((8, 128), I32), *[shape((256, 256))] * 3, shape((512, 512)), shape((256, 512)), shape((512, 128), F32)),
-        in_specs=[VM, SM] + [VM] * 6,
-        out_specs=(VM,) * 7,
-        scratch_shapes=[V((8, 128), I32), V((REACH, 8, 128), I32), DMA((REACH,)), DMA((REACH,))],
+        out_shape=(
+            shape((8, 128), I32), *[shape((256, 256))] * 3, shape((512, 512)), shape((256, 512)), shape((512, 128), F32),
+            shape((SUBS, OWN, HALF, D)), shape((OWN, KEYS), F32),
+        ),
+        in_specs=[VM, SM, VM, SM, VM] + [VM] * 6,
+        out_specs=(VM,) * 9,
+        scratch_shapes=[
+            V((8, 128), I32), V((REACH, 8, 128), I32), V((SUBS, OWN, KEYS), F32),
+            DMA((REACH,)), DMA((REACH,)), DMA((2, SUBS - 1)), DMA((2, SUBS - 1)),
+        ],
         compiler_params=talk(0),
-    )(pair_list, pair_count, w_attend, w_value, w_output, w_hidden, norm_gain.reshape(1, -1), w_down)
-    own, xj, okeep, jkeep, *early = pl.pallas_call(
+    )(pair_list, pair_count, descriptors, counts, visible, w_attend, w_value, w_output, w_hidden, norm_gain.reshape(1, -1), w_down)
+    own, xj, jkeep = pl.pallas_call(
         fetch_kernel,
-        out_shape=(
-            shape((OWN, KEYS, D)), shape((JOBS, KEYS, D)), shape((OWN, KEYS), F32), shape((JOBS, KEYS), F32),
-            shape((EARLY, KEYS, D)), shape((EARLY, KEYS, D)), shape((EARLY, KEYS, KEYS), F32),
-        ),
-        in_specs=[SM, VM, SM, VM] + [VM] * 8,
-        out_specs=(VM,) * 7,
+        out_shape=(shape((OWN, KEYS, D)), shape((JOBS, KEYS, D)), shape((JOBS, KEYS), F32)),
+        in_specs=[SM, VM, VM, VM],
+        out_specs=(VM,) * 3,
         scratch_shapes=[
-            V((256, 256), BF),
-            V((REACH, MOST, ROWS, D), BF), V((REACH, MOST, ROWS, D), BF), V((REACH, 8, KEYS), F32), V((REACH, 8, KEYS), F32),
-            V((SUBS - 1, JOBS, ROWS, D), BF), V((SUBS, JOBS, KEYS), F32), V((SUBS - 1, JOBS, KEYS), F32), V((SUBS, OWN, KEYS), F32),
-            DMA((2, REACH)), DMA((2, REACH)), DMA((JOBS + 1, SUBS - 1)), DMA((JOBS + 1, SUBS - 1)), DMA((2, SUBS - 1)), DMA((2, SUBS - 1)),
+            V((PARTS, REACH, MOST, PART, D), BF), *[V((REACH, MOST, PART, D), BF)] * PARTS, V((REACH, 8, KEYS), F32), V((REACH, 8, KEYS), F32),
+            V((PARTS, SUBS - 1, JOBS, PART, D), BF), V((PARTS, SUBS, JOBS, PART, D), BF), V((SUBS, JOBS, KEYS), F32), V((SUBS - 1, JOBS, KEYS), F32),
+            V((SUBS, OWN, HALF, D), BF),
+            DMA((PARTS + 1, REACH)), DMA((PARTS + 1, REACH)), DMA((PARTS + 1, SUBS - 1)), DMA((PARTS + 1, SUBS - 1)), DMA(peer), DMA(peer),
         ],
         compiler_params=talk(1),
-    )(tab, descriptors, counts, visible, w_attend, w_match, *ready)
-    common = (tab, own, xj, okeep, jkeep, unassigned_bucket.reshape(1, 1), w_attend, w_match, *ready)
+    )(tab, descriptors, upper, okeep)
+    bucket = unassigned_bucket.reshape(1, 1)
     late = JOBS - FIXED
-    rest = pl.pallas_call(
+    done = pl.pallas_call(
         work_kernel,
-        out_shape=(shape((late, KEYS, D)), shape((late, KEYS, D)), shape((late, 8, KEYS), F32), shape((late, 8, KEYS), F32)),
+        out_shape=(
+            shape((JOBS, KEYS, D)), shape((JOBS, KEYS, D)), shape((FIXED, KEYS, KEYS), F32),
+            shape((late, 8, KEYS), F32), shape((late, 8, KEYS), F32),
+        ),
         in_specs=[SM] + [VM] * 13,
-        out_specs=(VM,) * 4,
+        out_specs=(VM,) * 5,
         scratch_shapes=[V((256, 256), BF), V((late, KEYS, KEYS), F32)],
         compiler_params=pltpu.CompilerParams(vmem_limit_bytes=LIMIT),
-    )(*common)
-    mid = FIXED - EARLY
+    )(tab, own, xj, okeep, jkeep, bucket, w_attend, w_match, *ready)
     return pl.pallas_call(
         give_kernel,
         out_shape=(shape((OWN, ROWS, D)), shape((OWN, ROWS), F32)),
-        in_specs=[SM] + [VM] * 20,
+        in_specs=[SM] + [VM] * 8,
         out_specs=(VM, VM),
         scratch_shapes=[
-            V((256, 256), BF), V((mid, KEYS, D), BF), V((mid, KEYS, D), BF), V((mid, KEYS, KEYS), F32),
-            V((JOBS, SUBS, ROWS, D), BF), V((JOBS, KEYS), F32), V((SUBS, JOBS, KEYS), F32),
-            V((REACH, MOST, ROWS, D), BF), V((REACH, 8, KEYS), F32), V((REACH, MOST, ROWS, D), BF), V((REACH, 8, KEYS), F32),
+            V((256, 256), BF), *[V((SUBS, JOBS, PART, D), BF)] * PARTS, V((JOBS, KEYS), F32), V((SUBS, JOBS, KEYS), F32),
+            V((PARTS, REACH, MOST, PART, D), BF), V((REACH, 8, KEYS), F32), V((PARTS, REACH, MOST, PART, D), BF), V((REACH, 8, KEYS), F32),
             V((SUBS, OWN, ROWS, D), BF), V((SUBS - 1, OWN, ROWS, D), BF), V((OWN, KEYS), F32), V((SUBS - 1, OWN, KEYS), F32),
-            DMA((JOBS + 1, SUBS - 1)), DMA((JOBS + 1, SUBS - 1)), DMA((2, REACH)), DMA((2, REACH)), DMA((2, SUBS - 1)), DMA((2, SUBS - 1)),
+            DMA((PARTS + 1, SUBS - 1)), DMA((PARTS + 1, SUBS - 1)), DMA((PARTS + 1, REACH)), DMA((PARTS + 1, REACH)), DMA((2, SUBS - 1)), DMA((2, SUBS - 1)),
         ],
         compiler_params=talk(2),
-    )(*common, *early, *rest)
+    )(tab, okeep, jkeep, bucket, *done)
 
 
 def solution(mesh):

time: 118 us -> 118 us (level)
    pallas_call x1, Pallas kernels: 49 us -> 38 us  [local(): pl.pallas_call(give_kernel, out_shape=(shape((OWN, ROWS, D)), shape((OWN,...]
    pallas_call x1, Pallas kernels: 9.04 us -> 19.2 us  [local(): pl.pallas_call(work_kernel, out_shape=(shape((JOBS, KEYS, D)), shape((JOB...]
    pallas_call x1, Pallas kernels: 19 us -> 26.6 us  [local(): pl.pallas_call(meet_kernel, out_shape=(shape((8, 128), I32), *[shape((256...]
    pallas_call x1, Pallas kernels: 35.3 us -> 28 us  [local(): pl.pallas_call(fetch_kernel, out_shape=(shape((OWN, KEYS, D)), shape((JOB...]
where the time goes in v5:
time: 118 us; the launch traced here: 117 us
  Pallas kernels  112 us (95%)
  local copies, waits for them, and re-layouts  3.63 us (3%)
  between operations  1.97 us (2%)
    pallas_call x1, Pallas kernels, local(): pl.pallas_call(give_kernel, out_shape=(shape((OWN, ROWS, D)), shape((OWN,...  38 us
    pallas_call x1, Pallas kernels, local(): pl.pallas_call(fetch_kernel, out_shape=(shape((OWN, KEYS, D)), shape((JOB...  28 us
    pallas_call x1, Pallas kernels, local(): pl.pallas_call(meet_kernel, out_shape=(shape((8, 128), I32), *[shape((256...  26.6 us
    pallas_call x1, Pallas kernels, local(): pl.pallas_call(work_kernel, out_shape=(shape((JOBS, KEYS, D)), shape((JOB...  19.2 us
    unnamed x7, local copies, waits for them, and re-layouts  3.63 us

profile of v5, /device:TPU:1, one launch (start us, length us, event | category | flops | bytes accessed | tf_op | source)
XLA Modules:
  0.0 117.3 jit_solution(12507769011156474223)
XLA Ops:
  1.9 0.0 copy-start.1
  1.9 0.7 copy-done.1
  2.6 0.7 copy.15.pairs
  3.3 26.6 %shard_map.140 = (s32[8,128]{1,0:T(8,128)}, bf16[256,256]{1,0:T(8,128)(2,1)}, bf16[256,256]{1,0:T(8,128)(2,1)}, bf16[256,256]{1,0:T(8,128)(2,1)}, bf16[512,512]{...) custom-call(s32[32,2]{1,0:T(8,128)} %copy.15.pairs, ...), custom_call_target="tpu_custom_call" | custom-call | tf_op jit(solution)/shard_map/pallas_call | solution.py:656
  29.9 28.0 %shard_map.141 = (bf16[8,256,256]{2,1,0:T(8,128)(2,1)}, bf16[8,256,256]{2,1,0:T(8,128)(2,1)}, f32[8,256]{1,0:T(8,128)}) custom-call(s32[8,128]{1,0:T(8,128)} %get-tuple-element.19.tab, bf16[8,64,256]{2,1,0:T(8,128)(2,1)} %desc.3, bf16[4,8,32,256]{3,2,1,0:T(8,128)(2,1)} %get-tuple-element.21.upper, f32[8,256]{1,0:T(8,128)} %get-tuple-element.20.okeep), custom_call_target="tpu_custom_call" | custom-call | tf_op jit(solution)/shard_map/pallas_call | solution.py:670
  57.9 19.2 %shard_map.142 = (bf16[8,256,256]{2,1,0:T(8,128)(2,1)}, bf16[8,256,256]{2,1,0:T(8,128)(2,1)}, f32[4,256,256]{2,1,0:T(8,128)}, f32[4,8,256]{2,1,0:T(8,128)}, f32[4,8,256]{2,1,0:T(8,128)}) custom-call(s32[8,128]{1,0:T(8,128)} %get-tuple-element.19.tab, bf16[8,256,256]{2,1,0:T(8,128)(2,1)} %get-tuple-element.23.own, bf16[8,256,256]{2,1,0:T(8,128)(2,1)} %get-tuple-element.24.xj, ...), custom_call_target="tpu_custom_call" | custom-call | tf_op jit(solution)/shard_map/pallas_call | solution.py:685
  77.1 38.0 %shard_map.143 = (bf16[8,64,256]{2,1,0:T(8,128)(2,1)}, f32[8,64]{1,0:T(8,128)}) custom-call(s32[8,128]{1,0:T(8,128)} %get-tuple-element.19.tab, f32[8,256]{1,0:T(8,128)} %get-tuple-element.20.okeep, f32[8,256]{1,0:T(8,128)} %get-tuple-element.22.jkeep, f32[1,1]{1,0:T(1,128)} %bitcast.3.bucket, bf16[8,256,256]{2,1,0:T(8,128)(2,1)} %get-tuple-element.31.dmine, ...), custom_call_target="tpu_custom_call" | custom-call | tf_op jit(solution)/shard_map/pallas_call | solution.py:696
  115.1 0.0 copy-start
  115.1 1.7 %copy.20 = bf16[8,64,256]{2,1,0:T(8,128)(2,1)} copy(bf16[8,64,256]{2,1,0:T(8,128)(2,1)} %get-tuple-element.38) | data formatting | bytes 524288
  116.8 0.0 copy-done
  116.8 0.6 copy.21
Async XLA Ops:
  1.9 0.7 copy-start.1
  115.1 1.7 %copy-start = (f32[8,64]{1,0:T(8,128)S(1)}, f32[8,64]{1,0:T(8,128)}, u32[]{:S(2)}) copy-start(f32[8,64]{1,0:T(8,128)} %get-tuple-element.39) | copy-start | bytes 6148

commit v6 on v5

--- a/solution.py
+++ b/solution.py
@@ -28,7 +28,7 @@
 PART = ROWS // PARTS
 HALF = ROWS // 2
 MESH = pl.DeviceIdType.MESH
-LIMIT = 56 * 2**20
+LIMIT = 24 * 2**20
 
 
 def nn(a, b):
@@ -271,9 +271,12 @@
 
 
 def own_rows(pairs, live_count, me, img_count):
-    first = pairs[:, 0:1]
-    second = pairs[:, 1:2]
-    slots = pairs.shape[0]
+    slots = pairs.shape[1]
+    up = lax.broadcasted_iota(I32, (slots, slots), 0)
+    across = lax.broadcasted_iota(I32, (slots, slots), 1)
+    first, second = (
+        jnp.sum(jnp.where(up == across, pairs[k : k + 1, :], 0), axis=1, keepdims=True) for k in (0, 1)
+    )
     row_ids = lax.broadcasted_iota(I32, (slots, 1), 0)
     ahead = (second >> 3) - me
     ahead = jnp.where(ahead < 0, ahead + img_count, ahead)
@@ -281,8 +284,6 @@
     live = row_ids < live_count
     key = jnp.where(live, turn, 15)
     code = 1 + (first & 7) * 8 + (second & 7)
-    up = lax.broadcasted_iota(I32, (slots, slots), 0)
-    across = lax.broadcasted_iota(I32, (slots, slots), 1)
     key_row = jnp.sum(jnp.where(up == across, key, 0), axis=0, keepdims=True)
     rank = jnp.sum(jnp.where((key_row == key) & (across < up), 1, 0), axis=1, keepdims=True)
     lanes = lax.broadcasted_iota(I32, (slots, 128), 1)
@@ -366,10 +367,22 @@
 
 
 def meet_kernel(
-    pairs, pair_count, desc, counts, visible, wa, wv, wo, wh, gain, wd,
-    tab, waT, wvT, woT, whT, wdT, gcol, upper, okeep, told, near, omask, ssem, rsem, osem, orem,
+    pairs, pair_count, counts, desc_far, visible_far, wa_far, wv_far, wo_far, wh_far, gain_far, wd_far,
+    tab, waT, wvT, woT, whT, wdT, gcol, upper, okeep, told, near, omask, desc, visible, wa, wv, wo, wh, gain, wd,
+    ssem, rsem, osem, orem, lsem,
 ):
     me, sub, others, peers = places()
+    far = (desc_far, visible_far, wa_far, wv_far, wo_far, wh_far, gain_far, wd_far)
+    loads = [
+        pltpu.make_async_copy(src, dst, lsem.at[i])
+        for i, (src, dst) in enumerate(zip(far, (desc, visible, wa, wv, wo, wh, gain, wd)))
+    ]
+    for load in loads:
+        load.start()
+    own, out = own_rows(pairs[...], pair_count[0], me, lax.axis_size("img"))
+    told[...] = jnp.broadcast_to(out, (8, 128))
+    for load in loads[:2]:
+        load.wait()
     omask[0] = own_mask(counts, visible, sub)
     greet(others, peers)
     ocopies = []
@@ -377,12 +390,12 @@
         to = {"sub": peers[d - 1]}
         ocopies.append(send(omask.at[0], omask.at[d], osem.at[1, d - 1], orem.at[1, d - 1], to))
         ocopies.append(send(desc.at[:, 0:HALF, :], upper.at[sub], osem.at[0, d - 1], orem.at[0, d - 1], to))
-    own, out = own_rows(pairs[...], pair_count[0], me, lax.axis_size("img"))
-    told[...] = jnp.broadcast_to(out, (8, 128))
     copies = [send(told, near.at[t ^ 1], ssem.at[t], rsem.at[t ^ 1], {"img": others[t]}) for t in range(REACH)]
     for copy in copies + ocopies:
         copy.start()
     upper[sub] = desc[:, 0:HALF, :]
+    for load in loads[2:]:
+        load.wait()
     prepare(wa, wv, wo, wh, gain, wd, waT, wvT, woT, whT, wdT, gcol)
     for copy in copies:
         copy.wait()
@@ -478,7 +491,7 @@
 
 
 def work_kernel(
-    tab, own, xj, okeep, jkeep, bucket, wa, wm, waT, wvT, woT, whT, wdT, gcol, dmine, dother, sc, mm, mo, ident, sclate
+    tab, own, xj, okeep, jkeep, bucket, wa, wm, waT, wvT, woT, whT, wdT, gcol, dmine, dother, mm, mo, ident, sc
 ):
     sub = lax.axis_index("sub")
     ident[...] = eye(256)
@@ -486,22 +499,15 @@
     n = ((tab[3, 0] + (SUBS - 1) - sub) >> 2) - FIXED
     binv = bucket[...] * LOG2E
 
-    def scores(qs, ref, first):
-        outs = do_scores(qs, tab, sub, own, xj, okeep, jkeep, w)
-        for q, out in zip(qs, outs):
-            dmine[q], dother[q], ref[q - first] = out
-
     def late(ps):
-        scores([FIXED + p for p in ps], sclate, FIXED)
-        outs = do_masses([FIXED + p for p in ps], [(sclate, p) for p in ps], tab, sub, okeep, jkeep, binv, ident[...])
+        outs = do_scores([FIXED + p for p in ps], tab, sub, own, xj, okeep, jkeep, w)
+        for p, out in zip(ps, outs):
+            dmine[p], dother[p], sc[p] = out
+        outs = do_masses([FIXED + p for p in ps], [(sc, p) for p in ps], tab, sub, okeep, jkeep, binv, ident[...])
         for p, (a, b) in zip(ps, outs):
             mm[p] = jnp.broadcast_to(a, (8, KEYS))
             mo[p] = jnp.broadcast_to(b, (8, KEYS))
 
-    @pl.loop(0, FIXED // 2)
-    def _(p):
-        scores([2 * p, 2 * p + 1], sc, 0)
-
     @pl.loop(0, n >> 1)
     def _(p):
         late([2 * p, 2 * p + 1])
@@ -512,13 +518,14 @@
 
 
 def give_kernel(
-    tab, okeep, jkeep, bucket, dmine, dother, sc, mm2, mo2,
-    upd, mass, ident, yb0, yb1, yb2, yb3, ymst, yml, zst, zms, zret, zmr, parts, got, mparts, mgot,
+    tab, own, xj, okeep, jkeep, bucket, wa, wm, waT, wvT, woT, whT, wdT, gcol, dmine2, dother2, mm2, mo2,
+    zret, zmr, gm, mparts, mgot, ident, dmine, dother, sc, yb0, yb1, yb2, yb3, ymst, yml, zst, zms,
     ysem, yrem, zsem, zrem, osem, orem,
 ):
     me, sub, others, peers = places()
     yb = (yb0, yb1, yb2, yb3)
     ident[...] = eye(256)
+    w = dict(wa=wa, wm=wm, waT=waT, wvT=wvT, woT=woT, whT=whT, wdT=wdT, gcol=gcol, ident=ident)
     binv = bucket[...] * LOG2E
     mline = lax.broadcasted_iota(I32, (JOBS, KEYS), 0)
     order = (4, 5, 2, 3, 0, 1)
@@ -526,27 +533,42 @@
     def rows_of(p, c):
         return pl.ds(pl.multiple_of(p * ROWS + c * PART, PART), PART)
 
+    def block_of(p):
+        return pl.ds(pl.multiple_of(p * ROWS, ROWS), ROWS)
+
     greet(others, peers)
-    ycopies = []
-    for c in range(PARTS):
-        ycopies.append([])
+    ycopies = [[] for _ in range(PARTS)]
+    ocopies = []
+
+    def hand_back(group, theirs, at, to):
+        for c in range(PARTS):
+            for d in range(1, SUBS):
+                p = peers[d - 1]
+                copy = send(
+                    theirs.at[at, rows_of(p, c), :], yb[c].at[sub, to], ysem.at[group, c, d - 1], yrem.at[group, c, d - 1], {"sub": p}
+                )
+                copy.start()
+                ycopies[c].append(copy)
+        for c in range(PARTS):
+            yb[c][sub, to] = theirs[at, rows_of(sub, c), :]
+
+    def hand_mine(group, mine, at, to):
         for d in range(1, SUBS):
             p = peers[d - 1]
-            copy = send(
-                dother.at[:, rows_of(p, c), :], yb[c].at[sub], ysem.at[c, d - 1], yrem.at[c, d - 1], {"sub": p}
-            )
+            copy = send(mine.at[at, block_of(p), :], gm.at[sub, to], osem.at[group, d - 1], orem.at[group, d - 1], {"sub": p})
             copy.start()
-            ycopies[c].append(copy)
-    for c in range(PARTS):
-        yb[c][sub] = dother[:, rows_of(sub, c), :]
+            ocopies.append(copy)
+        gm[sub, to] = mine[at, block_of(sub), :]
+
+    hand_back(2, dother2, slice(0, JOBS - FIXED), slice(FIXED, JOBS))
+    for group in range(2):
+        at = slice(2 * group, 2 * group + 2)
+        outs = do_scores([2 * group, 2 * group + 1], tab, sub, own, xj, okeep, jkeep, w)
+        for q, out in enumerate(outs, 2 * group):
+            dmine[q], dother[q], sc[q] = out
+        hand_back(group, dother, at, at)
     n = (tab[3, 0] + (SUBS - 1) - sub) >> 2
     owners = [jnp.where(q < n, job_of(tab, q, sub)[0], -1) for q in range(JOBS)]
-    for a in range(OWN):
-        for s in range(SUBS):
-            value = jnp.zeros((ROWS, D), F32)
-            for q in range(JOBS):
-                value = value + jnp.where(owners[q] == a, dmine[q, s * ROWS : s * ROWS + ROWS, :].astype(F32), 0.0)
-            parts[s, a] = value.astype(BF)
     places_of = [[tab[2, t * 8 + u] for u in range(MOST)] for t in range(REACH)]
     zcopies = [[] for _ in range(PARTS)]
 
@@ -563,15 +585,13 @@
     def some_masses(qs):
         return do_masses(qs, [(sc, q) for q in qs], tab, sub, okeep, jkeep, binv, ident[...])
 
-    pass_on(0)
+    for c in range(PARTS):
+        pass_on(c)
+    hand_mine(2, dmine2, slice(0, JOBS - FIXED), slice(FIXED, JOBS))
+    for group in range(2):
+        at = slice(2 * group, 2 * group + 2)
+        hand_mine(group, dmine, at, at)
     masses = some_masses([0, 1])
-    pass_on(1)
-    pass_on(2)
-    ocopies = []
-    for d in range(1, SUBS):
-        to = {"sub": peers[d - 1]}
-        ocopies.append(send(parts.at[peers[d - 1]], got.at[d - 1], osem.at[0, d - 1], orem.at[0, d - 1], to))
-        ocopies[-1].start()
     masses += some_masses([2, 3])
     mine = [masses[q][0] if q < FIXED else mm2[q - FIXED, 0:1, :] for q in range(JOBS)]
     away = [masses[q][1] if q < FIXED else mo2[q - FIXED, 0:1, :] for q in range(JOBS)]
@@ -583,16 +603,15 @@
     ymcopies = []
     for d in range(1, SUBS):
         to = {"sub": peers[d - 1]}
-        ymcopies.append(send(ymst, yml.at[sub], ysem.at[PARTS, d - 1], yrem.at[PARTS, d - 1], to))
+        ymcopies.append(send(ymst, yml.at[sub], ysem.at[3, 0, d - 1], yrem.at[3, 0, d - 1], to))
         ymcopies[-1].start()
-    pass_on(3)
     table = jnp.zeros((OWN, KEYS), F32)
     for a in range(OWN):
         for q in range(JOBS):
             table = table + jnp.where((mline == a) & (owners[q] == a), mine[q], 0.0)
     mparts[...] = table
     for d in range(1, SUBS):
-        copy = send(mparts, mgot.at[d - 1], osem.at[1, d - 1], orem.at[1, d - 1], {"sub": peers[d - 1]})
+        copy = send(mparts, mgot.at[d - 1], osem.at[3, d - 1], orem.at[3, d - 1], {"sub": peers[d - 1]})
         copy.start()
         ocopies.append(copy)
     for copy in ymcopies:
@@ -608,29 +627,43 @@
         to = {"img": others[t]}
         zmcopies.append(send(zms.at[t], zmr.at[t ^ 1], zsem.at[PARTS, t], zrem.at[PARTS, t ^ 1], to))
         zmcopies[-1].start()
-    wants = [(t, u, sent_image(tab, t, u) - 1) for t in range(REACH) for u in range(MOST)]
-    for copy in ocopies[: SUBS - 1]:
+    for copy in ocopies + zmcopies:
         copy.wait()
-    for c in (0, 2):
-        for copy in zcopies[c] + zcopies[c + 1]:
+    for c in range(PARTS):
+        for copy in zcopies[c]:
             copy.wait()
-        part = slice(c * PART, c * PART + 2 * PART)
-        for a in range(OWN):
-            value = parts[sub, a, part].astype(F32)
-            for d in range(SUBS - 1):
-                value = value + got[d, a, part].astype(F32)
-            for t, u, which in wants:
-                come = zret[c : c + 2, t, u].reshape(2 * PART, D)
-                value = value + jnp.where(which == a, come.astype(F32), 0.0)
-            upd[a, part] = value.astype(BF)
-    for copy in ocopies[SUBS - 1 :] + zmcopies:
-        copy.wait()
-    total = mparts[...] + mgot[0] + mgot[1] + mgot[2]
-    for a in range(OWN):
-        extra = jnp.zeros((1, KEYS), F32)
-        for t, u, which in wants:
-            extra = extra + jnp.where(which == a, zmr[t, u : u + 1, :], 0.0)
-        total = total + jnp.where(mline == a, extra, 0.0)
+
+
+def sum_kernel(tab, zret, zmr, gm, mparts, mgot, upd, mass, acc, macc):
+    sub = lax.axis_index("sub")
+    acc[...] = jnp.zeros_like(acc)
+
+    @pl.loop(0, SUBS * JOBS)
+    def _(g):
+        code = tab[0, g]
+
+        @pl.when(code > 0)
+        def _():
+            which = (code >> 8) & 7
+            acc[which] = acc[which] + gm[g & 3, g >> 2].astype(F32)
+
+    macc[...] = mparts[...] + mgot[0] + mgot[1] + mgot[2]
+    line = lax.broadcasted_iota(I32, (8, KEYS), 0)
+
+    @pl.loop(0, REACH)
+    def _(t):
+        for u in range(MOST):
+            which = tab[1, t * 8 + u] - 1
+
+            @pl.when(which >= 0)
+            def _():
+                for c in range(PARTS):
+                    rows = slice(c * PART, c * PART + PART)
+                    acc[which, rows] = acc[which, rows] + zret[c, t, u].astype(F32)
+                macc[...] = macc[...] + jnp.where(line == which, zmr[t, u : u + 1, :], 0.0)
+
+    upd[...] = acc[...].astype(BF)
+    total = macc[...]
     out = jnp.zeros((OWN, ROWS), F32)
     for s in range(SUBS):
         out = jnp.where(sub == s, total[:, s * ROWS : s * ROWS + ROWS], out)
@@ -640,14 +673,18 @@
 VM = pl.BlockSpec(memory_space=pltpu.VMEM)
 SM = pl.BlockSpec(memory_space=pltpu.SMEM)
 DMA = pltpu.SemaphoreType.DMA
+HB = pl.BlockSpec(memory_space=pltpu.HBM)
 
 
 def shape(dims, kind=BF):
     return jax.ShapeDtypeStruct(dims, kind)
 
 
-def talk(number):
-    return pltpu.CompilerParams(collective_id=number, has_side_effects=True, vmem_limit_bytes=LIMIT)
+def talk(number, limit=LIMIT):
+    return pltpu.CompilerParams(collective_id=number, has_side_effects=True, vmem_limit_bytes=limit)
+
+
+COST = pl.CostEstimate(flops=10**10, bytes_accessed=5 * 10**7, transcendentals=10**7)
 
 
 def local(descriptors, counts, visible, pair_list, pair_count, w_attend, w_value, w_output, w_hidden, norm_gain, w_down, w_match, unassigned_bucket):
@@ -659,14 +696,16 @@
             shape((8, 128), I32), *[shape((256, 256))] * 3, shape((512, 512)), shape((256, 512)), shape((512, 128), F32),
             shape((SUBS, OWN, HALF, D)), shape((OWN, KEYS), F32),
         ),
-        in_specs=[VM, SM, VM, SM, VM] + [VM] * 6,
+        in_specs=[VM, SM, SM] + [HB] * 8,
         out_specs=(VM,) * 9,
         scratch_shapes=[
             V((8, 128), I32), V((REACH, 8, 128), I32), V((SUBS, OWN, KEYS), F32),
-            DMA((REACH,)), DMA((REACH,)), DMA((2, SUBS - 1)), DMA((2, SUBS - 1)),
+            V((OWN, ROWS, D), BF), V((OWN, ROWS), I32), *[V((256, 256), BF)] * 3, V((512, 512), BF), V((1, 512), F32), V((512, 256), BF),
+            DMA((REACH,)), DMA((REACH,)), DMA((2, SUBS - 1)), DMA((2, SUBS - 1)), DMA((8,)),
         ],
-        compiler_params=talk(0),
-    )(pair_list, pair_count, descriptors, counts, visible, w_attend, w_value, w_output, w_hidden, norm_gain.reshape(1, -1), w_down)
+        compiler_params=talk(0, 56 * 2**20),
+        cost_estimate=COST,
+    )(pair_list.T, pair_count, counts, descriptors, visible, w_attend, w_value, w_output, w_hidden, norm_gain.reshape(1, -1), w_down)
     own, xj, jkeep = pl.pallas_call(
         fetch_kernel,
         out_shape=(shape((OWN, KEYS, D)), shape((JOBS, KEYS, D)), shape((JOBS, KEYS), F32)),
@@ -679,33 +718,44 @@
             DMA((PARTS + 1, REACH)), DMA((PARTS + 1, REACH)), DMA((PARTS + 1, SUBS - 1)), DMA((PARTS + 1, SUBS - 1)), DMA(peer), DMA(peer),
         ],
         compiler_params=talk(1),
+        cost_estimate=COST,
     )(tab, descriptors, upper, okeep)
     bucket = unassigned_bucket.reshape(1, 1)
     late = JOBS - FIXED
-    done = pl.pallas_call(
+    common = (tab, own, xj, okeep, jkeep, bucket, w_attend, w_match, *ready)
+    rest = pl.pallas_call(
         work_kernel,
-        out_shape=(
-            shape((JOBS, KEYS, D)), shape((JOBS, KEYS, D)), shape((FIXED, KEYS, KEYS), F32),
-            shape((late, 8, KEYS), F32), shape((late, 8, KEYS), F32),
-        ),
+        out_shape=(shape((late, KEYS, D)), shape((late, KEYS, D)), shape((late, 8, KEYS), F32), shape((late, 8, KEYS), F32)),
         in_specs=[SM] + [VM] * 13,
-        out_specs=(VM,) * 5,
+        out_specs=(VM,) * 4,
         scratch_shapes=[V((256, 256), BF), V((late, KEYS, KEYS), F32)],
         compiler_params=pltpu.CompilerParams(vmem_limit_bytes=LIMIT),
-    )(tab, own, xj, okeep, jkeep, bucket, w_attend, w_match, *ready)
-    return pl.pallas_call(
+    )(*common)
+    back = pl.pallas_call(
         give_kernel,
-        out_shape=(shape((OWN, ROWS, D)), shape((OWN, ROWS), F32)),
-        in_specs=[SM] + [VM] * 8,
-        out_specs=(VM, VM),
+        out_shape=(
+            shape((PARTS, REACH, MOST, PART, D)), shape((REACH, 8, KEYS), F32), shape((SUBS, JOBS, ROWS, D)),
+            shape((OWN, KEYS), F32), shape((SUBS - 1, OWN, KEYS), F32),
+        ),
+        in_specs=[SM] + [VM] * 17,
+        out_specs=(VM,) * 5,
         scratch_shapes=[
-            V((256, 256), BF), *[V((SUBS, JOBS, PART, D), BF)] * PARTS, V((JOBS, KEYS), F32), V((SUBS, JOBS, KEYS), F32),
-            V((PARTS, REACH, MOST, PART, D), BF), V((REACH, 8, KEYS), F32), V((PARTS, REACH, MOST, PART, D), BF), V((REACH, 8, KEYS), F32),
-            V((SUBS, OWN, ROWS, D), BF), V((SUBS - 1, OWN, ROWS, D), BF), V((OWN, KEYS), F32), V((SUBS - 1, OWN, KEYS), F32),
-            DMA((PARTS + 1, SUBS - 1)), DMA((PARTS + 1, SUBS - 1)), DMA((PARTS + 1, REACH)), DMA((PARTS + 1, REACH)), DMA((2, SUBS - 1)), DMA((2, SUBS - 1)),
+            V((256, 256), BF), V((FIXED, KEYS, D), BF), V((FIXED, KEYS, D), BF), V((FIXED, KEYS, KEYS), F32),
+            *[V((SUBS, JOBS, PART, D), BF)] * PARTS, V((JOBS, KEYS), F32), V((SUBS, JOBS, KEYS), F32),
+            V((PARTS, REACH, MOST, PART, D), BF), V((REACH, 8, KEYS), F32),
+            DMA((4, PARTS, SUBS - 1)), DMA((4, PARTS, SUBS - 1)), DMA((PARTS + 1, REACH)), DMA((PARTS + 1, REACH)), DMA((4, SUBS - 1)), DMA((4, SUBS - 1)),
         ],
         compiler_params=talk(2),
-    )(tab, okeep, jkeep, bucket, *done)
+        cost_estimate=COST,
+    )(*common, *rest)
+    return pl.pallas_call(
+        sum_kernel,
+        out_shape=(shape((OWN, ROWS, D)), shape((OWN, ROWS), F32)),
+        in_specs=[SM] + [VM] * 5,
+        out_specs=(VM, VM),
+        scratch_shapes=[V((OWN, ROWS, D), F32), V((OWN, KEYS), F32)],
+        compiler_params=pltpu.CompilerParams(vmem_limit_bytes=LIMIT),
+    )(tab, *back)
 
 
 def solution(mesh):

time: 118 us -> 107 us (0.907)
  Pallas kernels: 112 us -> 103 us
    pallas_call x2 -> x3, Pallas kernels: 57.2 us -> 49.4 us  [the longest x1 46 us: local(): pl.pallas_call(give_kernel, out_shape=(shape((PARTS, REACH, MOST, PART, D...]
    pallas_call x1, Pallas kernels: 28 us -> 26.4 us  [local(): pl.pallas_call(fetch_kernel, out_shape=(shape((OWN, KEYS, D)), shape((JOB...]
    unnamed x7 -> x24, local copies, waits for them, and re-layouts: 3.63 us -> 2.45 us
where the time goes in v6:
time: 107 us
  Pallas kernels  103 us (96%)
  local copies, waits for them, and re-layouts  2.45 us (2%)
  between operations  2.08 us (2%)
    pallas_call x1, Pallas kernels, local(): pl.pallas_call(give_kernel, out_shape=(shape((PARTS, REACH, MOST, PART, D...  46 us
    pallas_call x1, Pallas kernels, local(): pl.pallas_call(meet_kernel, out_shape=(shape((8, 128), I32), *[shape((256...  26.8 us
    pallas_call x1, Pallas kernels, local(): pl.pallas_call(fetch_kernel, out_shape=(shape((OWN, KEYS, D)), shape((JOB...  26.4 us
    pallas_call x1, Pallas kernels, local(): pl.pallas_call(sum_kernel, out_shape=(shape((OWN, ROWS, D)), shape((OWN,...  2.63 us
    unnamed x24, local copies, waits for them, and re-layouts  2.45 us

profile of v6, /device:TPU:1, one launch (start us, length us, event | category | flops | bytes accessed | tf_op | source)
XLA Modules:
  0.0 107.1 jit_solution(5606676581183035463)
XLA Ops:
  1.9 0.0 copy-start.10
  1.9 26.8 %shard_map.140 = (s32[8,128]{1,0:T(8,128)}, bf16[256,256]{1,0:T(8,128)(2,1)}, bf16[256,256]{1,0:T(8,128)(2,1)}, bf16[256,256]{1,0:T(8,128)(2,1)}, bf16[512,512]{...) custom-call(s32[2,32]{1,0:T(2,128)} %bitcast.6, ...), custom_call_target="tpu_custom_call" | custom-call | flops 10000000000 | bytes 50000000 | tf_op jit(solution)/shard_map/pallas_call | solution.py:693
  28.7 0.0 copy-done.10
  28.7 0.0 copy-start.8
  28.7 0.7 copy-done.8
  29.4 0.0 copy-start.9
  29.4 0.7 copy-done.9
  30.1 0.0 copy-start.11
  30.1 1.0 copy-done.11
  31.1 0.0 copy-start
  31.1 0.0 copy-start.1
  31.1 0.0 copy-start.2
  31.1 0.0 copy-start.3
  31.2 0.0 copy-start.4
  31.2 0.0 copy-start.5
  31.2 0.0 copy-start.6
  31.2 0.0 copy-start.7
  31.2 26.4 %shard_map.141 = (bf16[8,256,256]{2,1,0:T(8,128)(2,1)S(1)}, bf16[8,256,256]{2,1,0:T(8,128)(2,1)S(1)}, f32[8,256]{1,0:T(8,128)S(1)}) custom-call(s32[8,128]{1,0:T(8,128)S(1)} %copy-done.8, bf16[8,64,256]{2,1,0:T(8,128)(2,1)S(1)} %copy-done.10, bf16[4,8,32,256]{3,2,1,0:T(8,128)(2,1)S(1)} %copy-done.11, f32[8,256]{1,0:T(8,128)S(1)} %copy-done.9), custom_call_target="tpu_custom_call" | custom-call | flops 10000000000 | bytes 50000000 | tf_op jit(solution)/shard_map/pallas_call | solution.py:709
  57.6 0.0 copy-done
  57.6 0.0 copy-done.1
  57.6 0.0 copy-done.2
  57.6 0.0 copy-done.3
  57.6 0.0 copy-done.4
  57.6 0.0 copy-done.5
  57.6 0.0 copy-done.6
  57.6 0.0 copy-done.7
  57.6 0.8 shard_map.142
  58.5 46.0 %shard_map.143 = (bf16[4,6,6,16,256]{4,3,2,1,0:T(8,128)(2,1)S(1)}, f32[6,8,256]{2,1,0:T(8,128)S(1)}, bf16[4,8,64,256]{3,2,1,0:T(8,128)(2,1)S(1)}, f32[8,256]{1,0:T(8,128)S(1)}, f32[3,8,256]{2,1,0:T(8,128)S(1)}) custom-call(s32[8,128]{1,0:T(8,128)S(1)} %copy-done.8, bf16[8,256,256]{2,1,0:T(8,128)(2,1)S(1)} %get-tuple-element.26.own, ...), custom_call_target="tpu_custom_call" | custom-call | flops 10000000000 | bytes 50000000 | tf_op jit(solution)/shard_map/pallas_call | solution.py:734
  104.5 2.6 %shard_map.144 = (bf16[8,64,256]{2,1,0:T(8,128)(2,1)}, f32[8,64]{1,0:T(8,128)}) custom-call(s32[8,128]{1,0:T(8,128)S(1)} %copy-done.8, bf16[4,6,6,16,256]{4,3,2,1,0:T(8,128)(2,1)S(1)} %get-tuple-element.39.zret, f32[6,8,256]{2,1,0:T(8,128)S(1)} %get-tuple-element.40.zmr, bf16[4,8,64,256]{3,2,1,0:T(8,128)(2,1)S(1)} %get-tuple-element.41.gm, ...), custom_call_target="tpu_custom_call" | custom-call | tf_op jit(solution)/shard_map/pallas_call | solution.py:751
Async XLA Ops:
  1.9 26.8 %copy-start.10 = (bf16[8,64,256]{2,1,0:T(8,128)(2,1)S(1)}, bf16[8,64,256]{2,1,0:T(8,128)(2,1)}, u32[]{:S(2)}) copy-start(bf16[8,64,256]{2,1,0:T(8,128)(2,1)} %desc.1) | copy-start | bytes 786436
  28.7 0.7 copy-start.8
  29.4 0.7 copy-start.9
  30.1 1.0 copy-start.11
  31.1 26.4 %copy-start = (bf16[512,512]{1,0:T(8,128)(2,1)S(1)}, bf16[512,512]{1,0:T(8,128)(2,1)}, u32[]{:S(2)}) copy-start(bf16[512,512]{1,0:T(8,128)(2,1)} %get-tuple-element.32.whT) | copy-start | bytes 1572868
  31.1 26.4 %copy-start.1 = (bf16[256,512]{1,0:T(8,128)(2,1)S(1)}, bf16[256,512]{1,0:T(8,128)(2,1)}, u32[]{:S(2)}) copy-start(bf16[256,512]{1,0:T(8,128)(2,1)} %get-tuple-element.33.wdT) | copy-start | bytes 786436
  31.1 26.4 %copy-start.2 = (f32[512,128]{1,0:T(8,128)S(1)}, f32[512,128]{1,0:T(8,128)}, u32[]{:S(2)}) copy-start(f32[512,128]{1,0:T(8,128)} %get-tuple-element.34.gcol) | copy-start | bytes 786436
  31.1 26.4 %copy-start.3 = (bf16[256,256]{1,0:T(8,128)(2,1)S(1)}, bf16[256,256]{1,0:T(8,128)(2,1)}, u32[]{:S(2)}) copy-start(bf16[256,256]{1,0:T(8,128)(2,1)} %wa.3) | copy-start | bytes 393220
  31.2 26.4 %copy-start.4 = (bf16[256,256]{1,0:T(8,128)(2,1)S(1)}, bf16[256,256]{1,0:T(8,128)(2,1)}, u32[]{:S(2)}) copy-start(bf16[256,256]{1,0:T(8,128)(2,1)} %wm.3) | copy-start | bytes 393220
  31.2 26.4 %copy-start.5 = (bf16[256,256]{1,0:T(8,128)(2,1)S(1)}, bf16[256,256]{1,0:T(8,128)(2,1)}, u32[]{:S(2)}) copy-start(bf16[256,256]{1,0:T(8,128)(2,1)} %get-tuple-element.29.waT) | copy-start | bytes 393220
  31.2 26.4 %copy-start.6 = (bf16[256,256]{1,0:T(8,128)(2,1)S(1)}, bf16[256,256]{1,0:T(8,128)(2,1)}, u32[]{:S(2)}) copy-start(bf16[256,256]{1,0:T(8,128)(2,1)} %get-tuple-element.30.wvT) | copy-start | bytes 393220
  31.2 26.4 %copy-start.7 = (bf16[256,256]{1,0:T(8,128)(2,1)S(1)}, bf16[256,256]{1,0:T(8,128)(2,1)}, u32[]{:S(2)}) copy-start(bf16[256,256]{1,0:T(8,128)(2,1)} %get-tuple-element.31.woT) | copy-start | bytes 393220

commit v7 on v6

--- a/solution.py
+++ b/solution.py
@@ -26,7 +26,7 @@
 FIXED = 4
 PARTS = 4
 PART = ROWS // PARTS
-HALF = ROWS // 2
+HALF = 16
 MESH = pl.DeviceIdType.MESH
 LIMIT = 24 * 2**20
 
@@ -714,7 +714,7 @@
         scratch_shapes=[
             V((PARTS, REACH, MOST, PART, D), BF), *[V((REACH, MOST, PART, D), BF)] * PARTS, V((REACH, 8, KEYS), F32), V((REACH, 8, KEYS), F32),
             V((PARTS, SUBS - 1, JOBS, PART, D), BF), V((PARTS, SUBS, JOBS, PART, D), BF), V((SUBS, JOBS, KEYS), F32), V((SUBS - 1, JOBS, KEYS), F32),
-            V((SUBS, OWN, HALF, D), BF),
+            V((SUBS, OWN, ROWS - HALF, D), BF),
             DMA((PARTS + 1, REACH)), DMA((PARTS + 1, REACH)), DMA((PARTS + 1, SUBS - 1)), DMA((PARTS + 1, SUBS - 1)), DMA(peer), DMA(peer),
         ],
         compiler_params=talk(1),

time: 107 us -> 104 us (0.972)
  Pallas kernels: 103 us -> 99.4 us
    pallas_call x1, Pallas kernels: 46 us -> 40.1 us  [local(): pl.pallas_call(give_kernel, out_shape=(shape((PARTS, REACH, MOST, PART, D...]
    pallas_call x1, Pallas kernels: 0.82 us -> 6.43 us  [local(): pl.pallas_call(work_kernel, out_shape=(shape((late, KEYS, D)), shape((lat...]
    pallas_call x1, Pallas kernels: 26.8 us -> 23.9 us  [local(): pl.pallas_call(meet_kernel, out_shape=(shape((8, 128), I32), *[shape((256...]
where the time goes in v7:
time: 104 us
  Pallas kernels  99.4 us (96%)
  local copies, waits for them, and re-layouts  2.35 us (2%)
  between operations  2.08 us (2%)
    pallas_call x1, Pallas kernels, local(): pl.pallas_call(give_kernel, out_shape=(shape((PARTS, REACH, MOST, PART, D...  40.1 us
    pallas_call x1, Pallas kernels, local(): pl.pallas_call(fetch_kernel, out_shape=(shape((OWN, KEYS, D)), shape((JOB...  26.4 us
    pallas_call x1, Pallas kernels, local(): pl.pallas_call(meet_kernel, out_shape=(shape((8, 128), I32), *[shape((256...  23.9 us
    pallas_call x1, Pallas kernels, local(): pl.pallas_call(work_kernel, out_shape=(shape((late, KEYS, D)), shape((lat...  6.43 us
    pallas_call x1, Pallas kernels, local(): pl.pallas_call(sum_kernel, out_shape=(shape((OWN, ROWS, D)), shape((OWN,...  2.64 us
    unnamed x24, local copies, waits for them, and re-layouts  2.35 us

profile of v7, /device:TPU:1, one launch (start us, length us, event | category | flops | bytes accessed | tf_op | source)
XLA Modules:
  0.0 103.9 jit_solution(15632881501470024330)
XLA Ops:
  1.9 0.0 copy-start.10
  1.9 23.9 %shard_map.140 = (s32[8,128]{1,0:T(8,128)}, bf16[256,256]{1,0:T(8,128)(2,1)}, bf16[256,256]{1,0:T(8,128)(2,1)}, bf16[256,256]{1,0:T(8,128)(2,1)}, bf16[512,512]{...) custom-call(s32[2,32]{1,0:T(2,128)} %bitcast.6, ...), custom_call_target="tpu_custom_call" | custom-call | flops 10000000000 | bytes 50000000 | tf_op jit(solution)/shard_map/pallas_call | solution.py:693
  25.8 0.0 copy-done.10
  25.8 0.0 copy-start.8
  25.8 0.7 copy-done.8
  26.5 0.0 copy-start.9
  26.5 0.7 copy-done.9
  27.2 0.0 copy-start.11
  27.2 0.9 copy-done.11
  28.1 0.0 copy-start
  28.1 0.0 copy-start.1
  28.1 0.0 copy-start.2
  28.1 0.0 copy-start.3
  28.1 0.0 copy-start.4
  28.2 0.0 copy-start.5
  28.2 0.0 copy-start.6
  28.2 0.0 copy-start.7
  28.2 26.4 %shard_map.141 = (bf16[8,256,256]{2,1,0:T(8,128)(2,1)S(1)}, bf16[8,256,256]{2,1,0:T(8,128)(2,1)S(1)}, f32[8,256]{1,0:T(8,128)S(1)}) custom-call(s32[8,128]{1,0:T(8,128)S(1)} %copy-done.8, bf16[8,64,256]{2,1,0:T(8,128)(2,1)S(1)} %copy-done.10, bf16[4,8,16,256]{3,2,1,0:T(8,128)(2,1)S(1)} %copy-done.11, f32[8,256]{1,0:T(8,128)S(1)} %copy-done.9), custom_call_target="tpu_custom_call" | custom-call | flops 10000000000 | bytes 50000000 | tf_op jit(solution)/shard_map/pallas_call | solution.py:709
  54.6 0.0 copy-done
  54.6 0.0 copy-done.1
  54.6 0.0 copy-done.2
  54.6 0.0 copy-done.3
  54.6 0.0 copy-done.4
  54.6 0.0 copy-done.5
  54.6 0.0 copy-done.6
  54.7 0.0 copy-done.7
  54.7 6.4 %shard_map.142 = (bf16[4,256,256]{2,1,0:T(8,128)(2,1)S(1)}, bf16[4,256,256]{2,1,0:T(8,128)(2,1)S(1)}, f32[4,8,256]{2,1,0:T(8,128)S(1)}, f32[4,8,256]{2,1,0:T(8,128)S(1)}) custom-call(s32[8,128]{1,0:T(8,128)S(1)} %copy-done.8, bf16[8,256,256]{2,1,0:T(8,128)(2,1)S(1)} %get-tuple-element.26.own, bf16[8,256,256]{2,1,0:T(8,128)(2,1)S(1)} %get-tuple-element.27.xj, ...), custom_call_target="tpu_custom_call" | custom-call | tf_op jit(solution)/shard_map/pallas_call | solution.py:726
  61.1 40.1 %shard_map.143 = (bf16[4,6,6,16,256]{4,3,2,1,0:T(8,128)(2,1)S(1)}, f32[6,8,256]{2,1,0:T(8,128)S(1)}, bf16[4,8,64,256]{3,2,1,0:T(8,128)(2,1)S(1)}, f32[8,256]{1,0:T(8,128)S(1)}, f32[3,8,256]{2,1,0:T(8,128)S(1)}) custom-call(s32[8,128]{1,0:T(8,128)S(1)} %copy-done.8, bf16[8,256,256]{2,1,0:T(8,128)(2,1)S(1)} %get-tuple-element.26.own, ...), custom_call_target="tpu_custom_call" | custom-call | flops 10000000000 | bytes 50000000 | tf_op jit(solution)/shard_map/pallas_call | solution.py:734
  101.2 2.6 %shard_map.144 = (bf16[8,64,256]{2,1,0:T(8,128)(2,1)}, f32[8,64]{1,0:T(8,128)}) custom-call(s32[8,128]{1,0:T(8,128)S(1)} %copy-done.8, bf16[4,6,6,16,256]{4,3,2,1,0:T(8,128)(2,1)S(1)} %get-tuple-element.39.zret, f32[6,8,256]{2,1,0:T(8,128)S(1)} %get-tuple-element.40.zmr, bf16[4,8,64,256]{3,2,1,0:T(8,128)(2,1)S(1)} %get-tuple-element.41.gm, ...), custom_call_target="tpu_custom_call" | custom-call | tf_op jit(solution)/shard_map/pallas_call | solution.py:751
Async XLA Ops:
  1.9 23.9 %copy-start.10 = (bf16[8,64,256]{2,1,0:T(8,128)(2,1)S(1)}, bf16[8,64,256]{2,1,0:T(8,128)(2,1)}, u32[]{:S(2)}) copy-start(bf16[8,64,256]{2,1,0:T(8,128)(2,1)} %desc.1) | copy-start | bytes 786436
  25.8 0.7 copy-start.8
  26.5 0.7 copy-start.9
  27.2 0.9 copy-start.11
  28.1 26.5 %copy-start = (bf16[512,512]{1,0:T(8,128)(2,1)S(1)}, bf16[512,512]{1,0:T(8,128)(2,1)}, u32[]{:S(2)}) copy-start(bf16[512,512]{1,0:T(8,128)(2,1)} %get-tuple-element.32.whT) | copy-start | bytes 1572868
  28.1 26.5 %copy-start.1 = (bf16[256,512]{1,0:T(8,128)(2,1)S(1)}, bf16[256,512]{1,0:T(8,128)(2,1)}, u32[]{:S(2)}) copy-start(bf16[256,512]{1,0:T(8,128)(2,1)} %get-tuple-element.33.wdT) | copy-start | bytes 786436
  28.1 26.5 %copy-start.2 = (f32[512,128]{1,0:T(8,128)S(1)}, f32[512,128]{1,0:T(8,128)}, u32[]{:S(2)}) copy-start(f32[512,128]{1,0:T(8,128)} %get-tuple-element.34.gcol) | copy-start | bytes 786436
  28.1 26.5 %copy-start.3 = (bf16[256,256]{1,0:T(8,128)(2,1)S(1)}, bf16[256,256]{1,0:T(8,128)(2,1)}, u32[]{:S(2)}) copy-start(bf16[256,256]{1,0:T(8,128)(2,1)} %wa.3) | copy-start | bytes 393220
  28.1 26.5 %copy-start.4 = (bf16[256,256]{1,0:T(8,128)(2,1)S(1)}, bf16[256,256]{1,0:T(8,128)(2,1)}, u32[]{:S(2)}) copy-start(bf16[256,256]{1,0:T(8,128)(2,1)} %wm.3) | copy-start | bytes 393220
  28.2 26.5 %copy-start.5 = (bf16[256,256]{1,0:T(8,128)(2,1)S(1)}, bf16[256,256]{1,0:T(8,128)(2,1)}, u32[]{:S(2)}) copy-start(bf16[256,256]{1,0:T(8,128)(2,1)} %get-tuple-element.29.waT) | copy-start | bytes 393220
  28.2 26.5 %copy-start.6 = (bf16[256,256]{1,0:T(8,128)(2,1)S(1)}, bf16[256,256]{1,0:T(8,128)(2,1)}, u32[]{:S(2)}) copy-start(bf16[256,256]{1,0:T(8,128)(2,1)} %get-tuple-element.30.wvT) | copy-start | bytes 393220
  28.2 26.5 %copy-start.7 = (bf16[256,256]{1,0:T(8,128)(2,1)S(1)}, bf16[256,256]{1,0:T(8,128)(2,1)}, u32[]{:S(2)}) copy-start(bf16[256,256]{1,0:T(8,128)(2,1)} %get-tuple-element.31.woT) | copy-start | bytes 393220

commit v8 on v7

--- a/solution.py
+++ b/solution.py
@@ -26,7 +26,6 @@
 FIXED = 4
 PARTS = 4
 PART = ROWS // PARTS
-HALF = 16
 MESH = pl.DeviceIdType.MESH
 LIMIT = 24 * 2**20
 
@@ -367,21 +366,21 @@
 
 
 def meet_kernel(
-    pairs, pair_count, counts, desc_far, visible_far, wa_far, wv_far, wo_far, wh_far, gain_far, wd_far,
-    tab, waT, wvT, woT, whT, wdT, gcol, upper, okeep, told, near, omask, desc, visible, wa, wv, wo, wh, gain, wd,
+    pairs, pair_count, counts, visible_far, wa_far, wv_far, wo_far, wh_far, gain_far, wd_far,
+    tab, waT, wvT, woT, whT, wdT, gcol, okeep, told, near, omask, visible, wa, wv, wo, wh, gain, wd,
     ssem, rsem, osem, orem, lsem,
 ):
     me, sub, others, peers = places()
-    far = (desc_far, visible_far, wa_far, wv_far, wo_far, wh_far, gain_far, wd_far)
+    far = (visible_far, wa_far, wv_far, wo_far, wh_far, gain_far, wd_far)
     loads = [
         pltpu.make_async_copy(src, dst, lsem.at[i])
-        for i, (src, dst) in enumerate(zip(far, (desc, visible, wa, wv, wo, wh, gain, wd)))
+        for i, (src, dst) in enumerate(zip(far, (visible, wa, wv, wo, wh, gain, wd)))
     ]
     for load in loads:
         load.start()
     own, out = own_rows(pairs[...], pair_count[0], me, lax.axis_size("img"))
     told[...] = jnp.broadcast_to(out, (8, 128))
-    for load in loads[:2]:
+    for load in loads[:1]:
         load.wait()
     omask[0] = own_mask(counts, visible, sub)
     greet(others, peers)
@@ -389,12 +388,10 @@
     for d in range(1, SUBS):
         to = {"sub": peers[d - 1]}
         ocopies.append(send(omask.at[0], omask.at[d], osem.at[1, d - 1], orem.at[1, d - 1], to))
-        ocopies.append(send(desc.at[:, 0:HALF, :], upper.at[sub], osem.at[0, d - 1], orem.at[0, d - 1], to))
     copies = [send(told, near.at[t ^ 1], ssem.at[t], rsem.at[t ^ 1], {"img": others[t]}) for t in range(REACH)]
     for copy in copies + ocopies:
         copy.start()
-    upper[sub] = desc[:, 0:HALF, :]
-    for load in loads[2:]:
+    for load in loads[1:]:
         load.wait()
     prepare(wa, wv, wo, wh, gain, wd, waT, wvT, woT, whT, wdT, gcol)
     for copy in copies:
@@ -414,7 +411,7 @@
 
 
 def fetch_kernel(
-    tab, desc, upper, okeep, own, xj, jkeep, zst, zl0, zl1, zl2, zl3, zms, zml, yst, yl, yms, yml, lower,
+    tab, desc, okeep, own, xj, jkeep, zst, zl0, zl1, zl2, zl3, zms, zml, yst, yl, yms, yml, lower,
     zsem, zrem, ysem, yrem, osem, orem,
 ):
     me, sub, others, peers = places()
@@ -445,10 +442,10 @@
             zcopies[c].append(copy)
     ocopies = []
     for d in range(1, SUBS):
-        copy = send(desc.at[:, HALF:ROWS, :], lower.at[sub], osem.at[d - 1], orem.at[d - 1], {"sub": peers[d - 1]})
+        copy = send(desc, lower.at[sub], osem.at[d - 1], orem.at[d - 1], {"sub": peers[d - 1]})
         copy.start()
         ocopies.append(copy)
-    lower[sub] = desc[:, HALF:ROWS, :]
+    lower[sub] = desc[...]
     for copy in zmcopies:
         copy.wait()
     zmasks = jnp.concatenate([zml[t] for t in range(REACH)], axis=0)
@@ -479,8 +476,7 @@
     for copy in ocopies:
         copy.wait()
     for s in range(SUBS):
-        own[:, s * ROWS : s * ROWS + HALF, :] = upper[s]
-        own[:, s * ROWS + HALF : s * ROWS + ROWS, :] = lower[s]
+        own[:, s * ROWS : s * ROWS + ROWS, :] = lower[s]
     for copy in ycopies:
         copy.wait()
     for s in range(SUBS):
@@ -690,36 +686,36 @@
 def local(descriptors, counts, visible, pair_list, pair_count, w_attend, w_value, w_output, w_hidden, norm_gain, w_down, w_match, unassigned_bucket):
     V = pltpu.VMEM
     peer = (SUBS - 1,)
-    tab, *ready, upper, okeep = pl.pallas_call(
+    tab, *ready, okeep = pl.pallas_call(
         meet_kernel,
         out_shape=(
             shape((8, 128), I32), *[shape((256, 256))] * 3, shape((512, 512)), shape((256, 512)), shape((512, 128), F32),
-            shape((SUBS, OWN, HALF, D)), shape((OWN, KEYS), F32),
+            shape((OWN, KEYS), F32),
         ),
-        in_specs=[VM, SM, SM] + [HB] * 8,
-        out_specs=(VM,) * 9,
+        in_specs=[VM, SM, SM] + [HB] * 7,
+        out_specs=(VM,) * 8,
         scratch_shapes=[
             V((8, 128), I32), V((REACH, 8, 128), I32), V((SUBS, OWN, KEYS), F32),
-            V((OWN, ROWS, D), BF), V((OWN, ROWS), I32), *[V((256, 256), BF)] * 3, V((512, 512), BF), V((1, 512), F32), V((512, 256), BF),
-            DMA((REACH,)), DMA((REACH,)), DMA((2, SUBS - 1)), DMA((2, SUBS - 1)), DMA((8,)),
+            V((OWN, ROWS), I32), *[V((256, 256), BF)] * 3, V((512, 512), BF), V((1, 512), F32), V((512, 256), BF),
+            DMA((REACH,)), DMA((REACH,)), DMA((2, SUBS - 1)), DMA((2, SUBS - 1)), DMA((7,)),
         ],
         compiler_params=talk(0, 56 * 2**20),
         cost_estimate=COST,
-    )(pair_list.T, pair_count, counts, descriptors, visible, w_attend, w_value, w_output, w_hidden, norm_gain.reshape(1, -1), w_down)
+    )(pair_list.T, pair_count, counts, visible, w_attend, w_value, w_output, w_hidden, norm_gain.reshape(1, -1), w_down)
     own, xj, jkeep = pl.pallas_call(
         fetch_kernel,
         out_shape=(shape((OWN, KEYS, D)), shape((JOBS, KEYS, D)), shape((JOBS, KEYS), F32)),
-        in_specs=[SM, VM, VM, VM],
+        in_specs=[SM, VM, VM],
         out_specs=(VM,) * 3,
         scratch_shapes=[
             V((PARTS, REACH, MOST, PART, D), BF), *[V((REACH, MOST, PART, D), BF)] * PARTS, V((REACH, 8, KEYS), F32), V((REACH, 8, KEYS), F32),
             V((PARTS, SUBS - 1, JOBS, PART, D), BF), V((PARTS, SUBS, JOBS, PART, D), BF), V((SUBS, JOBS, KEYS), F32), V((SUBS - 1, JOBS, KEYS), F32),
-            V((SUBS, OWN, ROWS - HALF, D), BF),
+            V((SUBS, OWN, ROWS, D), BF),
             DMA((PARTS + 1, REACH)), DMA((PARTS + 1, REACH)), DMA((PARTS + 1, SUBS - 1)), DMA((PARTS + 1, SUBS - 1)), DMA(peer), DMA(peer),
         ],
         compiler_params=talk(1),
         cost_estimate=COST,
-    )(tab, descriptors, upper, okeep)
+    )(tab, descriptors, okeep)
     bucket = unassigned_bucket.reshape(1, 1)
     late = JOBS - FIXED
     common = (tab, own, xj, okeep, jkeep, bucket, w_attend, w_match, *ready)

time: 104 us -> 106 us (1.019)
  Pallas kernels: 99.4 us -> 102 us
    pallas_call x1, Pallas kernels: 26.4 us -> 31 us  [local(): pl.pallas_call(fetch_kernel, out_shape=(shape((OWN, KEYS, D)), shape((JOB...]
    pallas_call x1, Pallas kernels: 23.9 us -> 21.6 us  [local(): pl.pallas_call(meet_kernel, out_shape=(shape((8, 128), I32), *[shape((256...]
    unnamed x24 -> x22, local copies, waits for them, and re-layouts: 2.35 us -> 1.41 us
where the time goes in v8:
time: 106 us; the launch traced here: 105 us
  Pallas kernels  102 us (96%)
  between operations  2.08 us (2%)
  local copies, waits for them, and re-layouts  1.41 us (1%)
    pallas_call x1, Pallas kernels, local(): pl.pallas_call(give_kernel, out_shape=(shape((PARTS, REACH, MOST, PART, D...  40.1 us
    pallas_call x1, Pallas kernels, local(): pl.pallas_call(fetch_kernel, out_shape=(shape((OWN, KEYS, D)), shape((JOB...  31 us
    pallas_call x1, Pallas kernels, local(): pl.pallas_call(meet_kernel, out_shape=(shape((8, 128), I32), *[shape((256...  21.6 us
    pallas_call x1, Pallas kernels, local(): pl.pallas_call(work_kernel, out_shape=(shape((late, KEYS, D)), shape((lat...  6.43 us
    pallas_call x1, Pallas kernels, local(): pl.pallas_call(sum_kernel, out_shape=(shape((OWN, ROWS, D)), shape((OWN,...  2.66 us

profile of v8, /device:TPU:1, one launch (start us, length us, event | category | flops | bytes accessed | tf_op | source)
XLA Modules:
  0.0 105.2 jit_solution(2708494766274567457)
XLA Ops:
  1.9 0.0 copy-start.10
  1.9 21.6 %shard_map.140 = (s32[8,128]{1,0:T(8,128)}, bf16[256,256]{1,0:T(8,128)(2,1)}, bf16[256,256]{1,0:T(8,128)(2,1)}, bf16[256,256]{1,0:T(8,128)(2,1)}, bf16[512,512]{...) custom-call(s32[2,32]{1,0:T(2,128)} %bitcast.6, s32[1]{0:T(128)S(6)} %copy.15.pair_count, ...), custom_call_target="tpu_custom_call" | custom-call | flops 10000000000 | bytes 50000000 | tf_op jit(solution)/shard_map/pallas_call | solution.py:689
  23.5 0.0 copy-done.10
  23.5 0.0 copy-start.8
  23.6 0.7 copy-done.8
  24.2 0.0 copy-start.9
  24.2 0.7 copy-done.9
  24.9 0.0 copy-start
  24.9 0.0 copy-start.1
  24.9 0.0 copy-start.2
  24.9 0.0 copy-start.3
  24.9 0.0 copy-start.4
  24.9 0.0 copy-start.5
  25.0 0.0 copy-start.6
  25.0 0.0 copy-start.7
  25.0 31.0 %shard_map.141 = (bf16[8,256,256]{2,1,0:T(8,128)(2,1)S(1)}, bf16[8,256,256]{2,1,0:T(8,128)(2,1)S(1)}, f32[8,256]{1,0:T(8,128)S(1)}) custom-call(s32[8,128]{1,0:T(8,128)S(1)} %copy-done.8, bf16[8,64,256]{2,1,0:T(8,128)(2,1)S(1)} %copy-done.10, f32[8,256]{1,0:T(8,128)S(1)} %copy-done.9), custom_call_target="tpu_custom_call" | custom-call | flops 10000000000 | bytes 50000000 | tf_op jit(solution)/shard_map/pallas_call | solution.py:705
  56.0 0.0 copy-done
  56.0 0.0 copy-done.1
  56.0 0.0 copy-done.2
  56.0 0.0 copy-done.3
  56.0 0.0 copy-done.4
  56.0 0.0 copy-done.5
  56.0 0.0 copy-done.6
  56.0 0.0 copy-done.7
  56.0 6.4 %shard_map.142 = (bf16[4,256,256]{2,1,0:T(8,128)(2,1)S(1)}, bf16[4,256,256]{2,1,0:T(8,128)(2,1)S(1)}, f32[4,8,256]{2,1,0:T(8,128)S(1)}, f32[4,8,256]{2,1,0:T(8,128)S(1)}) custom-call(s32[8,128]{1,0:T(8,128)S(1)} %copy-done.8, bf16[8,256,256]{2,1,0:T(8,128)(2,1)S(1)} %get-tuple-element.24.own, bf16[8,256,256]{2,1,0:T(8,128)(2,1)S(1)} %get-tuple-element.25.xj, ...), custom_call_target="tpu_custom_call" | custom-call | tf_op jit(solution)/shard_map/pallas_call | solution.py:722
  62.5 40.1 %shard_map.143 = (bf16[4,6,6,16,256]{4,3,2,1,0:T(8,128)(2,1)S(1)}, f32[6,8,256]{2,1,0:T(8,128)S(1)}, bf16[4,8,64,256]{3,2,1,0:T(8,128)(2,1)S(1)}, f32[8,256]{1,0:T(8,128)S(1)}, f32[3,8,256]{2,1,0:T(8,128)S(1)}) custom-call(s32[8,128]{1,0:T(8,128)S(1)} %copy-done.8, bf16[8,256,256]{2,1,0:T(8,128)(2,1)S(1)} %get-tuple-element.24.own, ...), custom_call_target="tpu_custom_call" | custom-call | flops 10000000000 | bytes 50000000 | tf_op jit(solution)/shard_map/pallas_call | solution.py:730
  102.5 2.7 %shard_map.144 = (bf16[8,64,256]{2,1,0:T(8,128)(2,1)}, f32[8,64]{1,0:T(8,128)}) custom-call(s32[8,128]{1,0:T(8,128)S(1)} %copy-done.8, bf16[4,6,6,16,256]{4,3,2,1,0:T(8,128)(2,1)S(1)} %get-tuple-element.37.zret, f32[6,8,256]{2,1,0:T(8,128)S(1)} %get-tuple-element.38.zmr, bf16[4,8,64,256]{3,2,1,0:T(8,128)(2,1)S(1)} %get-tuple-element.39.gm, ...), custom_call_target="tpu_custom_call" | custom-call | tf_op jit(solution)/shard_map/pallas_call | solution.py:747
Async XLA Ops:
  1.9 21.6 %copy-start.10 = (bf16[8,64,256]{2,1,0:T(8,128)(2,1)S(1)}, bf16[8,64,256]{2,1,0:T(8,128)(2,1)}, u32[]{:S(2)}) copy-start(bf16[8,64,256]{2,1,0:T(8,128)(2,1)} %desc.1) | copy-start | bytes 786436
  23.5 0.7 copy-start.8
  24.2 0.7 copy-start.9
  24.9 31.0 %copy-start = (bf16[512,512]{1,0:T(8,128)(2,1)S(1)}, bf16[512,512]{1,0:T(8,128)(2,1)}, u32[]{:S(2)}) copy-start(bf16[512,512]{1,0:T(8,128)(2,1)} %get-tuple-element.30.whT) | copy-start | bytes 1572868
  24.9 31.0 %copy-start.1 = (bf16[256,512]{1,0:T(8,128)(2,1)S(1)}, bf16[256,512]{1,0:T(8,128)(2,1)}, u32[]{:S(2)}) copy-start(bf16[256,512]{1,0:T(8,128)(2,1)} %get-tuple-element.31.wdT) | copy-start | bytes 786436
  24.9 31.1 %copy-start.2 = (f32[512,128]{1,0:T(8,128)S(1)}, f32[512,128]{1,0:T(8,128)}, u32[]{:S(2)}) copy-start(f32[512,128]{1,0:T(8,128)} %get-tuple-element.32.gcol) | copy-start | bytes 786436
  24.9 31.1 %copy-start.3 = (bf16[256,256]{1,0:T(8,128)(2,1)S(1)}, bf16[256,256]{1,0:T(8,128)(2,1)}, u32[]{:S(2)}) copy-start(bf16[256,256]{1,0:T(8,128)(2,1)} %wa.3) | copy-start | bytes 393220
  24.9 31.1 %copy-start.4 = (bf16[256,256]{1,0:T(8,128)(2,1)S(1)}, bf16[256,256]{1,0:T(8,128)(2,1)}, u32[]{:S(2)}) copy-start(bf16[256,256]{1,0:T(8,128)(2,1)} %wm.3) | copy-start | bytes 393220
  24.9 31.1 %copy-start.5 = (bf16[256,256]{1,0:T(8,128)(2,1)S(1)}, bf16[256,256]{1,0:T(8,128)(2,1)}, u32[]{:S(2)}) copy-start(bf16[256,256]{1,0:T(8,128)(2,1)} %get-tuple-element.27.waT) | copy-start | bytes 393220
  25.0 31.1 %copy-start.6 = (bf16[256,256]{1,0:T(8,128)(2,1)S(1)}, bf16[256,256]{1,0:T(8,128)(2,1)}, u32[]{:S(2)}) copy-start(bf16[256,256]{1,0:T(8,128)(2,1)} %get-tuple-element.28.wvT) | copy-start | bytes 393220
  25.0 31.1 %copy-start.7 = (bf16[256,256]{1,0:T(8,128)(2,1)S(1)}, bf16[256,256]{1,0:T(8,128)(2,1)}, u32[]{:S(2)}) copy-start(bf16[256,256]{1,0:T(8,128)(2,1)} %get-tuple-element.29.woT) | copy-start | bytes 393220
